TPU v7x, 512 devices: a whole 4x4x16 slice. The times are simulated.
512 devices in a mesh: dom: 32 (over y_hi, z), kb: 16 (over y_lo, x, core).
Axes of the slice: x: 4, y: 4 (y_hi: 2, y_lo: 2; y = y_hi * 2 + y_lo), z: 16, core: 2. Of those that a mesh axis runs over, the one named last changes fastest.
Arguments:
- features: bfloat16 [64, 65536], P(None, ('dom', 'kb')), may hold values from -6 to 6
- vectors: bfloat16 [3, 64, 65536], P(None, None, ('dom', 'kb')), may hold values from -6 to 6
- positions: float32 [3, 65536], P(None, ('dom', 'kb')), may hold values from 0 to 1, as said below
- neighbours: int32 [16, 65536], P(None, ('dom', 'kb')), may hold values from 0 to 384, as said below
- halo_lists: int32 [2, 65536], P(None, ('dom', 'kb')), may hold values from 0 to 127, as said below
- lattice: int32 [3, 8192], replicated, may hold values from -1024 to 1024, as said below
- kspace_filter: float32 [64, 8192], P(None, 'kb'), may hold values from -6 to 6
- node_weight: bfloat16 [64, 64], replicated, may hold values from -0.75 to 0.75
- node_bias: float32 [64], replicated, may hold values from -4 to 4
- message_weight: bfloat16 [64, 192], replicated, may hold values from -0.75 to 0.75
- radial_weight: bfloat16 [20, 192], replicated, may hold values from -3 to 3
- ewald_weight: bfloat16 [64, 64], replicated, may hold values from -0.75 to 0.75
Outputs:
- new_features: bfloat16 [64, 65536], P(None, ('dom', 'kb'))
- new_vectors: bfloat16 [3, 64, 65536], P(None, None, ('dom', 'kb'))
Inputs may be any that keep to these rules, and one draw needn't show every extreme that they name: `neighbours`: entry j of column a names atom a's neighbour in the numbering of E = 385 columns: own atoms, then the atoms received from the device below, then those from the device above; 384 marks an empty slot. Empty slots come last in a column, and each atom has 8 or more filled slots. `halo_lists`: for each device, 128 different local atom numbers in each row. `positions`: atom a's third coordinate times 32 * 16 lies between a // 128 and the next integer. `lattice`: rows 0 and 1 lie between -16 and 16.
All inputs are finite; a program needn't handle non-finite values.
Results may differ from a plain program's by a relative error of at most 0.01.
Values may be sent and summed in bfloat16 or wider, within the bound.
No kernel may reach another device: no remote copies, remote signals or barrier semaphores. Data moves between devices by JAX's collectives and lax.ppermute only.
A program may use at most 64 MiB of HBM per device.

v0:
```python
import math

import jax
import jax.numpy as jnp
from jax import lax
from jax.sharding import PartitionSpec as P

full_turn = 2.0 * math.pi
side_length = 6.0
slab_depth = 6.0
radial_reach = 6.0
distance_floor = 1.0


def shifted(value, axis, steps):
    count = lax.axis_size(axis)
    pairs = [(source, (source + steps) % count) for source in range(count)]
    return lax.ppermute(value, axis, pairs)


def in_order(pieces, dim):
    dims = list(pieces.shape[1:])
    dims[dim] *= pieces.shape[0]
    return jnp.moveaxis(pieces, 0, dim).reshape(dims)


def sent_to_all(x, axis):
    copies = jnp.broadcast_to(x, (lax.axis_size(axis), *x.shape))
    return lax.all_to_all(copies, axis, split_axis=0, concat_axis=0, tiled=True)


def collect(x, axis, dim):
    return in_order(sent_to_all(x, axis), dim)


def filled_up(lines, peers):
    spare = -len(lines) % peers
    return jnp.pad(lines, [(0, spare)] + [(0, 0)] * (lines.ndim - 1))


def split_up(x, dim, peers):
    dims = x.shape
    pieces = x.reshape(*dims[:dim], peers, dims[dim] // peers, *dims[dim + 1 :])
    return jnp.moveaxis(pieces, dim, 0)


def sum_at_owner(x, axis, dim):
    pieces = split_up(x, dim, lax.axis_size(axis))
    arrived = lax.all_to_all(pieces, axis, split_axis=0, concat_axis=0, tiled=True)
    return arrived.astype(jnp.float32).sum(axis=0)


def sum_by_parts(x, axes):
    lines = x.reshape(-1, x.shape[-1])
    padded = filled_up(lines, lax.axis_size(axes))
    whole = collect(sum_at_owner(padded, axes, 0).astype(jnp.bfloat16), axes, 0)
    return lax.slice_in_dim(whole, 0, len(lines)).reshape(x.shape).astype(jnp.float32)


def in_one_piece(arrays, axis, dim, along):
    ends, at = ([], 0)
    for a in arrays[:-1]:
        at += a.shape[along]
        ends.append(at)
    both = jnp.concatenate(arrays, axis=along)
    return tuple(jnp.split(lax.all_gather(both, axis, axis=dim, tiled=True), ends, axis=along))


def over_first(first_operand, second_operand):
    return lax.dot_general(
        first_operand, second_operand, (((0,), (0,)), ((), ())), preferred_element_type=jnp.float32
    )


def over_last(first_operand, second_operand):
    return lax.dot_general(
        first_operand, second_operand, (((1,), (1,)), ((), ())), preferred_element_type=jnp.float32
    )


def phase_tables(coords, lattice_rows):
    phase_angle = (
        coords[0][:, None] * lattice_rows[0][None, :]
        + coords[1][:, None] * lattice_rows[1][None, :]
        + coords[2][:, None] * lattice_rows[2][None, :]
    ) * full_turn
    return (jnp.cos(phase_angle).astype(jnp.bfloat16), jnp.sin(phase_angle).astype(jnp.bfloat16))


def short_range(
    own_feat,
    own_vec,
    own_pos,
    neighbour_ids,
    side_feat,
    side_vec,
    side_pos,
    node_weight,
    node_bias,
    message_weight,
    radial_weight,
    slab_count,
):
    channels = own_feat.shape[0]
    own_count = own_feat.shape[1]
    slot_count = neighbour_ids.shape[0]
    radial_count = radial_weight.shape[0]
    ext_feat = jnp.concatenate(
        [own_feat, side_feat, jnp.zeros((channels, 1), jnp.bfloat16)], axis=1
    )
    ext_vec = jnp.concatenate(
        [own_vec, side_vec, jnp.zeros((3, channels, 1), jnp.bfloat16)], axis=2
    )
    ext_pos = jnp.concatenate([own_pos, side_pos, jnp.zeros((3, 1), jnp.float32)], axis=1)
    empty_slot = ext_feat.shape[1] - 1
    hidden = jax.nn.silu(over_first(node_weight, ext_feat) + node_bias[:, None]).astype(
        jnp.bfloat16
    )
    message_in = over_first(message_weight, hidden).astype(jnp.bfloat16)
    flat_ids = neighbour_ids.reshape(-1)
    weights_on = (flat_ids < empty_slot).astype(jnp.float32)
    offsets = (
        jnp.take(ext_pos, flat_ids, axis=1).reshape(3, slot_count, own_count) - own_pos[:, None, :]
    )
    offsets = offsets - jnp.floor(offsets + 0.5)
    box_sides = jnp.array([side_length, side_length, slab_depth * slab_count], jnp.float32)
    cartesian = offsets * box_sides[:, None, None]
    distance = jnp.sqrt(jnp.sum(cartesian * cartesian, axis=0))
    direction = cartesian / jnp.maximum(distance, distance_floor)
    centers = jnp.arange(radial_count).astype(jnp.float32) * (radial_reach / (radial_count - 1))
    spread = 1.5 * radial_reach / radial_count
    radial = jnp.exp(-jnp.square((distance[None] - centers[:, None, None]) / spread)).astype(
        jnp.bfloat16
    )
    edge_filter = over_first(radial_weight, radial.reshape(radial_count, -1))
    edge_terms = (
        jnp.take(message_in, flat_ids, axis=1).astype(jnp.float32) * edge_filter * weights_on
    )
    edge_terms = edge_terms.reshape(3 * channels, slot_count, own_count)
    scalar_part = jnp.sum(edge_terms[:channels], axis=1)
    neighbour_vec = (
        jnp.take(ext_vec, flat_ids, axis=2)
        .reshape(3, channels, slot_count, own_count)
        .astype(jnp.float32)
    )
    vector_part = jnp.sum(
        neighbour_vec * edge_terms[channels : 2 * channels][None]
        + edge_terms[2 * channels :][None] * direction[:, None],
        axis=2,
    )
    return (scalar_part, vector_part)


def shards(
    features,
    vectors,
    positions,
    neighbours,
    halo_lists,
    lattice,
    kspace_filter,
    node_weight,
    node_bias,
    message_weight,
    radial_weight,
    ewald_weight,
):
    channels = features.shape[0]
    own_count = features.shape[1]
    column_count = kspace_filter.shape[1]
    slab_count = lax.axis_size("dom") * lax.axis_size("kb")
    all_columns = column_count * lax.axis_size("kb")
    norm_scale = 1.0 / math.sqrt(all_columns * own_count * slab_count)
    up_feat = jnp.take(features, halo_lists[0], axis=1)
    up_vec = jnp.take(vectors, halo_lists[0], axis=2)
    up_pos = jnp.take(positions, halo_lists[0], axis=1)
    down_feat = jnp.take(features, halo_lists[1], axis=1)
    down_vec = jnp.take(vectors, halo_lists[1], axis=2)
    down_pos = jnp.take(positions, halo_lists[1], axis=1)
    from_below = shifted((up_feat, up_vec), ("dom", "kb"), 1)
    from_above = shifted((down_feat, down_vec), ("dom", "kb"), -1)
    below_pos = shifted(up_pos, ("dom", "kb"), 1)
    above_pos = shifted(down_pos, ("dom", "kb"), -1)
    ewald_in = over_first(ewald_weight, features).astype(jnp.bfloat16)
    lattice_rows = lattice.astype(jnp.float32)
    own_lattice = lax.dynamic_slice_in_dim(
        lattice_rows, lax.axis_index("kb") * column_count, column_count, 1
    )
    zero_columns = jnp.zeros((channels, column_count), jnp.float32)
    domain_pos = collect(positions, "kb", 1)
    feat_piece = collect(ewald_in, "kb", 1)
    piece_width = math.gcd(feat_piece.shape[1], own_count)

    def one_block(block_index, totals):
        start_at = block_index * piece_width
        feat_block = lax.dynamic_slice_in_dim(feat_piece, start_at, piece_width, 1)
        pos_block = lax.dynamic_slice_in_dim(domain_pos, start_at, piece_width, 1)
        cosine_table, sine_table = phase_tables(pos_block, own_lattice)
        return (
            totals[0] + jnp.dot(feat_block, cosine_table, preferred_element_type=jnp.float32),
            totals[1] + jnp.dot(feat_block, sine_table, preferred_element_type=jnp.float32),
        )

    partial_sums = lax.fori_loop(
        0, feat_piece.shape[1] // piece_width, one_block, (zero_columns, zero_columns)
    )
    total_re, total_im = (
        sum_by_parts(partial_sums[0].astype(jnp.bfloat16), "dom"),
        sum_by_parts(partial_sums[1].astype(jnp.bfloat16), "dom"),
    )
    filt_re = (kspace_filter * total_re * norm_scale).astype(jnp.bfloat16)
    filt_im = (kspace_filter * total_im * norm_scale).astype(jnp.bfloat16)
    side_feat = jnp.concatenate([from_below[0], from_above[0]], axis=1)
    side_vec = jnp.concatenate([from_below[1], from_above[1]], axis=2)
    side_pos = jnp.concatenate([below_pos, above_pos], axis=1)
    scalar_part, vector_part = short_range(
        features,
        vectors,
        positions,
        neighbours,
        side_feat,
        side_vec,
        side_pos,
        node_weight,
        node_bias,
        message_weight,
        radial_weight,
        slab_count,
    )
    re_piece, im_piece = in_one_piece((filt_re, filt_im), "kb", 1, 0)
    add_piece_width = math.gcd(re_piece.shape[1], column_count)

    def one_block(block_index, summed):
        start_at = block_index * add_piece_width
        re_block = lax.dynamic_slice_in_dim(re_piece, start_at, add_piece_width, 1)
        im_block = lax.dynamic_slice_in_dim(im_piece, start_at, add_piece_width, 1)
        lattice_block = lax.dynamic_slice_in_dim(lattice_rows, start_at, add_piece_width, 1)
        cosine_table, sine_table = phase_tables(positions, lattice_block)
        return summed + over_last(re_block, cosine_table) + over_last(im_block, sine_table)

    message = lax.fori_loop(
        0,
        re_piece.shape[1] // add_piece_width,
        one_block,
        jnp.zeros((channels, own_count), jnp.float32),
    )
    new_features = (features.astype(jnp.float32) + scalar_part + message).astype(jnp.bfloat16)
    new_vectors = (vectors.astype(jnp.float32) + vector_part).astype(jnp.bfloat16)
    return (new_features, new_vectors)


def solution(mesh):
    placed = (
        P(None, ("dom", "kb")),
        P(None, None, ("dom", "kb")),
        P(None, ("dom", "kb")),
        P(None, ("dom", "kb")),
        P(None, ("dom", "kb")),
        P(),
        P(None, "kb"),
        P(),
        P(),
        P(),
        P(),
        P(),
    )
    return jax.shard_map(
        shards,
        mesh=mesh,
        in_specs=placed,
        out_specs=(P(None, ("dom", "kb")), P(None, None, ("dom", "kb"))),
        check_vma=False,
    )
```

profile of v0, /device:TPU:1, one launch (start us, length us, event | category | flops | bytes accessed | tf_op | source)
XLA Modules:
  0.0 271.7 jit_solution(7614816665776123111)
XLA Ops:
  8.9 10.2 %all-to-all-start = ((bf16[16,64,128]{2,1,0:T(8,128)(2,1)}), bf16[16,64,128]{2,1,0:T(8,128)(2,1)S(1)}, u32[]{:S(2)}, u32[]{:S(2)}) async-start(bf16[16,64,128]{2,1,0:T(8,128)(2,1)} %broadcast_in_dim.105), calls=%async_computation | async-start | bytes 524288 | tf_op jit(solution)/shard_map/all_to_all | solution.py:29
  21.5 3.5 %collective-permute-start = (bf16[64,128]{0,1:T(8,128)(2,1)S(1)}, bf16[64,128]{0,1:T(8,128)(2,1)S(1)}, u32[]{:S(2)}, u32[]{:S(2)}) collective-permute-start(bf16[64,128]{0,1:T(8,128)(2,1)S(1)} %select_bitcast_fusion.5), channel_id=1, source_target_pairs={{0,1},{1,2},{2,3},{3,4},{4,5},{5,6},{6,7},{7,8},{8,9},{9,10},{10,1... | collective-permute-start | bytes 49160 | tf_op jit(solution)/shard_map/ppermute | solution.py:18
  26.7 1.3 broadcast_in_dim.106
  28.0 5.1 %all-to-all-start.1 = ((f32[16,3,128]{2,1,0:T(4,128)}), f32[16,3,128]{2,1,0:T(4,128)S(1)}, u32[]{:S(2)}, u32[]{:S(2)}) async-start(f32[16,3,128]{2,1,0:T(4,128)} %broadcast_in_dim.106), calls=%async_computation.1 | async-start | bytes 65536 | tf_op jit(solution)/shard_map/all_to_all | solution.py:29
  33.1 5.8 %all-to-all-done.1 = f32[16,3,128]{2,1,0:T(4,128)S(1)} async-done(((f32[16,3,128]{2,1,0:T(4,128)}), f32[16,3,128]{2,1,0:T(4,128)S(1)}, u32[]{:S(2)}, u32[]{:S(2)}) %all-to-all-start.1) | async-done | bytes 24608 | tf_op jit(solution)/shard_map/all_to_all | solution.py:29
  38.9 38.6 %while.30 = (s32[]{:T(128)}, f32[64,512]{1,0:T(8,128)S(1)}, f32[64,512]{1,0:T(8,128)S(1)}, bf16[64,2048]{1,0:T(8,128)(2,1)S(1)}, f32[3,2048]{1,0:T(4,128)S(1)}, ...) while((s32[]{:T(128)}, f32[64,512]{1,0:T(8,128)S(1)}, ...), condition=%wide.region_3.6_spmd.clone, body=%wide.region_2.5_spmd.clone.sunk | while | flops 17825800 | bytes 591026 | solution.py:204
  41.3 1.2 convolution_add_fusion.10
  46.2 1.2 convolution_add_fusion.10
  60.6 1.2 convolution_add_fusion.10
  65.5 1.2 convolution_add_fusion.10
  70.3 1.2 convolution_add_fusion.10
  78.2 14.1 %all-to-all-start.4 = ((bf16[32,2,512]{2,1,0:T(2,128)(2,1)}), bf16[32,2,512]{2,1,0:T(2,128)(2,1)S(1)}, u32[]{:S(2)}, u32[]{:S(2)}) async-start(bf16[32,2,512]{2,1,0:T(2,128)(2,1)} %reshape.164), calls=%async_computation.4 | async-start | bytes 131072 | tf_op jit(solution)/shard_map/all_to_all | solution.py:49
  92.4 2.6 collective-permute-start.1
  95.8 3.0 %collective-permute-start.2 = (f32[3,128]{0,1:T(8,128)S(1)}, f32[3,128]{0,1:T(8,128)S(1)}, u32[]{:S(2)}, u32[]{:S(2)}) collective-permute-start(f32[3,128]{0,1:T(8,128)S(1)} %select_bitcast_fusion.3), channel_id=1, source_target_pairs={{0,1},{1,2},{2,3},{3,4},{4,5},{5,6},{6,7},{7,8},{8,9},{9,10},{10,1... | collective-permute-start | bytes 4616 | tf_op jit(solution)/shard_map/ppermute | solution.py:18
  100.1 6.7 %all-to-all-done.4 = bf16[32,2,512]{2,1,0:T(2,128)(2,1)S(1)} async-done(((bf16[32,2,512]{2,1,0:T(2,128)(2,1)}), bf16[32,2,512]{2,1,0:T(2,128)(2,1)S(1)}, u32[]{:S(2)}, u32[]{:S(2)}) %all-to-all-start.4) | async-done | bytes 65568 | tf_op jit(solution)/shard_map/all_to_all | solution.py:49
  106.8 7.4 %all-to-all-start.2 = ((bf16[32,2,512]{2,1,0:T(2,128)(2,1)}), bf16[32,2,512]{2,1,0:T(2,128)(2,1)S(1)}, u32[]{:S(2)}, u32[]{:S(2)}) async-start(bf16[32,2,512]{2,1,0:T(2,128)(2,1)} %reshape.163), calls=%async_computation.2 | async-start | bytes 131072 | tf_op jit(solution)/shard_map/all_to_all | solution.py:49
  114.3 1.9 collective-permute-start.3
  118.0 3.8 %collective-permute-start.4 = (bf16[3,64,128]{1,0,2:T(4,128)(2,1)}, bf16[3,64,128]{1,0,2:T(4,128)(2,1)}, u32[]{:S(2)}, u32[]{:S(2)}) collective-permute-start(bf16[3,64,128]{1,0,2:T(4,128)(2,1)} %select_bitcast_fusion.1), channel_id=1, source_target_pairs={{0,1},{1,2},{2,3},{3,4},{4,5},{5,6},{6,7},{7,8},{8,9},{9,10},{10,1... | collective-permute-start | bytes 147464 | tf_op jit(solution)/shard_map/ppermute | solution.py:18
  121.8 7.7 %all-to-all-done.2 = bf16[32,2,512]{2,1,0:T(2,128)(2,1)S(1)} async-done(((bf16[32,2,512]{2,1,0:T(2,128)(2,1)}), bf16[32,2,512]{2,1,0:T(2,128)(2,1)S(1)}, u32[]{:S(2)}, u32[]{:S(2)}) %all-to-all-start.2) | async-done | bytes 65568 | tf_op jit(solution)/shard_map/all_to_all | solution.py:49
  130.2 6.4 %all-to-all-start.5 = ((bf16[32,2,512]{2,1,0:T(2,128)(2,1)}), bf16[32,2,512]{2,1,0:T(2,128)(2,1)S(1)}, u32[]{:S(2)}, u32[]{:S(2)}) async-start(bf16[32,2,512]{2,1,0:T(2,128)(2,1)} %broadcast_in_dim.108), calls=%async_computation.5 | async-start | bytes 131072 | tf_op jit(solution)/shard_map/all_to_all | solution.py:29
  136.7 14.6 %all-to-all-done.5 = bf16[32,2,512]{2,1,0:T(2,128)(2,1)S(1)} async-done(((bf16[32,2,512]{2,1,0:T(2,128)(2,1)}), bf16[32,2,512]{2,1,0:T(2,128)(2,1)S(1)}, u32[]{:S(2)}, u32[]{:S(2)}) %all-to-all-start.5) | async-done | bytes 65568 | tf_op jit(solution)/shard_map/all_to_all | solution.py:29
  151.9 3.8 %all-to-all-start.3 = ((bf16[32,2,512]{2,1,0:T(2,128)(2,1)}), bf16[32,2,512]{2,1,0:T(2,128)(2,1)S(1)}, u32[]{:S(2)}, u32[]{:S(2)}) async-start(bf16[32,2,512]{2,1,0:T(2,128)(2,1)} %broadcast_in_dim.107), calls=%async_computation.3 | async-start | bytes 131072 | tf_op jit(solution)/shard_map/all_to_all | solution.py:29
  155.9 14.6 %all-to-all-done.3 = bf16[32,2,512]{2,1,0:T(2,128)(2,1)S(1)} async-done(((bf16[32,2,512]{2,1,0:T(2,128)(2,1)}), bf16[32,2,512]{2,1,0:T(2,128)(2,1)S(1)}, u32[]{:S(2)}, u32[]{:S(2)}) %all-to-all-start.3) | async-done | bytes 65568 | tf_op jit(solution)/shard_map/all_to_all | solution.py:29
  172.9 7.1 %collective-permute-start.5 = (bf16[3,64,128]{1,0,2:T(4,128)(2,1)}, bf16[3,64,128]{1,0,2:T(4,128)(2,1)}, u32[]{:S(2)}, u32[]{:S(2)}) collective-permute-start(bf16[3,64,128]{1,0,2:T(4,128)(2,1)} %select_bitcast_fusion), channel_id=1, source_target_pairs={{0,511},{1,0},{2,1},{3,2},{4,3},{5,4},{6,5},{7,6},{8,7},{9,8},{10,... | collective-permute-start | bytes 147464 | tf_op jit(solution)/shard_map/ppermute | solution.py:18
  180.2 5.5 %gather_fusion.1 = f32[2048,3]{1,0:T(8,128)S(1)} fusion(f32[3,385]{0,1:T(8,128)S(1)} %maximum_maximum_fusion.1, s32[2048]{0:T(1024)S(1)} %broadcast_clamp_fusion), kind=kCustom, calls=%fused_computation.7 | custom fusion | bytes 57344 | tf_op jit(solution)/shard_map/jit(_take)/gather | solution.py:123
  187.3 7.5 %gather_fusion = bf16[2048,192]{1,0:T(8,128)(2,1)S(1)} fusion(bf16[192,385]{0,1:T(8,128)(2,1)S(1)} %copy.100, s32[2048]{0:T(1024)S(1)} %broadcast_clamp_fusion), kind=kCustom, calls=%fused_computation.6 | custom fusion | bytes 1581056 | tf_op jit(solution)/shard_map/jit(_take)/gather | solution.py:137
  197.2 1.4 copy.116
  198.7 2.2 maximum_maximum_fusion
  200.9 15.5 %gather_fusion.2 = bf16[2048,3,64]{2,1,0:T(4,128)(2,1)} fusion(bf16[3,64,385]{1,0,2:T(4,128)(2,1)} %maximum_maximum_fusion, s32[2048]{0:T(1024)S(1)} %broadcast_clamp_fusion), kind=kCustom, calls=%fused_computation.8 | custom fusion | bytes 1581056 | tf_op jit(solution)/shard_map/jit(_take)/gather | solution.py:142
  216.4 6.7 %add_reduce_fusion = f32[3,64,128]{1,0,2:T(4,128)S(1)} fusion(f32[3,16,128]{0,2,1:T(8,128)S(1)} %copy.113, f32[64,16,128]{0,2,1:T(8,128)S(1)} %bitcast.121, f32[64,16,128]{0,2,1:T(8,128)S(1)} %bitcast.120, bf16[3,64,16,128]{1,0,3,2:T(4,128)(2,1)} %bitcast.122, pred[16,128]{1,0:T(8,128)(4,1)S(1)} %compare_and_fusion), kind=kLoop, calls=%fused_computation.67 | loop fusion | flops 2334720 | bytes 1959936 | tf_op jit(solution)/shard_map/reduce_sum | solution.py:146
  223.9 1.7 fusion.70
  225.6 38.6 %while.31 = (s32[]{:T(128)}, f32[64,128]{1,0:T(8,128)S(1)}, bf16[64,8192]{1,0:T(8,128)(2,1)S(1)}, f32[3,128]{1,0:T(4,128)S(1)}, f32[3,8192]{1,0:T(4,128)S(1)}, /...) while((s32[]{:T(128)}, f32[64,128]{1,0:T(8,128)S(1)}, ...), condition=%wide.region_7.10_spmd.clone, body=%wide.region_6.9_spmd.clone.sunk | while | flops 17719304 | bytes 293089 | solution.py:241
  (237 shorter events, 89.6 us)
Async XLA Ops:
  7.2 179.4 %copy-start = (bf16[64,192]{1,0:T(8,128)(2,1)S(1)}, bf16[64,192]{1,0:T(8,128)(2,1)}, u32[]{:S(2)}) copy-start(bf16[64,192]{1,0:T(8,128)(2,1)} %param.32) | copy-start | bytes 73732
  8.9 17.9 %all-to-all-start = ((bf16[16,64,128]{2,1,0:T(8,128)(2,1)}), bf16[16,64,128]{2,1,0:T(8,128)(2,1)S(1)}, u32[]{:S(2)}, u32[]{:S(2)}) async-start(bf16[16,64,128]{2,1,0:T(8,128)(2,1)} %broadcast_in_dim.105), calls=%async_computation | async-start | bytes 524288 | tf_op jit(solution)/shard_map/all_to_all | solution.py:29
  21.5 165.1 %collective-permute-start = (bf16[64,128]{0,1:T(8,128)(2,1)S(1)}, bf16[64,128]{0,1:T(8,128)(2,1)S(1)}, u32[]{:S(2)}, u32[]{:S(2)}) collective-permute-start(bf16[64,128]{0,1:T(8,128)(2,1)S(1)} %select_bitcast_fusion.5), channel_id=1, source_target_pairs={{0,1},{1,2},{2,3},{3,4},{4,5},{5,6},{6,7},{7,8},{8,9},{9,10},{10,1... | collective-permute-start | bytes 49160 | tf_op jit(solution)/shard_map/ppermute | solution.py:18
  28.0 10.9 %all-to-all-start.1 = ((f32[16,3,128]{2,1,0:T(4,128)}), f32[16,3,128]{2,1,0:T(4,128)S(1)}, u32[]{:S(2)}, u32[]{:S(2)}) async-start(f32[16,3,128]{2,1,0:T(4,128)} %broadcast_in_dim.106), calls=%async_computation.1 | async-start | bytes 65536 | tf_op jit(solution)/shard_map/all_to_all | solution.py:29
  38.9 56.1 %copy-start.4 = (f32[3,128]{1,0:T(4,128)S(1)}, f32[3,128]{1,0:T(4,128)}, u32[]{:S(2)}) copy-start(f32[3,128]{1,0:T(4,128)} %param.25) | copy-start | bytes 4612
  38.9 77.3 %copy-start.5 = (bf16[3,64,128]{2,1,0:T(8,128)(2,1)S(1)}, bf16[3,64,128]{2,1,0:T(8,128)(2,1)}, u32[]{:S(2)}) copy-start(bf16[3,64,128]{2,1,0:T(8,128)(2,1)} %param.24) | copy-start | bytes 147460
  77.5 59.1 %copy-start.2 = (s32[16,128]{1,0:T(8,128)S(1)}, s32[16,128]{1,0:T(8,128)}, u32[]{:S(2)}) copy-start(s32[16,128]{1,0:T(8,128)} %param.26) | copy-start | bytes 24580
  77.5 93.0 %copy-start.3 = (f32[64,512]{1,0:T(8,128)S(1)}, f32[64,512]{1,0:T(8,128)}, u32[]{:S(2)}) copy-start(f32[64,512]{1,0:T(8,128)} %param.29) | copy-start | bytes 393220
  78.2 28.7 %all-to-all-start.4 = ((bf16[32,2,512]{2,1,0:T(2,128)(2,1)}), bf16[32,2,512]{2,1,0:T(2,128)(2,1)S(1)}, u32[]{:S(2)}, u32[]{:S(2)}) async-start(bf16[32,2,512]{2,1,0:T(2,128)(2,1)} %reshape.164), calls=%async_computation.4 | async-start | bytes 131072 | tf_op jit(solution)/shard_map/all_to_all | solution.py:49
  92.4 94.2 %collective-permute-start.1 = (bf16[64,128]{0,1:T(8,128)(2,1)S(1)}, bf16[64,128]{0,1:T(8,128)(2,1)S(1)}, u32[]{:S(2)}, u32[]{:S(2)}) collective-permute-start(bf16[64,128]{0,1:T(8,128)(2,1)S(1)} %select_bitcast_fusion.4), channel_id=1, source_target_pairs={{0,511},{1,0},{2,1},{3,2},{4,3},{5,4},{6,5},{7,6},{8,7},{9,8},{10,... | collective-permute-start | bytes 49160 | tf_op jit(solution)/shard_map/ppermute | solution.py:18
  95.8 77.1 %collective-permute-start.2 = (f32[3,128]{0,1:T(8,128)S(1)}, f32[3,128]{0,1:T(8,128)S(1)}, u32[]{:S(2)}, u32[]{:S(2)}) collective-permute-start(f32[3,128]{0,1:T(8,128)S(1)} %select_bitcast_fusion.3), channel_id=1, source_target_pairs={{0,1},{1,2},{2,3},{3,4},{4,5},{5,6},{6,7},{7,8},{8,9},{9,10},{10,1... | collective-permute-start | bytes 4616 | tf_op jit(solution)/shard_map/ppermute | solution.py:18
  106.8 22.7 %all-to-all-start.2 = ((bf16[32,2,512]{2,1,0:T(2,128)(2,1)}), bf16[32,2,512]{2,1,0:T(2,128)(2,1)S(1)}, u32[]{:S(2)}, u32[]{:S(2)}) async-start(bf16[32,2,512]{2,1,0:T(2,128)(2,1)} %reshape.163), calls=%async_computation.2 | async-start | bytes 131072 | tf_op jit(solution)/shard_map/all_to_all | solution.py:49
  114.3 65.8 %collective-permute-start.3 = (f32[3,128]{0,1:T(8,128)S(1)}, f32[3,128]{0,1:T(8,128)S(1)}, u32[]{:S(2)}, u32[]{:S(2)}) collective-permute-start(f32[3,128]{0,1:T(8,128)S(1)} %select_bitcast_fusion.2), channel_id=1, source_target_pairs={{0,511},{1,0},{2,1},{3,2},{4,3},{5,4},{6,5},{7,6},{8,7},{9,8},{10,... | collective-permute-start | bytes 4616 | tf_op jit(solution)/shard_map/ppermute | solution.py:18
  118.0 68.0 %copy-start.9 = (f32[3]{0:T(128)S(1)}, f32[3]{0:T(128)}, u32[]{:S(2)}) copy-start(f32[3]{0:T(128)} %constant.174.clone) | copy-start | bytes 40
  118.0 80.7 %collective-permute-start.4 = (bf16[3,64,128]{1,0,2:T(4,128)(2,1)}, bf16[3,64,128]{1,0,2:T(4,128)(2,1)}, u32[]{:S(2)}, u32[]{:S(2)}) collective-permute-start(bf16[3,64,128]{1,0,2:T(4,128)(2,1)} %select_bitcast_fusion.1), channel_id=1, source_target_pairs={{0,1},{1,2},{2,3},{3,4},{4,5},{5,6},{6,7},{7,8},{8,9},{9,10},{10,1... | collective-permute-start | bytes 147464 | tf_op jit(solution)/shard_map/ppermute | solution.py:18
  130.2 21.1 %all-to-all-start.5 = ((bf16[32,2,512]{2,1,0:T(2,128)(2,1)}), bf16[32,2,512]{2,1,0:T(2,128)(2,1)S(1)}, u32[]{:S(2)}, u32[]{:S(2)}) async-start(bf16[32,2,512]{2,1,0:T(2,128)(2,1)} %broadcast_in_dim.108), calls=%async_computation.5 | async-start | bytes 131072 | tf_op jit(solution)/shard_map/all_to_all | solution.py:29
  151.9 18.5 %all-to-all-start.3 = ((bf16[32,2,512]{2,1,0:T(2,128)(2,1)}), bf16[32,2,512]{2,1,0:T(2,128)(2,1)S(1)}, u32[]{:S(2)}, u32[]{:S(2)}) async-start(bf16[32,2,512]{2,1,0:T(2,128)(2,1)} %broadcast_in_dim.107), calls=%async_computation.3 | async-start | bytes 131072 | tf_op jit(solution)/shard_map/all_to_all | solution.py:29
  155.8 68.2 %all-gather.2.cloned.1.call-start = ((), (), s32[]{:S(2)}) async-start(), calls=%async_computation.6 | async-start | bytes 2228224 | tf_op jit(solution)/shard_map/all_gather | solution.py:66
  170.5 16.1 %copy-start.10 = (bf16[64,64]{1,0:T(8,128)(2,1)S(1)}, bf16[64,64]{1,0:T(8,128)(2,1)}, u32[]{:S(2)}) copy-start(bf16[64,64]{1,0:T(8,128)(2,1)} %param.30) | copy-start | bytes 24580
  170.5 16.1 %copy-start.11 = (f32[64]{0:T(128)S(1)}, f32[64]{0:T(128)}, u32[]{:S(2)}) copy-start(f32[64]{0:T(128)} %param.31) | copy-start | bytes 772
  172.9 14.4 %copy-start.7 = (bf16[385]{0:T(512)(128)(2,1)}, bf16[385]{0:T(512)(128)(2,1)S(1)}, u32[]{:S(2)}) copy-start(bf16[385]{0:T(512)(128)(2,1)S(1)} %pad.13.clone) | copy-start | bytes 2314
  172.9 25.7 %collective-permute-start.5 = (bf16[3,64,128]{1,0,2:T(4,128)(2,1)}, bf16[3,64,128]{1,0,2:T(4,128)(2,1)}, u32[]{:S(2)}, u32[]{:S(2)}) collective-permute-start(bf16[3,64,128]{1,0,2:T(4,128)(2,1)} %select_bitcast_fusion), channel_id=1, source_target_pairs={{0,511},{1,0},{2,1},{3,2},{4,3},{5,4},{6,5},{7,6},{8,7},{9,8},{10,... | collective-permute-start | bytes 147464 | tf_op jit(solution)/shard_map/ppermute | solution.py:18
  187.3 8.0 %copy-start.6 = (bf16[20,192]{1,0:T(8,128)(2,1)S(1)}, bf16[20,192]{1,0:T(8,128)(2,1)}, u32[]{:S(2)}) copy-start(bf16[20,192]{1,0:T(8,128)(2,1)} %param.33) | copy-start | bytes 23044
  196.8 1.8 copy-start.8
  225.6 38.7 %copy-start.1 = (bf16[64,128]{1,0:T(8,128)(2,1)S(1)}, bf16[64,128]{1,0:T(8,128)(2,1)}, u32[]{:S(2)}) copy-start(bf16[64,128]{1,0:T(8,128)(2,1)} %param.23) | copy-start | bytes 49156
Sparse Core Ops, SparseCore 0:
  171.4 33.9 all-gather.1
where the time goes:
time: 273 us; the launch traced here: 272 us
  matrix products  75.6 us (28%)
  starting transfers between devices  68.9 us (25%)
  waiting for transfers between devices  49.4 us (18%)
  local copies, waits for them, and re-layouts  46.9 us (17%)
  other arithmetic  14.7 us (5%)
  between operations  14.7 us (5%)
    dot_general x32, matrix products, over_last(): lax.dot_general(first_operand, second_operand, (((1,), (1,)), ((), ())),...  36.4 us
    all_to_all x4, waiting for transfers between devices, sent_to_all(): return lax.all_to_all(copies, axis, split_axis=0, concat_axis=0, tiled=True)  35 us
    all_to_all x4, starting transfers between devices, sent_to_all(): return lax.all_to_all(copies, axis, split_axis=0, concat_axis=0, tiled=True)  25.5 us
    ppermute x6, starting transfers between devices, shifted(): return lax.ppermute(value, axis, pairs)  21.9 us
    all_to_all x2, starting transfers between devices, sum_at_owner(): lax.all_to_all(pieces, axis, split_axis=0, concat_axis=0, tiled=True)  21.4 us
    dot_general x16, matrix products, one_block(): jnp.dot(feat_block, sine_table, preferred_element_type=jnp.float32)  18.7 us
    dot_general x16, matrix products, one_block(): jnp.dot(feat_block, cosine_table, preferred_element_type=jnp.float32)  18.6 us
    gather x1, local copies, waits for them, and re-layouts, short_range(): jnp.take(ext_vec, flat_ids, axis=2)  15.5 us
  transfers between devices with their start and end apart: 13, of which 5 were waited for; matrix products, arithmetic and copies ran while one was open for 35% of the time, Pallas kernels for 0%

commit v1 on v0

v1 whole, which is shorter than its diff:
```python
import math

import jax
import jax.numpy as jnp
from jax import lax
from jax.experimental import pallas as pl
from jax.experimental.pallas import tpu as pltpu
from jax.sharding import Mesh
from jax.sharding import PartitionSpec as P

F = 64
NRBF = 20
NBR = 16
ATOM = 128
KDEV = 256
PLANE = 32
DEPTH = 16
SLABS = 512
KVEC = 8192
ATOMS = 65536
PACK = 80
HALO_ROWS = 288
EXT_ROWS = 416

plane_axes = ("yh", "yl", "x", "c")
kb_axes = ("yl", "x", "c")
all_axes = ("yh", "z", "yl", "x", "c")

side_length = 6.0
slab_depth = 6.0
radial_reach = 6.0
distance_floor = 1.0
norm_scale = 1.0 / math.sqrt(KVEC * ATOMS)

sine_terms = (4.44287959, -7.30781805, 3.59778873, -0.79123821)
cosine_terms = (1.41420408, -6.97764206, 5.71523839, -1.72834865)
whole_turns = 1.5 * 2.0**23

VMEM_LIMIT = 40 * 2**20


def dot(a, b, dims):
    return lax.dot_general(a, b, (dims, ((), ())), preferred_element_type=jnp.float32)


def in_three(value):
    first = value.astype(jnp.bfloat16)
    rest = value - first.astype(jnp.float32)
    second = rest.astype(jnp.bfloat16)
    third = (rest - second.astype(jnp.float32)).astype(jnp.bfloat16)
    return first, second, third


def polynomial(terms, u):
    value = terms[-1] * u + terms[-2]
    for term in terms[-3::-1]:
        value = value * u + term
    return value


def cosine_and_sine(turns):
    r = turns - ((turns + whole_turns) - whole_turns)
    u = r * r
    s = r * polynomial(sine_terms, u)
    c = polynomial(cosine_terms, u)
    return 1.0 - s * s, s * c


def call(kernel, outs, scratch=(), flops=0, bytes_accessed=0, smem=0, count=0):
    vmem = pl.BlockSpec(memory_space=pltpu.VMEM)
    scalars = [pl.BlockSpec(memory_space=pltpu.SMEM)] * smem
    return pl.pallas_call(
        kernel,
        out_shape=outs,
        in_specs=scalars + [vmem] * count,
        out_specs=jax.tree.map(lambda _: vmem, outs),
        scratch_shapes=list(scratch),
        compiler_params=pltpu.CompilerParams(vmem_limit_bytes=VMEM_LIMIT),
        cost_estimate=pl.CostEstimate(flops=flops, bytes_accessed=bytes_accessed, transcendentals=0),
    )


def pack_kernel(feat, pos, weight, out):
    projected = dot(weight[...], feat[...], ((0,), (0,))).astype(jnp.bfloat16)
    pieces = in_three(pos[...])
    pad = jnp.zeros((PACK - F - 9, ATOM), jnp.bfloat16)
    row = jnp.concatenate([projected, *pieces, pad], axis=0)
    for p in range(PLANE):
        out[p] = row


def halo_kernel(feat, vec, pos, halo, up, down):
    pieces = in_three(pos[...])
    pad = jnp.zeros((5, ATOM), jnp.bfloat16)
    tail = jnp.zeros((HALO_ROWS - 280, ATOM), jnp.bfloat16)
    rows = jnp.concatenate(
        [feat[...], vec[0], vec[1], vec[2], pieces[0], pad, pieces[1], pad, pieces[2], pad, tail], axis=0
    )
    atom = lax.broadcasted_iota(jnp.int32, (ATOM, ATOM), 0)
    for side, out in ((0, up), (1, down)):
        chosen = jnp.where(atom == halo[side : side + 1, :], 1.0, 0.0).astype(jnp.bfloat16)
        out[...] = dot(rows, chosen, ((1,), (0,))).astype(jnp.bfloat16)


def table_kernel(k_at, got, lattice, table, partial, columns, total):
    rows = lattice[:, pl.ds(pl.multiple_of(k_at[0], KDEV), KDEV)].astype(jnp.float32)
    turned = jnp.concatenate([rows, jnp.zeros((5, KDEV), jnp.float32)], axis=0).T
    for i in range(3):
        columns[i] = jnp.broadcast_to(turned[:, i : i + 1], (KDEV, ATOM))
    total[...] = jnp.zeros_like(total)

    @pl.loop(0, PLANE // 2)
    def _(step):
        left, right = got[2 * step], got[2 * step + 1]
        both = jnp.concatenate([left, right], axis=1)
        pieces = both[F : F + 16].astype(jnp.float32)
        pos = pieces[0:3] + pieces[3:6] + pieces[6:9]
        at = pl.ds(pl.multiple_of(step * 2 * ATOM, 2 * ATOM), 2 * ATOM)
        for k in range(0, KDEV, 32):
            halves = []
            for half in range(2):
                lanes = slice(half * ATOM, (half + 1) * ATOM)
                turns = (
                    columns[0, k : k + 32] * pos[0:1, lanes] + columns[1, k : k + 32] * pos[1:2, lanes]
                ) + columns[2, k : k + 32] * pos[2:3, lanes]
                halves.append(cosine_and_sine(turns))
            for i in range(2):
                table[i * KDEV + k : i * KDEV + k + 32, at] = jnp.concatenate(
                    [halves[0][i], halves[1][i]], axis=1
                ).astype(jnp.bfloat16)
        total[...] += dot(table[:, at], both[:F], ((1,), (1,)))

    partial[...] = jnp.concatenate([total[:KDEV], total[KDEV:]], axis=1).astype(jnp.bfloat16)


def sum_kernel(arrived, out):
    total = arrived[0].astype(jnp.float32)
    for i in range(1, DEPTH):
        total = total + arrived[i].astype(jnp.float32)
    total = total.astype(jnp.bfloat16)
    for i in range(DEPTH):
        out[i] = total


def project_kernel(half_at, got, kfilter, table, out):
    total = got[...].astype(jnp.float32).T
    own = kfilter[:, pl.ds(pl.multiple_of(half_at[0], KDEV), KDEV)]
    filtered = jnp.concatenate([own * total[:F] * norm_scale, own * total[F:] * norm_scale], axis=1)
    filtered = filtered.astype(jnp.bfloat16)

    @pl.loop(0, PLANE // 2)
    def _(step):
        at = pl.ds(pl.multiple_of(step * 2 * ATOM, 2 * ATOM), 2 * ATOM)
        message = dot(filtered, table[:, at], ((1,), (0,))).astype(jnp.bfloat16)
        out[2 * step] = message[:, :ATOM]
        out[2 * step + 1] = message[:, ATOM:]


def finish_kernel(arrived, scalar, out):
    total = arrived[0].astype(jnp.float32)
    for i in range(1, PLANE):
        total = total + arrived[i].astype(jnp.float32)
    out[...] = (scalar[...] + total).astype(jnp.bfloat16)


def short_kernel(
    feat, vec, pos, ids, below, above, node_weight, bias, message_weight, radial_weight,
    scalar_out, vector_out, ext, chosen, filters, directions,
):
    pieces = in_three(pos[...])
    pad = jnp.zeros((5, ATOM), jnp.bfloat16)
    tail = jnp.zeros((8, ATOM), jnp.bfloat16)
    own_tail = jnp.concatenate([pieces[0], pad, pieces[1], pad, pieces[2], pad, tail], axis=0)
    own_vec = jnp.concatenate([vec[0], vec[1], vec[2]], axis=0)
    ext[192:, :ATOM] = jnp.concatenate([own_vec, own_tail], axis=0)
    ext[192:, ATOM : 2 * ATOM] = below[F:]
    ext[192:, 2 * ATOM :] = above[F:]
    ext_feat = jnp.concatenate([feat[...], below[:F], above[:F]], axis=1)
    hidden = dot(node_weight[...], ext_feat, ((0,), (0,))) + bias[...]
    hidden = (hidden / (1.0 + jnp.exp(-hidden))).astype(jnp.bfloat16)
    ext[:192] = dot(message_weight[...], hidden, ((0,), (0,))).astype(jnp.bfloat16)

    number = lax.broadcasted_iota(jnp.int32, (3 * ATOM, ATOM), 0)
    for j in range(NBR):
        chosen[:, j * ATOM : (j + 1) * ATOM] = jnp.where(number == ids[j : j + 1, :], 1.0, 0.0).astype(jnp.bfloat16)
    found = dot(ext[384:], chosen[...], ((1,), (0,)))
    there = found[0:3] + found[8:11] + found[16:19]
    here = jnp.concatenate([pos[...]] * NBR, axis=1)
    offset = there - here
    offset = offset - jnp.floor(offset + 0.5)
    side = lax.broadcasted_iota(jnp.int32, (3, 1), 0)
    box = jnp.where(side == 2, slab_depth * SLABS, side_length).astype(jnp.float32)
    cartesian = offset * box
    square = cartesian * cartesian
    distance = jnp.sqrt(square[0:1] + square[1:2] + square[2:3])
    directions[0:3] = cartesian / jnp.maximum(distance, distance_floor)
    center = lax.broadcasted_iota(jnp.int32, (NRBF, 1), 0).astype(jnp.float32) * (radial_reach / (NRBF - 1))
    away = (distance - center) / (1.5 * radial_reach / NRBF)
    radial = jnp.exp(-(away * away)).astype(jnp.bfloat16)
    filters[...] = dot(radial_weight[...], radial, ((0,), (0,)))

    def slots(step, sums):
        at = pl.ds(pl.multiple_of(step * 2 * ATOM, 2 * ATOM), 2 * ATOM)
        picked = dot(ext[:384], chosen[:, at], ((1,), (0,)))
        terms = picked[:192] * filters[:, at]
        toward = directions[:, at]
        parts = [terms[:F]]
        for x in range(3):
            parts.append(
                picked[192 + x * F : 192 + (x + 1) * F] * terms[F : 2 * F] + terms[2 * F :] * toward[x : x + 1]
            )
        return tuple(s + p[:, :ATOM] + p[:, ATOM:] for s, p in zip(sums, parts))

    zero = jnp.zeros((F, ATOM), jnp.float32)
    sums = lax.fori_loop(0, NBR // 2, slots, (zero,) * 4)
    scalar_out[...] = feat[...].astype(jnp.float32) + sums[0]
    for x in range(3):
        vector_out[x] = (vec[x].astype(jnp.float32) + sums[1 + x]).astype(jnp.bfloat16)


def exchanged(x, axes):
    return lax.all_to_all(x, axes, split_axis=0, concat_axis=0, tiled=True)


def shifted(x, steps):
    return lax.ppermute(x, all_axes, [(i, (i + steps) % SLABS) for i in range(SLABS)])


def shards(
    features, vectors, positions, neighbours, halo_lists, lattice, kspace_filter,
    node_weight, node_bias, message_weight, radial_weight, ewald_weight,
):
    bf16, f32 = jnp.bfloat16, jnp.float32
    shape = jax.ShapeDtypeStruct
    half_at = (lax.axis_index("yh") * KDEV).astype(jnp.int32).reshape(1)
    k_at = (lax.axis_index(kb_axes) * 2 * KDEV + half_at).astype(jnp.int32).reshape(1)
    packed = call(pack_kernel, shape((PLANE, PACK, ATOM), bf16), count=3)(features, positions, ewald_weight)
    got = exchanged(packed, plane_axes)
    up, down = call(halo_kernel, (shape((HALO_ROWS, ATOM), bf16),) * 2, count=4)(
        features, vectors, positions, halo_lists
    )
    below, above = shifted(up, 1), shifted(down, -1)
    table, partial = call(
        table_kernel,
        (shape((2 * KDEV, PLANE * ATOM), bf16), shape((KDEV, 2 * F), bf16)),
        scratch=[pltpu.VMEM((3, KDEV, ATOM), f32), pltpu.VMEM((2 * KDEV, F), f32)],
        smem=1,
        count=2,
    )(k_at, got, lattice)
    arrived = exchanged(partial.reshape(DEPTH, KDEV // DEPTH, 2 * F), "z")
    scalar, new_vectors = call(
        short_kernel,
        (shape((F, ATOM), f32), shape((3, F, ATOM), bf16)),
        scratch=[
            pltpu.VMEM((EXT_ROWS, 3 * ATOM), bf16),
            pltpu.VMEM((3 * ATOM, NBR * ATOM), bf16),
            pltpu.VMEM((192, NBR * ATOM), f32),
            pltpu.VMEM((8, NBR * ATOM), f32),
        ],
        count=10,
    )(
        features, vectors, positions, neighbours, below, above,
        node_weight, node_bias[:, None], message_weight, radial_weight,
    )
    owned = call(sum_kernel, shape((DEPTH, KDEV // DEPTH, 2 * F), bf16), count=1)(arrived)
    totals = exchanged(owned, "z").reshape(KDEV, 2 * F)
    messages = call(project_kernel, shape((PLANE, F, ATOM), bf16), smem=1, count=3)(
        half_at, totals, kspace_filter, table
    )
    returned = exchanged(messages, plane_axes)
    new_features = call(finish_kernel, shape((F, ATOM), bf16), count=2)(returned, scalar)
    return new_features, new_vectors


def solution(mesh):
    fine = Mesh(mesh.devices.reshape(2, 16, 2, 4, 2), all_axes)
    atoms = P(None, all_axes)
    placed = (
        atoms, P(None, None, all_axes), atoms, atoms, atoms, P(), P(None, kb_axes),
        P(), P(), P(), P(), P(),
    )
    return jax.shard_map(
        shards,
        mesh=fine,
        in_specs=placed,
        out_specs=(atoms, P(None, None, all_axes)),
        check_vma=False,
    )
```

time: 273 us -> 101 us (0.37)
  matrix products: 75.6 us -> 0 us
  starting transfers between devices: 68.9 us -> 22.4 us
  local copies, waits for them, and re-layouts: 46.9 us -> 4.06 us
  blocking collectives: 0 us -> 39.5 us
  waiting for transfers between devices: 49.4 us -> 16.9 us
  Pallas kernels: 0 us -> 15.8 us
  other arithmetic: 14.7 us -> 0 us
  between operations: 14.7 us -> 0.79 us
    dot_general x67 -> x0, matrix products: 75.6 us -> none  [the longest x32 36.4 us: over_last(): lax.dot_general(first_operand, second_operand, (((1,), (1,)), ((), ())),...]
    all_to_all x0 -> x2, blocking collectives: none -> 39.5 us  [exchanged(): return lax.all_to_all(x, axes, split_axis=0, concat_axis=0, tiled=True)]
    all_to_all x6 -> x2, waiting for transfers between devices: 49.3 us -> 13 us  [exchanged(): return lax.all_to_all(x, axes, split_axis=0, concat_axis=0, tiled=True)]
    gather x11 -> x0, local copies, waits for them, and re-layouts: 33.5 us -> none  [the longest x1 15.5 us: short_range(): jnp.take(ext_vec, flat_ids, axis=2)]
    all_to_all x6 -> x2, starting transfers between devices: 46.9 us -> 16.9 us  [exchanged(): return lax.all_to_all(x, axes, split_axis=0, concat_axis=0, tiled=True)]
    ppermute x6 -> x2, starting transfers between devices: 21.9 us -> 5.46 us  [shifted(): lax.ppermute(x, all_axes, [(i, (i + steps) % SLABS) for i in range(SLABS)])]
    pallas_call x0 -> x7, Pallas kernels: none -> 15.8 us  [the longest x1 6.17 us: shards(): call(table_kernel, (shape((2 * KDEV, PLANE * ATOM), bf16), shape((KDEV, 2...]
    reduce_sum x5 -> x0, other arithmetic: 7.08 us -> none  [the longest x1 6.74 us: short_range(): jnp.sum(neighbour_vec * edge_terms[channels:2 * channels][None] + edge_te...]
  transfers between devices with their start and end apart: 13 -> 4, of which waited for: 5 -> 3; matrix products, arithmetic and copies ran while one was open for 35% -> 0% of each run, Pallas kernels for 0% -> 4%
where the time goes in v1:
time: 101 us; the launch traced here: 99.6 us
  blocking collectives  39.5 us (39%)
  starting transfers between devices  22.4 us (22%)
  waiting for transfers between devices  16.9 us (17%)
  Pallas kernels  15.8 us (16%)
  local copies, waits for them, and re-layouts  4.06 us (4%)
    all_to_all x2, blocking collectives, exchanged(): return lax.all_to_all(x, axes, split_axis=0, concat_axis=0, tiled=True)  39.5 us
    all_to_all x2, starting transfers between devices, exchanged(): return lax.all_to_all(x, axes, split_axis=0, concat_axis=0, tiled=True)  16.9 us
    all_to_all x2, waiting for transfers between devices, exchanged(): return lax.all_to_all(x, axes, split_axis=0, concat_axis=0, tiled=True)  13 us
    pallas_call x1, Pallas kernels, shards(): call(table_kernel, (shape((2 * KDEV, PLANE * ATOM), bf16), shape((KDEV, 2...  6.17 us
    ppermute x2, starting transfers between devices, shifted(): lax.ppermute(x, all_axes, [(i, (i + steps) % SLABS) for i in range(SLABS)])  5.46 us
    unnamed x28, local copies, waits for them, and re-layouts  3.97 us
    ppermute x2, waiting for transfers between devices, shifted(): lax.ppermute(x, all_axes, [(i, (i + steps) % SLABS) for i in range(SLABS)])  3.93 us
    pallas_call x1, Pallas kernels, shards(): call(short_kernel, (shape((F, ATOM), f32), shape((3, F, ATOM), bf16)), sc...  3.92 us
  transfers between devices with their start and end apart: 4, of which 3 were waited for; matrix products, arithmetic and copies ran while one was open for 0% of the time, Pallas kernels for 4%

profile of v1, /device:TPU:1, one launch (start us, length us, event | category | flops | bytes accessed | tf_op | source)
XLA Modules:
  0.0 99.6 jit_solution(13391869633635949923)
XLA Ops:
  0.6 0.0 copy-start.1
  0.6 0.7 copy-done.1
  1.4 0.7 copy-done.6
  2.0 0.7 copy-done.8
  2.8 1.1 %shard_map.131 = bf16[32,80,128]{2,1,0:T(8,128)(2,1)} custom-call(bf16[64,128]{1,0:T(8,128)(2,1)S(1)} %copy-done.1, f32[3,128]{1,0:T(4,128)S(1)} %copy-done.6, bf16[64,64]{1,0:T(8,128)(2,1)S(1)} %copy-done.8), custom_call_target="tpu_custom_call" | custom-call | tf_op jit(solution)/shard_map/pallas_call | solution.py:237
  3.8 0.0 copy-start.13
  3.9 0.0 copy-start.5
  3.9 0.0 copy-start.9
  3.9 0.0 copy-start.10
  3.9 0.0 copy-start.11
  3.9 10.6 %all-to-all-start = ((bf16[32,80,128]{2,1,0:T(8,128)(2,1)}), bf16[32,80,128]{2,1,0:T(8,128)(2,1)S(1)}, u32[]{:S(2)}, u32[]{:S(2)}) async-start(bf16[32,80,128]{2,1,0:T(8,128)(2,1)} %shard_map.131), calls=%async_computation | async-start | bytes 1310720 | tf_op jit(solution)/shard_map/all_to_all | solution.py:222
  14.5 13.0 %all-to-all-done.got = bf16[32,80,128]{2,1,0:T(8,128)(2,1)S(1)} async-done(((bf16[32,80,128]{2,1,0:T(8,128)(2,1)}), bf16[32,80,128]{2,1,0:T(8,128)(2,1)S(1)}, u32[]{:S(2)}, u32[]{:S(2)}) %all-to-all-start) | async-done | bytes 655392 | tf_op jit(solution)/shard_map/all_to_all | solution.py:222
  27.5 0.9 copy-done.4
  28.4 6.2 %shard_map.132 = (bf16[512,4096]{1,0:T(8,128)(2,1)S(1)}, bf16[256,128]{1,0:T(8,128)(2,1)S(1)}) custom-call(s32[1]{0:T(128)S(6)} %add.15.k_at, bf16[32,80,128]{2,1,0:T(8,128)(2,1)S(1)} %all-to-all-done.got, s32[3,8192]{1,0:T(4,128)S(1)} %copy-done.4), custom_call_target="tpu_custom_call" | custom-call | tf_op jit(solution)/shard_map/pallas_call | solution.py:243
  34.6 24.3 %all_to_all.20.arrived = bf16[16,16,128]{2,1,0:T(8,128)(2,1)S(1)} all-to-all(bf16[16,16,128]{2,1,0:T(8,128)(2,1)S(1)} %bitcast.6), channel_id=1, replica_groups=mesh['yh'=2,'z'=16,'yl'=2,'x'=4,'c'=2] {'z'}, dimensions={0} | all-to-all | bytes 131072 | tf_op jit(solution)/shard_map/all_to_all | solution.py:222
  58.9 15.2 %all_to_all.21 = bf16[16,16,128]{2,1,0:T(8,128)(2,1)S(1)} all-to-all(bf16[16,16,128]{2,1,0:T(8,128)(2,1)S(1)} %shard_map.133), channel_id=1, replica_groups=mesh['yh'=2,'z'=16,'yl'=2,'x'=4,'c'=2] {'z'}, dimensions={0} | all-to-all | bytes 131072 | tf_op jit(solution)/shard_map/all_to_all | solution.py:222
  74.2 0.9 copy-done.3
  75.1 3.7 %shard_map.134 = bf16[32,64,128]{2,1,0:T(8,128)(2,1)} custom-call(s32[1]{0:T(128)} %bitcast.half_at, bf16[256,128]{1,0:T(8,128)(2,1)S(1)} %bitcast.5, f32[64,512]{1,0:T(8,128)S(1)} %copy-done.3, bf16[512,4096]{1,0:T(8,128)(2,1)S(1)} %get-tuple-element.9.table), custom_call_target="tpu_custom_call" | custom-call | tf_op jit(solution)/shard_map/pallas_call | solution.py:267
  78.8 6.4 %all-to-all-start.3 = ((bf16[32,64,128]{2,1,0:T(8,128)(2,1)}), bf16[32,64,128]{2,1,0:T(8,128)(2,1)S(1)}, u32[]{:S(2)}, u32[]{:S(2)}) async-start(bf16[32,64,128]{2,1,0:T(8,128)(2,1)} %shard_map.134), calls=%async_computation.3 | async-start | bytes 1048576 | tf_op jit(solution)/shard_map/all_to_all | solution.py:222
  85.2 0.0 copy-done
  85.2 0.0 copy-done.2
  85.2 0.2 shard_map.135
  85.4 3.5 %collective-permute-start = (bf16[288,128]{1,0:T(8,128)(2,1)S(1)}, bf16[288,128]{1,0:T(8,128)(2,1)S(1)}, u32[]{:S(2)}, u32[]{:S(2)}) collective-permute-start(bf16[288,128]{1,0:T(8,128)(2,1)S(1)} %get-tuple-element.10), channel_id=1, source_target_pairs={{0,1},{1,2},{2,3},{3,4},{4,5},{5,6},{6,7},{7,8},{8,9},{9,10},{10,1... | collective-permute-start | bytes 221192 | tf_op jit(solution)/shard_map/ppermute | solution.py:226
  89.0 1.9 %collective-permute-start.1 = (bf16[288,128]{1,0:T(8,128)(2,1)S(1)}, bf16[288,128]{1,0:T(8,128)(2,1)S(1)}, u32[]{:S(2)}, u32[]{:S(2)}) collective-permute-start(bf16[288,128]{1,0:T(8,128)(2,1)S(1)} %get-tuple-element.11), channel_id=1, source_target_pairs={{0,511},{1,0},{2,1},{3,2},{4,3},{5,4},{6,5},{7,6},{8,7},{9,8},{10,... | collective-permute-start | bytes 221192 | tf_op jit(solution)/shard_map/ppermute | solution.py:226
  90.9 0.1 copy.14.bias
  91.0 1.2 %collective-permute-done.below = bf16[288,128]{1,0:T(8,128)(2,1)S(1)} collective-permute-done((bf16[288,128]{1,0:T(8,128)(2,1)S(1)}, bf16[288,128]{1,0:T(8,128)(2,1)S(1)}, u32[]{:S(2)}, u32[]{:S(2)}) %collective-permute-start) | collective-permute-done | bytes 73760 | tf_op jit(solution)/shard_map/ppermute | solution.py:226
  92.2 2.7 %collective-permute-done.1.above = bf16[288,128]{1,0:T(8,128)(2,1)S(1)} collective-permute-done((bf16[288,128]{1,0:T(8,128)(2,1)S(1)}, bf16[288,128]{1,0:T(8,128)(2,1)S(1)}, u32[]{:S(2)}, u32[]{:S(2)}) %collective-permute-start.1) | collective-permute-done | bytes 73760 | tf_op jit(solution)/shard_map/ppermute | solution.py:226
  94.9 0.0 copy-done.10
  94.9 0.0 copy-done.11
  94.9 3.9 %shard_map.136 = (f32[64,128]{1,0:T(8,128)S(1)}, bf16[3,64,128]{2,1,0:T(8,128)(2,1)}) custom-call(bf16[64,128]{1,0:T(8,128)(2,1)S(1)} %copy-done.2, bf16[3,64,128]{2,1,0:T(8,128)(2,1)S(1)} %copy-done, f32[3,128]{1,0:T(4,128)S(1)} %copy-done.7, s32[16,128]{1,0:T(8,128)S(1)} %copy-done.11, bf16[288,128]{1,0:T(8,128)(2,1)S(1)} %collective-permute-done.below, ...), custom_call_target="tpu_custom_call" | custom-call | tf_op jit(solution)/shard_map/pallas_call | solution.py:251
  98.9 0.0 all-to-all-done.3.arrived
  98.9 0.7 shard_map.137
  (14 shorter events, 0.0 us)
Async XLA Ops:
  0.6 0.7 copy-start.1
  1.4 0.7 copy-start.6
  2.0 0.7 copy-start.8
  3.8 81.4 %copy-start = (bf16[3,64,128]{2,1,0:T(8,128)(2,1)S(1)}, bf16[3,64,128]{2,1,0:T(8,128)(2,1)}, u32[]{:S(2)}) copy-start(bf16[3,64,128]{2,1,0:T(8,128)(2,1)} %vec.3) | copy-start | bytes 147460
  3.8 81.4 %copy-start.2 = (bf16[64,128]{1,0:T(8,128)(2,1)S(1)}, bf16[64,128]{1,0:T(8,128)(2,1)}, u32[]{:S(2)}) copy-start(bf16[64,128]{1,0:T(8,128)(2,1)} %feat.5) | copy-start | bytes 49156
  3.8 81.4 %copy-start.7 = (f32[3,128]{1,0:T(4,128)S(1)}, f32[3,128]{1,0:T(4,128)}, u32[]{:S(2)}) copy-start(f32[3,128]{1,0:T(4,128)} %pos.5) | copy-start | bytes 4612
  3.8 81.4 %copy-start.12 = (s32[2,128]{1,0:T(2,128)S(1)}, s32[2,128]{1,0:T(2,128)}, u32[]{:S(2)}) copy-start(s32[2,128]{1,0:T(2,128)} %halo.1) | copy-start | bytes 3076
  3.8 87.0 %copy-start.13 = (f32[64]{0:T(128)S(1)}, f32[64]{0:T(128)}, u32[]{:S(2)}) copy-start(f32[64]{0:T(128)} %param.20) | copy-start | bytes 772
  3.9 91.1 %copy-start.5 = (bf16[64,192]{1,0:T(8,128)(2,1)S(1)}, bf16[64,192]{1,0:T(8,128)(2,1)}, u32[]{:S(2)}) copy-start(bf16[64,192]{1,0:T(8,128)(2,1)} %message_weight.1) | copy-start | bytes 73732
  3.9 91.1 %copy-start.9 = (bf16[64,64]{1,0:T(8,128)(2,1)S(1)}, bf16[64,64]{1,0:T(8,128)(2,1)}, u32[]{:S(2)}) copy-start(bf16[64,64]{1,0:T(8,128)(2,1)} %node_weight.1) | copy-start | bytes 24580
  3.9 91.1 %copy-start.10 = (bf16[20,192]{1,0:T(8,128)(2,1)S(1)}, bf16[20,192]{1,0:T(8,128)(2,1)}, u32[]{:S(2)}) copy-start(bf16[20,192]{1,0:T(8,128)(2,1)} %radial_weight.1) | copy-start | bytes 23044
  3.9 91.1 %copy-start.11 = (s32[16,128]{1,0:T(8,128)S(1)}, s32[16,128]{1,0:T(8,128)}, u32[]{:S(2)}) copy-start(s32[16,128]{1,0:T(8,128)} %ids.1) | copy-start | bytes 24580
  3.9 23.6 %all-to-all-start = ((bf16[32,80,128]{2,1,0:T(8,128)(2,1)}), bf16[32,80,128]{2,1,0:T(8,128)(2,1)S(1)}, u32[]{:S(2)}, u32[]{:S(2)}) async-start(bf16[32,80,128]{2,1,0:T(8,128)(2,1)} %shard_map.131), calls=%async_computation | async-start | bytes 1310720 | tf_op jit(solution)/shard_map/all_to_all | solution.py:222
  27.5 0.9 copy-start.4
  74.2 0.9 copy-start.3
  78.8 20.1 %all-to-all-start.3 = ((bf16[32,64,128]{2,1,0:T(8,128)(2,1)}), bf16[32,64,128]{2,1,0:T(8,128)(2,1)S(1)}, u32[]{:S(2)}, u32[]{:S(2)}) async-start(bf16[32,64,128]{2,1,0:T(8,128)(2,1)} %shard_map.134), calls=%async_computation.3 | async-start | bytes 1048576 | tf_op jit(solution)/shard_map/all_to_all | solution.py:222
  85.4 6.8 %collective-permute-start = (bf16[288,128]{1,0:T(8,128)(2,1)S(1)}, bf16[288,128]{1,0:T(8,128)(2,1)S(1)}, u32[]{:S(2)}, u32[]{:S(2)}) collective-permute-start(bf16[288,128]{1,0:T(8,128)(2,1)S(1)} %get-tuple-element.10), channel_id=1, source_target_pairs={{0,1},{1,2},{2,3},{3,4},{4,5},{5,6},{6,7},{7,8},{8,9},{9,10},{10,1... | collective-permute-start | bytes 221192 | tf_op jit(solution)/shard_map/ppermute | solution.py:226
  89.0 6.0 %collective-permute-start.1 = (bf16[288,128]{1,0:T(8,128)(2,1)S(1)}, bf16[288,128]{1,0:T(8,128)(2,1)S(1)}, u32[]{:S(2)}, u32[]{:S(2)}) collective-permute-start(bf16[288,128]{1,0:T(8,128)(2,1)S(1)} %get-tuple-element.11), channel_id=1, source_target_pairs={{0,511},{1,0},{2,1},{3,2},{4,3},{5,4},{6,5},{7,6},{8,7},{9,8},{10,... | collective-permute-start | bytes 221192 | tf_op jit(solution)/shard_map/ppermute | solution.py:226

commit v2 on v1

--- a/solution.py
+++ b/solution.py
@@ -21,6 +21,7 @@
 PACK = 80
 HALO_ROWS = 288
 EXT_ROWS = 416
+GROUP = 8
 
 plane_axes = ("yh", "yl", "x", "c")
 kb_axes = ("yl", "x", "c")
@@ -36,7 +37,8 @@
 cosine_terms = (1.41420408, -6.97764206, 5.71523839, -1.72834865)
 whole_turns = 1.5 * 2.0**23
 
-VMEM_LIMIT = 40 * 2**20
+VMEM_LIMIT = 16 * 2**20
+TABLE_LIMIT = 51 * 2**20
 
 
 def dot(a, b, dims):
@@ -66,30 +68,33 @@
     return 1.0 - s * s, s * c
 
 
-def call(kernel, outs, scratch=(), flops=0, bytes_accessed=0, smem=0, count=0):
-    vmem = pl.BlockSpec(memory_space=pltpu.VMEM)
-    scalars = [pl.BlockSpec(memory_space=pltpu.SMEM)] * smem
+VM, SM, ANY, FAR = pltpu.VMEM, pltpu.SMEM, pl.ANY, pltpu.HBM
+
+
+def call(kernel, places, outs, *operands, scratch=(), out_places=None, limit=VMEM_LIMIT):
     return pl.pallas_call(
         kernel,
         out_shape=outs,
-        in_specs=scalars + [vmem] * count,
-        out_specs=jax.tree.map(lambda _: vmem, outs),
+        in_specs=[pl.BlockSpec(memory_space=place) for place in places],
+        out_specs=jax.tree.map(lambda _: pl.BlockSpec(memory_space=VM), outs)
+        if out_places is None
+        else tuple(pl.BlockSpec(memory_space=place) for place in out_places),
         scratch_shapes=list(scratch),
-        compiler_params=pltpu.CompilerParams(vmem_limit_bytes=VMEM_LIMIT),
-        cost_estimate=pl.CostEstimate(flops=flops, bytes_accessed=bytes_accessed, transcendentals=0),
-    )
-
-
-def pack_kernel(feat, pos, weight, out):
-    projected = dot(weight[...], feat[...], ((0,), (0,))).astype(jnp.bfloat16)
-    pieces = in_three(pos[...])
+        compiler_params=pltpu.CompilerParams(vmem_limit_bytes=limit),
+        cost_estimate=pl.CostEstimate(flops=0, bytes_accessed=0, transcendentals=0),
+    )(*operands)
+
+
+def packed_for_all(feat, pos, count):
+    first = lax.reduce_precision(pos, 8, 7)
+    second = lax.reduce_precision(pos - first, 8, 7)
+    third = (pos - first) - second
+    pieces = [piece.astype(jnp.bfloat16) for piece in (first, second, third)]
     pad = jnp.zeros((PACK - F - 9, ATOM), jnp.bfloat16)
-    row = jnp.concatenate([projected, *pieces, pad], axis=0)
-    for p in range(PLANE):
-        out[p] = row
-
-
-def halo_kernel(feat, vec, pos, halo, up, down):
+    return jnp.broadcast_to(jnp.concatenate([feat, *pieces, pad], axis=0), (count, PACK, ATOM))
+
+
+def prepare_kernel(places, feat, vec, pos, halo, lattice, kfilter, up, down, columns, own_filter):
     pieces = in_three(pos[...])
     pad = jnp.zeros((5, ATOM), jnp.bfloat16)
     tail = jnp.zeros((HALO_ROWS - 280, ATOM), jnp.bfloat16)
@@ -100,40 +105,58 @@
     for side, out in ((0, up), (1, down)):
         chosen = jnp.where(atom == halo[side : side + 1, :], 1.0, 0.0).astype(jnp.bfloat16)
         out[...] = dot(rows, chosen, ((1,), (0,))).astype(jnp.bfloat16)
-
-
-def table_kernel(k_at, got, lattice, table, partial, columns, total):
-    rows = lattice[:, pl.ds(pl.multiple_of(k_at[0], KDEV), KDEV)].astype(jnp.float32)
-    turned = jnp.concatenate([rows, jnp.zeros((5, KDEV), jnp.float32)], axis=0).T
+    own = lattice[:, pl.ds(pl.multiple_of(places[0], KDEV), KDEV)].astype(jnp.float32)
+    turned = jnp.concatenate([own, jnp.zeros((5, KDEV), jnp.float32)], axis=0).T
     for i in range(3):
         columns[i] = jnp.broadcast_to(turned[:, i : i + 1], (KDEV, ATOM))
+    own_filter[...] = kfilter[:, pl.ds(pl.multiple_of(places[1], KDEV), KDEV)] * norm_scale
+
+
+def table_kernel(got, columns, weight, below, above, own_filter, table_at, partial, table, total, done):
     total[...] = jnp.zeros_like(total)
 
-    @pl.loop(0, PLANE // 2)
+    def stored(step):
+        columns_of = pl.ds(pl.multiple_of(step * GROUP * ATOM, GROUP * ATOM), GROUP * ATOM)
+        return pltpu.make_async_copy(table.at[:, columns_of], table_at.at[:, columns_of], done.at[step])
+
+    @pl.loop(0, PLANE // GROUP)
     def _(step):
-        left, right = got[2 * step], got[2 * step + 1]
-        both = jnp.concatenate([left, right], axis=1)
-        pieces = both[F : F + 16].astype(jnp.float32)
-        pos = pieces[0:3] + pieces[3:6] + pieces[6:9]
-        at = pl.ds(pl.multiple_of(step * 2 * ATOM, 2 * ATOM), 2 * ATOM)
-        for k in range(0, KDEV, 32):
-            halves = []
-            for half in range(2):
-                lanes = slice(half * ATOM, (half + 1) * ATOM)
-                turns = (
-                    columns[0, k : k + 32] * pos[0:1, lanes] + columns[1, k : k + 32] * pos[1:2, lanes]
-                ) + columns[2, k : k + 32] * pos[2:3, lanes]
-                halves.append(cosine_and_sine(turns))
-            for i in range(2):
-                table[i * KDEV + k : i * KDEV + k + 32, at] = jnp.concatenate(
-                    [halves[0][i], halves[1][i]], axis=1
-                ).astype(jnp.bfloat16)
-        total[...] += dot(table[:, at], both[:F], ((1,), (1,)))
+        for pair in range(0, GROUP, 2):
+            first = step * GROUP + pair
+            both = jnp.concatenate([got[first], got[first + 1]], axis=1)
+            pieces = both[F : F + 16].astype(jnp.float32)
+            pos = pieces[0:3] + pieces[3:6] + pieces[6:9]
+            projected = dot(weight[...], both[:F], ((0,), (0,))).astype(jnp.bfloat16)
+            at = pl.ds(pl.multiple_of(first * ATOM, 2 * ATOM), 2 * ATOM)
+            for k in range(0, KDEV, 64):
+                tiles = []
+                for part in range(k, k + 64, 16):
+                    halves = []
+                    for half in range(2):
+                        lanes = slice(half * ATOM, (half + 1) * ATOM)
+                        turns = (
+                            columns[0, part : part + 16] * pos[0:1, lanes]
+                            + columns[1, part : part + 16] * pos[1:2, lanes]
+                        ) + columns[2, part : part + 16] * pos[2:3, lanes]
+                        halves.append(cosine_and_sine(turns))
+                    tiles.append(
+                        [jnp.concatenate([halves[0][i], halves[1][i]], axis=1).astype(jnp.bfloat16) for i in range(2)]
+                    )
+                cosines = jnp.concatenate([t[0] for t in tiles], axis=0)
+                sines = jnp.concatenate([t[1] for t in tiles], axis=0)
+                table[k : k + 64, at] = cosines
+                table[KDEV + k : KDEV + k + 64, at] = sines
+                sums = dot(jnp.concatenate([cosines, sines], axis=0), projected, ((1,), (1,)))
+                total[k : k + 64] += sums[:64]
+                total[KDEV + k : KDEV + k + 64] += sums[64:]
+        stored(step).start()
 
     partial[...] = jnp.concatenate([total[:KDEV], total[KDEV:]], axis=1).astype(jnp.bfloat16)
-
-
-def sum_kernel(arrived, out):
+    for step in range(PLANE // GROUP):
+        stored(step).wait()
+
+
+def sum_kernel(arrived, scalar, out):
     total = arrived[0].astype(jnp.float32)
     for i in range(1, DEPTH):
         total = total + arrived[i].astype(jnp.float32)
@@ -142,18 +165,24 @@
         out[i] = total
 
 
-def project_kernel(half_at, got, kfilter, table, out):
+def project_kernel(got, own_filter, table_at, out, table, done):
+    width = 8 * ATOM
+    loads = [
+        pltpu.make_async_copy(
+            table_at.at[:, i * width : (i + 1) * width], table.at[:, i * width : (i + 1) * width], done.at[i]
+        )
+        for i in range(PLANE // 8)
+    ]
+    for load in loads:
+        load.start()
     total = got[...].astype(jnp.float32).T
-    own = kfilter[:, pl.ds(pl.multiple_of(half_at[0], KDEV), KDEV)]
-    filtered = jnp.concatenate([own * total[:F] * norm_scale, own * total[F:] * norm_scale], axis=1)
-    filtered = filtered.astype(jnp.bfloat16)
-
-    @pl.loop(0, PLANE // 2)
-    def _(step):
-        at = pl.ds(pl.multiple_of(step * 2 * ATOM, 2 * ATOM), 2 * ATOM)
-        message = dot(filtered, table[:, at], ((1,), (0,))).astype(jnp.bfloat16)
-        out[2 * step] = message[:, :ATOM]
-        out[2 * step + 1] = message[:, ATOM:]
+    own = own_filter[...]
+    filtered = jnp.concatenate([own * total[:F], own * total[F:]], axis=1).astype(jnp.bfloat16)
+    for i, load in enumerate(loads):
+        load.wait()
+        message = dot(filtered, table[:, i * width : (i + 1) * width], ((1,), (0,))).astype(jnp.bfloat16)
+        for p in range(8):
+            out[8 * i + p] = message[:, p * ATOM : (p + 1) * ATOM]
 
 
 def finish_kernel(arrived, scalar, out):
@@ -232,43 +261,53 @@
 ):
     bf16, f32 = jnp.bfloat16, jnp.float32
     shape = jax.ShapeDtypeStruct
-    half_at = (lax.axis_index("yh") * KDEV).astype(jnp.int32).reshape(1)
-    k_at = (lax.axis_index(kb_axes) * 2 * KDEV + half_at).astype(jnp.int32).reshape(1)
-    packed = call(pack_kernel, shape((PLANE, PACK, ATOM), bf16), count=3)(features, positions, ewald_weight)
-    got = exchanged(packed, plane_axes)
-    up, down = call(halo_kernel, (shape((HALO_ROWS, ATOM), bf16),) * 2, count=4)(
-        features, vectors, positions, halo_lists
+    half_at = lax.axis_index("yh") * KDEV
+    places = jnp.stack([lax.axis_index(kb_axes) * 2 * KDEV + half_at, half_at]).astype(jnp.int32)
+    got = exchanged(packed_for_all(features, positions, PLANE), plane_axes)
+    halo = shape((HALO_ROWS, ATOM), bf16)
+    up, down, columns, own_filter = call(
+        prepare_kernel,
+        [SM] + [VM] * 6,
+        (halo, halo, shape((3, KDEV, ATOM), f32), shape((F, KDEV), f32)),
+        places, features, vectors, positions, halo_lists, lattice, kspace_filter,
     )
     below, above = shifted(up, 1), shifted(down, -1)
     table, partial = call(
         table_kernel,
+        [VM, VM, VM, ANY, ANY, ANY],
         (shape((2 * KDEV, PLANE * ATOM), bf16), shape((KDEV, 2 * F), bf16)),
-        scratch=[pltpu.VMEM((3, KDEV, ATOM), f32), pltpu.VMEM((2 * KDEV, F), f32)],
-        smem=1,
-        count=2,
-    )(k_at, got, lattice)
+        got, columns, ewald_weight, below, above, own_filter,
+        scratch=[
+            VM((2 * KDEV, PLANE * ATOM), bf16),
+            VM((2 * KDEV, F), f32),
+            pltpu.SemaphoreType.DMA((PLANE // GROUP,)),
+        ],
+        out_places=[FAR, VM],
+        limit=TABLE_LIMIT,
+    )
     arrived = exchanged(partial.reshape(DEPTH, KDEV // DEPTH, 2 * F), "z")
     scalar, new_vectors = call(
         short_kernel,
+        [VM] * 10,
         (shape((F, ATOM), f32), shape((3, F, ATOM), bf16)),
-        scratch=[
-            pltpu.VMEM((EXT_ROWS, 3 * ATOM), bf16),
-            pltpu.VMEM((3 * ATOM, NBR * ATOM), bf16),
-            pltpu.VMEM((192, NBR * ATOM), f32),
-            pltpu.VMEM((8, NBR * ATOM), f32),
-        ],
-        count=10,
-    )(
         features, vectors, positions, neighbours, below, above,
         node_weight, node_bias[:, None], message_weight, radial_weight,
-    )
-    owned = call(sum_kernel, shape((DEPTH, KDEV // DEPTH, 2 * F), bf16), count=1)(arrived)
+        scratch=[
+            VM((EXT_ROWS, 3 * ATOM), bf16),
+            VM((3 * ATOM, NBR * ATOM), bf16),
+            VM((192, NBR * ATOM), f32),
+            VM((8, NBR * ATOM), f32),
+        ],
+    )
+    owned = call(sum_kernel, [VM, ANY], shape((DEPTH, KDEV // DEPTH, 2 * F), bf16), arrived, scalar)
     totals = exchanged(owned, "z").reshape(KDEV, 2 * F)
-    messages = call(project_kernel, shape((PLANE, F, ATOM), bf16), smem=1, count=3)(
-        half_at, totals, kspace_filter, table
+    messages = call(
+        project_kernel, [VM, VM, FAR], shape((PLANE, F, ATOM), bf16), totals, own_filter, table,
+        scratch=[VM((2 * KDEV, PLANE * ATOM), bf16), pltpu.SemaphoreType.DMA((PLANE // 8,))],
+        limit=TABLE_LIMIT,
     )
     returned = exchanged(messages, plane_axes)
-    new_features = call(finish_kernel, shape((F, ATOM), bf16), count=2)(returned, scalar)
+    new_features = call(finish_kernel, [VM] * 2, shape((F, ATOM), bf16), returned, scalar)
     return new_features, new_vectors
 
 

time: 101 us -> 107 us (1.059)
  waiting for transfers between devices: 16.9 us -> 5.56 us
  local copies, waits for them, and re-layouts: 4.06 us -> 13 us
  starting transfers between devices: 22.4 us -> 29.3 us
  blocking collectives: 39.5 us -> 41.8 us
    all_to_all x2, waiting for transfers between devices: 13 us -> 1.83 us  [exchanged(): return lax.all_to_all(x, axes, split_axis=0, concat_axis=0, tiled=True)]
    all_to_all x2, starting transfers between devices: 16.9 us -> 23.8 us  [exchanged(): return lax.all_to_all(x, axes, split_axis=0, concat_axis=0, tiled=True)]
    unnamed x28, local copies, waits for them, and re-layouts: 3.97 us -> 10.5 us
    all_to_all x2, blocking collectives: 39.5 us -> 41.8 us  [exchanged(): return lax.all_to_all(x, axes, split_axis=0, concat_axis=0, tiled=True)]
    pallas_call x7 -> x6, Pallas kernels: 15.8 us -> 15 us  [call(): pl.pallas_call(kernel, out_shape=outs, in_specs=[pl.BlockSpec(memory_spac...]
  transfers between devices with their start and end apart: 4 -> 4, of which waited for: 3 -> 2; matrix products, arithmetic and copies ran while one was open for 0% -> 1% of each run, Pallas kernels for 4% -> 5%
where the time goes in v2:
time: 107 us; the launch traced here: 106 us
  blocking collectives  41.8 us (39%)
  starting transfers between devices  29.3 us (27%)
  Pallas kernels  15 us (14%)
  local copies, waits for them, and re-layouts  13 us (12%)
  waiting for transfers between devices  5.56 us (5%)
    all_to_all x2, blocking collectives, exchanged(): return lax.all_to_all(x, axes, split_axis=0, concat_axis=0, tiled=True)  41.8 us
    all_to_all x2, starting transfers between devices, exchanged(): return lax.all_to_all(x, axes, split_axis=0, concat_axis=0, tiled=True)  23.8 us
    pallas_call x6, Pallas kernels, call(): pl.pallas_call(kernel, out_shape=outs, in_specs=[pl.BlockSpec(memory_spac...  15 us
    unnamed x28, local copies, waits for them, and re-layouts  10.5 us
    ppermute x2, starting transfers between devices, shifted(): lax.ppermute(x, all_axes, [(i, (i + steps) % SLABS) for i in range(SLABS)])  5.47 us
    ppermute x2, waiting for transfers between devices, shifted(): lax.ppermute(x, all_axes, [(i, (i + steps) % SLABS) for i in range(SLABS)])  3.74 us
  transfers between devices with their start and end apart: 4, of which 2 were waited for; matrix products, arithmetic and copies ran while one was open for 1% of the time, Pallas kernels for 5%

profile of v2, /device:TPU:1, one launch (start us, length us, event | category | flops | bytes accessed | tf_op | source)
XLA Modules:
  0.0 106.1 jit_solution(9498765725029518122)
XLA Ops:
  0.6 0.7 fusion
  1.3 0.8 concatenate.3
  2.2 1.0 broadcast_in_dim.10
  3.1 10.4 %all-to-all-start = ((bf16[32,80,128]{2,1,0:T(8,128)(2,1)}), bf16[32,80,128]{2,1,0:T(8,128)(2,1)S(1)}, u32[]{:S(2)}, u32[]{:S(2)}) async-start(bf16[32,80,128]{2,1,0:T(8,128)(2,1)} %broadcast_in_dim.10), calls=%async_computation | async-start | bytes 1310720 | tf_op jit(solution)/shard_map/all_to_all | solution.py:251
  13.6 0.1 pad_add_fusion.places
  13.7 0.8 copy-done
  14.5 0.7 copy-done.2
  15.2 0.9 copy-done.4
  16.1 0.9 copy-done.5
  17.0 0.7 copy-done.7
  17.7 0.7 copy-done.13
  18.3 0.9 shard_map.131
  19.2 3.5 %collective-permute-start = (bf16[288,128]{1,0:T(8,128)(2,1)S(1)}, bf16[288,128]{1,0:T(8,128)(2,1)S(1)}, u32[]{:S(2)}, u32[]{:S(2)}) collective-permute-start(bf16[288,128]{1,0:T(8,128)(2,1)S(1)} %get-tuple-element.11), channel_id=1, source_target_pairs={{0,1},{1,2},{2,3},{3,4},{4,5},{5,6},{6,7},{7,8},{8,9},{9,10},{10,1... | collective-permute-start | bytes 221192 | tf_op jit(solution)/shard_map/ppermute | solution.py:255
  22.8 1.9 %collective-permute-start.1 = (bf16[288,128]{1,0:T(8,128)(2,1)S(1)}, bf16[288,128]{1,0:T(8,128)(2,1)S(1)}, u32[]{:S(2)}, u32[]{:S(2)}) collective-permute-start(bf16[288,128]{1,0:T(8,128)(2,1)S(1)} %get-tuple-element.12), channel_id=1, source_target_pairs={{0,511},{1,0},{2,1},{3,2},{4,3},{5,4},{6,5},{7,6},{8,7},{9,8},{10,... | collective-permute-start | bytes 221192 | tf_op jit(solution)/shard_map/ppermute | solution.py:255
  24.7 3.7 %collective-permute-done.1.above = bf16[288,128]{1,0:T(8,128)(2,1)S(1)} collective-permute-done((bf16[288,128]{1,0:T(8,128)(2,1)S(1)}, bf16[288,128]{1,0:T(8,128)(2,1)S(1)}, u32[]{:S(2)}, u32[]{:S(2)}) %collective-permute-start.1) | collective-permute-done | bytes 73760 | tf_op jit(solution)/shard_map/ppermute | solution.py:255
  28.5 0.7 copy-done.9
  29.2 6.9 %shard_map.132 = (bf16[512,4096]{1,0:T(8,128)(2,1)}, bf16[256,128]{1,0:T(8,128)(2,1)}) custom-call(bf16[32,80,128]{2,1,0:T(8,128)(2,1)S(1)} %all-to-all-done.got, f32[3,256,128]{2,1,0:T(8,128)S(1)} %get-tuple-element.10.columns, bf16[64,64]{1,0:T(8,128)(2,1)S(1)} %copy-done.9, bf16[288,128]{1,0:T(8,128)(2,1)S(1)} %collective-permute-done.below, ...), custom_call_target="tpu_custom_call" | custom-call | tf_op jit(solution)/shard_map/pallas_call | solution.py:75
  36.1 13.4 %all-to-all-start.1 = ((bf16[16,16,128]{2,1,0:T(8,128)(2,1)}), bf16[16,16,128]{2,1,0:T(8,128)(2,1)S(1)}, u32[]{:S(2)}, u32[]{:S(2)}) async-start(bf16[16,16,128]{2,1,0:T(8,128)(2,1)} %bitcast.2), calls=%async_computation.1 | async-start | bytes 131072 | tf_op jit(solution)/shard_map/all_to_all | solution.py:251
  49.5 0.7 copy.14.bias
  50.3 0.8 copy-done.1
  51.1 0.7 copy-done.3
  51.8 0.8 copy-done.6
  52.5 0.7 copy-done.8
  53.2 0.7 copy-done.10
  53.9 0.7 copy-done.11
  54.6 0.7 copy-done.12
  55.3 3.9 %shard_map.133 = (f32[64,128]{1,0:T(8,128)S(1)}, bf16[3,64,128]{2,1,0:T(8,128)(2,1)}) custom-call(bf16[64,128]{1,0:T(8,128)(2,1)S(1)} %copy-done.3, bf16[3,64,128]{2,1,0:T(8,128)(2,1)S(1)} %copy-done.1, f32[3,128]{1,0:T(4,128)S(1)} %copy-done.8, s32[16,128]{1,0:T(8,128)S(1)} %copy-done.12, bf16[288,128]{1,0:T(8,128)(2,1)S(1)} %collective-permute-done.below, ...), custom_call_target="tpu_custom_call" | custom-call | tf_op jit(solution)/shard_map/pallas_call | solution.py:75
  59.2 1.8 %all-to-all-done.1.arrived = bf16[16,16,128]{2,1,0:T(8,128)(2,1)S(1)} async-done(((bf16[16,16,128]{2,1,0:T(8,128)(2,1)}), bf16[16,16,128]{2,1,0:T(8,128)(2,1)S(1)}, u32[]{:S(2)}, u32[]{:S(2)}) %all-to-all-start.1) | async-done | bytes 65568 | tf_op jit(solution)/shard_map/all_to_all | solution.py:251
  61.1 21.0 %all_to_all.20 = bf16[16,16,128]{2,1,0:T(8,128)(2,1)S(1)} all-to-all(bf16[16,16,128]{2,1,0:T(8,128)(2,1)S(1)} %shard_map.134), channel_id=1, replica_groups=mesh['yh'=2,'z'=16,'yl'=2,'x'=4,'c'=2] {'z'}, dimensions={0} | all-to-all | bytes 131072 | tf_op jit(solution)/shard_map/all_to_all | solution.py:251
  82.1 2.5 %shard_map.135 = bf16[32,64,128]{2,1,0:T(8,128)(2,1)S(1)} custom-call(bf16[256,128]{1,0:T(8,128)(2,1)S(1)} %bitcast.5, f32[64,256]{1,0:T(8,128)S(1)} %get-tuple-element.13.own_filter, bf16[512,4096]{1,0:T(8,128)(2,1)} %get-tuple-element.16.table_at), custom_call_target="tpu_custom_call" | custom-call | tf_op jit(solution)/shard_map/pallas_call | solution.py:75
  84.6 20.8 %all_to_all.21.arrived = bf16[32,64,128]{2,1,0:T(8,128)(2,1)S(1)} all-to-all(bf16[32,64,128]{2,1,0:T(8,128)(2,1)S(1)} %shard_map.135), channel_id=1, replica_groups=mesh['yh'=2,'z'=16,'yl'=2,'x'=4,'c'=2] {'yh','yl','x','c'}, dimensions={0} | all-to-all | bytes 1048576 | tf_op jit(solution)/shard_map/all_to_all | solution.py:251
  105.5 0.7 shard_map.136
  (18 shorter events, 0.1 us)
Async XLA Ops:
  3.1 25.3 %all-to-all-start = ((bf16[32,80,128]{2,1,0:T(8,128)(2,1)}), bf16[32,80,128]{2,1,0:T(8,128)(2,1)S(1)}, u32[]{:S(2)}, u32[]{:S(2)}) async-start(bf16[32,80,128]{2,1,0:T(8,128)(2,1)} %broadcast_in_dim.10), calls=%async_computation | async-start | bytes 1310720 | tf_op jit(solution)/shard_map/all_to_all | solution.py:251
  13.6 0.8 copy-start
  14.4 0.7 copy-start.2
  15.2 0.9 copy-start.4
  16.1 0.9 copy-start.5
  17.0 0.7 copy-start.7
  17.7 0.7 copy-start.13
  19.2 5.5 %collective-permute-start = (bf16[288,128]{1,0:T(8,128)(2,1)S(1)}, bf16[288,128]{1,0:T(8,128)(2,1)S(1)}, u32[]{:S(2)}, u32[]{:S(2)}) collective-permute-start(bf16[288,128]{1,0:T(8,128)(2,1)S(1)} %get-tuple-element.11), channel_id=1, source_target_pairs={{0,1},{1,2},{2,3},{3,4},{4,5},{5,6},{6,7},{7,8},{8,9},{9,10},{10,1... | collective-permute-start | bytes 221192 | tf_op jit(solution)/shard_map/ppermute | solution.py:255
  22.8 5.7 %collective-permute-start.1 = (bf16[288,128]{1,0:T(8,128)(2,1)S(1)}, bf16[288,128]{1,0:T(8,128)(2,1)S(1)}, u32[]{:S(2)}, u32[]{:S(2)}) collective-permute-start(bf16[288,128]{1,0:T(8,128)(2,1)S(1)} %get-tuple-element.12), channel_id=1, source_target_pairs={{0,511},{1,0},{2,1},{3,2},{4,3},{5,4},{6,5},{7,6},{8,7},{9,8},{10,... | collective-permute-start | bytes 221192 | tf_op jit(solution)/shard_map/ppermute | solution.py:255
  28.5 0.7 copy-start.9
  36.1 25.0 %all-to-all-start.1 = ((bf16[16,16,128]{2,1,0:T(8,128)(2,1)}), bf16[16,16,128]{2,1,0:T(8,128)(2,1)S(1)}, u32[]{:S(2)}, u32[]{:S(2)}) async-start(bf16[16,16,128]{2,1,0:T(8,128)(2,1)} %bitcast.2), calls=%async_computation.1 | async-start | bytes 131072 | tf_op jit(solution)/shard_map/all_to_all | solution.py:251
  50.2 0.8 copy-start.1
  51.0 0.7 copy-start.3
  51.8 0.8 copy-start.6
  52.5 0.7 copy-start.8
  53.2 0.7 copy-start.10
  53.9 0.7 copy-start.11
  54.6 0.7 copy-start.12

commit v3 on v2

v3 whole, which is shorter than its diff:
```python
import math

import jax
import jax.numpy as jnp
from jax import lax
from jax.experimental import pallas as pl
from jax.experimental.pallas import tpu as pltpu
from jax.sharding import Mesh
from jax.sharding import PartitionSpec as P

F = 64
NRBF = 20
NBR = 16
ATOM = 128
KDEV = 256
PLANE = 32
DEPTH = 16
SLABS = 512
KVEC = 8192
ATOMS = 65536
PACK = 80
HALO_ROWS = 272
GROUP = 8

plane_axes = ("yh", "yl", "x", "c")
kb_axes = ("yl", "x", "c")
all_axes = ("yh", "z", "yl", "x", "c")

side_length = 6.0
slab_depth = 6.0
radial_reach = 6.0
distance_floor = 1.0
norm_scale = 1.0 / math.sqrt(KVEC * ATOMS)

sine_terms = (4.44287959, -7.30781805, 3.59778873, -0.79123821)
cosine_terms = (1.41420408, -6.97764206, 5.71523839, -1.72834865)
whole_turns = 1.5 * 2.0**23

VMEM_LIMIT = 16 * 2**20


def dot(a, b, dims):
    return lax.dot_general(a, b, (dims, ((), ())), preferred_element_type=jnp.float32)


def polynomial(terms, u):
    value = terms[-1] * u + terms[-2]
    for term in terms[-3::-1]:
        value = value * u + term
    return value


def cosine_and_sine(turns):
    r = turns - ((turns + whole_turns) - whole_turns)
    u = r * r
    s = r * polynomial(sine_terms, u)
    c = polynomial(cosine_terms, u)
    return 1.0 - s * s, s * c


VM, SM, ANY = pltpu.VMEM, pltpu.SMEM, pl.ANY


def call(kernel, places, outs, *operands, scratch=()):
    return pl.pallas_call(
        kernel,
        out_shape=outs,
        in_specs=[pl.BlockSpec(memory_space=place) for place in places],
        out_specs=jax.tree.map(lambda _: pl.BlockSpec(memory_space=VM), outs),
        scratch_shapes=list(scratch),
        compiler_params=pltpu.CompilerParams(vmem_limit_bytes=VMEM_LIMIT),
        cost_estimate=pl.CostEstimate(flops=0, bytes_accessed=0, transcendentals=0),
    )(*operands)


def packed_rows(feat, pos):
    first = lax.reduce_precision(pos, 8, 7)
    second = lax.reduce_precision(pos - first, 8, 7)
    third = (pos - first) - second
    rows = jnp.pad(feat, ((0, PACK - F), (0, 0)))
    for i, piece in enumerate((first, second, third)):
        at = F + 3 * i
        rows = rows + jnp.pad(piece.astype(jnp.bfloat16), ((at, PACK - at - 3), (0, 0)))
    return rows


def summed(pieces):
    return pieces[0:3] + pieces[3:6] + pieces[6:9]


def halo_kernel(packed, vec, halo, up, down):
    rows = jnp.concatenate([packed[...], vec[0], vec[1], vec[2]], axis=0)
    atom = lax.broadcasted_iota(jnp.int32, (ATOM, ATOM), 0)
    for side, out in ((0, up), (1, down)):
        chosen = jnp.where(atom == halo[side : side + 1, :], 1.0, 0.0).astype(jnp.bfloat16)
        out[...] = dot(rows, chosen, ((1,), (0,))).astype(jnp.bfloat16)


def prepare_kernel(places, lattice, kfilter, weight, columns, own_filter, own_weight):
    own_weight[...] = weight[...]
    own = lattice[:, pl.ds(pl.multiple_of(places[0], KDEV), KDEV)].astype(jnp.float32)
    turned = jnp.concatenate([own, jnp.zeros((5, KDEV), jnp.float32)], axis=0).T
    for i in range(3):
        columns[i] = jnp.broadcast_to(turned[:, i : i + 1], (KDEV, ATOM))
    own_filter[...] = kfilter[:, pl.ds(pl.multiple_of(places[1], KDEV), KDEV)] * norm_scale


def table_kernel(got, columns, below, above, own_filter, table, partial, total):
    total[...] = jnp.zeros_like(total)

    @pl.loop(0, PLANE // GROUP)
    def _(step):
        for pair in range(0, GROUP, 2):
            first = step * GROUP + pair
            both = jnp.concatenate([got[first], got[first + 1]], axis=1)
            pos = summed(both[F:].astype(jnp.float32))
            at = pl.ds(pl.multiple_of(first * ATOM, 2 * ATOM), 2 * ATOM)
            for k in range(0, KDEV, 64):
                rows = slice(k, k + 64)
                halves = []
                for lanes in (slice(0, ATOM), slice(ATOM, 2 * ATOM)):
                    halves.append(
                        (columns[0, rows] * pos[0:1, lanes] + columns[1, rows] * pos[1:2, lanes])
                        + columns[2, rows] * pos[2:3, lanes]
                    )
                cosines, sines = cosine_and_sine(jnp.concatenate(halves, axis=1))
                cosines, sines = cosines.astype(jnp.bfloat16), sines.astype(jnp.bfloat16)
                table[k : k + 64, at] = cosines
                table[KDEV + k : KDEV + k + 64, at] = sines
                sums = dot(jnp.concatenate([cosines, sines], axis=0), both[:F], ((1,), (1,)))
                total[k : k + 64] += sums[:64]
                total[KDEV + k : KDEV + k + 64] += sums[64:]

    partial[...] = jnp.concatenate([total[:KDEV], total[KDEV:]], axis=1).astype(jnp.bfloat16)


def sum_kernel(arrived, out):
    total = arrived[0].astype(jnp.float32)
    for i in range(1, DEPTH):
        total = total + arrived[i].astype(jnp.float32)
    total = total.astype(jnp.bfloat16)
    for i in range(DEPTH):
        out[i] = total


def project_kernel(got, own_filter, weight, table, out):
    own = own_filter[...]
    total = [dot(weight[...], got[:, part * F : (part + 1) * F], ((0,), (1,))) for part in range(2)]
    filtered = jnp.concatenate([own * total[0], own * total[1]], axis=1).astype(jnp.bfloat16)
    for first in range(0, PLANE, 8):
        message = dot(filtered, table[:, first * ATOM : (first + 8) * ATOM], ((1,), (0,))).astype(jnp.bfloat16)
        for p in range(8):
            out[first + p] = message[:, p * ATOM : (p + 1) * ATOM]


def finish_kernel(arrived, scalar, out):
    total = arrived[0].astype(jnp.float32)
    for i in range(1, PLANE):
        total = total + arrived[i].astype(jnp.float32)
    out[...] = (scalar[...] + total).astype(jnp.bfloat16)


def short_kernel(
    packed, vec, ids, below, above, node_weight, bias, message_weight, radial_weight, messages,
    scalar_out, vector_out, ext, chosen, filters, directions,
):
    pos = summed(packed[F:].astype(jnp.float32))
    ext[192:384, :ATOM] = jnp.concatenate([vec[0], vec[1], vec[2]], axis=0)
    ext[384:, :ATOM] = packed[F:]
    for side, at in ((below, ATOM), (above, 2 * ATOM)):
        ext[192:384, at : at + ATOM] = side[PACK:]
        ext[384:, at : at + ATOM] = side[F:PACK]
    ext_feat = jnp.concatenate([packed[:F], below[:F], above[:F]], axis=1)
    bias_column = jnp.broadcast_to(bias[...], (8, F)).T[:, 0:1]
    hidden = dot(node_weight[...], ext_feat, ((0,), (0,))) + bias_column
    hidden = (hidden / (1.0 + jnp.exp(-hidden))).astype(jnp.bfloat16)
    ext[:192] = dot(message_weight[...], hidden, ((0,), (0,))).astype(jnp.bfloat16)

    number = lax.broadcasted_iota(jnp.int32, (3 * ATOM, ATOM), 0)
    for j in range(NBR):
        chosen[:, j * ATOM : (j + 1) * ATOM] = jnp.where(number == ids[j : j + 1, :], 1.0, 0.0).astype(jnp.bfloat16)
    found = dot(ext[384:], chosen[...], ((1,), (0,)))
    offset = summed(found) - jnp.concatenate([pos] * NBR, axis=1)
    offset = offset - jnp.floor(offset + 0.5)
    side = lax.broadcasted_iota(jnp.int32, (3, 1), 0)
    box = jnp.where(side == 2, slab_depth * SLABS, side_length).astype(jnp.float32)
    cartesian = offset * box
    square = cartesian * cartesian
    distance = jnp.sqrt(square[0:1] + square[1:2] + square[2:3])
    directions[0:3] = cartesian / jnp.maximum(distance, distance_floor)
    center = lax.broadcasted_iota(jnp.int32, (NRBF, 1), 0).astype(jnp.float32) * (radial_reach / (NRBF - 1))
    away = (distance - center) / (1.5 * radial_reach / NRBF)
    radial = jnp.exp(-(away * away)).astype(jnp.bfloat16)
    filters[...] = dot(radial_weight[...], radial, ((0,), (0,)))

    def slots(step, sums):
        at = pl.ds(pl.multiple_of(step * 2 * ATOM, 2 * ATOM), 2 * ATOM)
        picked = dot(ext[:384], chosen[:, at], ((1,), (0,)))
        terms = picked[:192] * filters[:, at]
        toward = directions[:, at]
        parts = [terms[:F]]
        for x in range(3):
            parts.append(
                picked[192 + x * F : 192 + (x + 1) * F] * terms[F : 2 * F] + terms[2 * F :] * toward[x : x + 1]
            )
        return tuple(s + p[:, :ATOM] + p[:, ATOM:] for s, p in zip(sums, parts))

    zero = jnp.zeros((F, ATOM), jnp.float32)
    sums = lax.fori_loop(0, NBR // 2, slots, (zero,) * 4)
    scalar_out[...] = packed[:F].astype(jnp.float32) + sums[0]
    for x in range(3):
        vector_out[x] = (vec[x].astype(jnp.float32) + sums[1 + x]).astype(jnp.bfloat16)


def exchanged(x, axes):
    return lax.all_to_all(x, axes, split_axis=0, concat_axis=0, tiled=True)


def shifted(x, steps):
    return lax.ppermute(x, all_axes, [(i, (i + steps) % SLABS) for i in range(SLABS)])


def shards(
    features, vectors, positions, neighbours, halo_lists, lattice, kspace_filter,
    node_weight, node_bias, message_weight, radial_weight, ewald_weight,
):
    bf16, f32 = jnp.bfloat16, jnp.float32
    shape = jax.ShapeDtypeStruct
    half_at = lax.axis_index("yh") * KDEV
    places = jnp.stack([lax.axis_index(kb_axes) * 2 * KDEV + half_at, half_at]).astype(jnp.int32)
    packed = packed_rows(features, positions)
    got = exchanged(jnp.broadcast_to(packed, (PLANE, PACK, ATOM)), plane_axes)
    halo = shape((HALO_ROWS, ATOM), bf16)
    up, down = call(halo_kernel, [VM] * 3, (halo, halo), packed, vectors, halo_lists)
    below, above = shifted(up, 1), shifted(down, -1)
    columns, own_filter, own_weight = call(
        prepare_kernel,
        [SM, VM, VM, VM],
        (shape((3, KDEV, ATOM), f32), shape((F, KDEV), f32), shape((F, F), bf16)),
        places, lattice, kspace_filter, ewald_weight,
    )
    table, partial = call(
        table_kernel,
        [VM, VM, ANY, ANY, ANY],
        (shape((2 * KDEV, PLANE * ATOM), bf16), shape((KDEV, 2 * F), bf16)),
        got, columns, below, above, own_filter,
        scratch=[VM((2 * KDEV, F), f32)],
    )
    arrived = exchanged(partial.reshape(DEPTH, KDEV // DEPTH, 2 * F), "z")
    owned = call(sum_kernel, [VM], shape((DEPTH, KDEV // DEPTH, 2 * F), bf16), arrived)
    totals = exchanged(owned, "z").reshape(KDEV, 2 * F)
    messages = call(
        project_kernel, [VM] * 4, shape((PLANE, F, ATOM), bf16), totals, own_filter, own_weight, table
    )
    returned = exchanged(messages, plane_axes)
    scalar, new_vectors = call(
        short_kernel,
        [VM] * 9 + [ANY],
        (shape((F, ATOM), f32), shape((3, F, ATOM), bf16)),
        packed, vectors, neighbours, below, above,
        node_weight, node_bias.reshape(1, F), message_weight, radial_weight, messages,
        scratch=[
            VM((400, 3 * ATOM), bf16),
            VM((3 * ATOM, NBR * ATOM), bf16),
            VM((192, NBR * ATOM), f32),
            VM((8, NBR * ATOM), f32),
        ],
    )
    new_features = call(finish_kernel, [VM] * 2, shape((F, ATOM), bf16), returned, scalar)
    return new_features, new_vectors


def solution(mesh):
    fine = Mesh(mesh.devices.reshape(2, 16, 2, 4, 2), all_axes)
    atoms = P(None, all_axes)
    placed = (
        atoms, P(None, None, all_axes), atoms, atoms, atoms, P(), P(None, kb_axes),
        P(), P(), P(), P(), P(),
    )
    return jax.shard_map(
        shards,
        mesh=fine,
        in_specs=placed,
        out_specs=(atoms, P(None, None, all_axes)),
        check_vma=False,
    )
```

time: 107 us -> 94.4 us (0.88)
  local copies, waits for them, and re-layouts: 13 us -> 4.97 us
  waiting for transfers between devices: 5.56 us -> 9.89 us
  starting transfers between devices: 29.3 us -> 25.1 us
  Pallas kernels: 15 us -> 12 us
  blocking collectives: 41.8 us -> 39.4 us
    all_to_all x2, waiting for transfers between devices: 1.83 us -> 9.4 us  [exchanged(): return lax.all_to_all(x, axes, split_axis=0, concat_axis=0, tiled=True)]
    unnamed x28 -> x22, local copies, waits for them, and re-layouts: 10.5 us -> 4.02 us
    all_to_all x2, starting transfers between devices: 23.8 us -> 19.7 us  [exchanged(): return lax.all_to_all(x, axes, split_axis=0, concat_axis=0, tiled=True)]
    ppermute x2, waiting for transfers between devices: 3.74 us -> 0.49 us  [shifted(): lax.ppermute(x, all_axes, [(i, (i + steps) % SLABS) for i in range(SLABS)])]
    pallas_call x6 -> x7, Pallas kernels: 15 us -> 12 us  [call(): pl.pallas_call(kernel, out_shape=outs, in_specs=[pl.BlockSpec(memory_spac...]
    all_to_all x2, blocking collectives: 41.8 us -> 39.4 us  [exchanged(): return lax.all_to_all(x, axes, split_axis=0, concat_axis=0, tiled=True)]
  transfers between devices with their start and end apart: 4 -> 4, of which waited for: 2 -> 3; matrix products, arithmetic and copies ran while one was open for 1% -> 0% of each run, Pallas kernels for 5% -> 5%
where the time goes in v3:
time: 94.4 us; the launch traced here: 93.7 us
  blocking collectives  39.4 us (42%)
  starting transfers between devices  25.1 us (27%)
  Pallas kernels  12 us (13%)
  waiting for transfers between devices  9.89 us (10%)
  local copies, waits for them, and re-layouts  4.97 us (5%)
  other arithmetic  1.49 us (2%)
    all_to_all x2, blocking collectives, exchanged(): return lax.all_to_all(x, axes, split_axis=0, concat_axis=0, tiled=True)  39.4 us
    all_to_all x2, starting transfers between devices, exchanged(): return lax.all_to_all(x, axes, split_axis=0, concat_axis=0, tiled=True)  19.7 us
    pallas_call x7, Pallas kernels, call(): pl.pallas_call(kernel, out_shape=outs, in_specs=[pl.BlockSpec(memory_spac...  12 us
    all_to_all x2, waiting for transfers between devices, exchanged(): return lax.all_to_all(x, axes, split_axis=0, concat_axis=0, tiled=True)  9.4 us
    ppermute x2, starting transfers between devices, shifted(): lax.ppermute(x, all_axes, [(i, (i + steps) % SLABS) for i in range(SLABS)])  5.47 us
    unnamed x22, local copies, waits for them, and re-layouts  4.02 us
  transfers between devices with their start and end apart: 4, of which 3 were waited for; matrix products, arithmetic and copies ran while one was open for 0% of the time, Pallas kernels for 5%

profile of v3, /device:TPU:1, one launch (start us, length us, event | category | flops | bytes accessed | tf_op | source)
XLA Modules:
  0.0 93.7 jit_solution(17750685040636002057)
XLA Ops:
  0.6 0.7 reduce-precision_convert_fusion.1
  1.3 0.7 pad_add_fusion.packed
  2.0 0.9 %broadcast_in_dim.3 = bf16[32,80,128]{2,1,0:T(8,128)(2,1)} broadcast(bf16[80,128]{1,0:T(8,128)(2,1)S(1)} %pad_add_fusion.packed), dimensions={1,2} | broadcast | bytes 675840 | tf_op jit(solution)/shard_map/broadcast_in_dim | solution.py:232
  3.0 10.6 %all-to-all-start = ((bf16[32,80,128]{2,1,0:T(8,128)(2,1)}), bf16[32,80,128]{2,1,0:T(8,128)(2,1)S(1)}, u32[]{:S(2)}, u32[]{:S(2)}) async-start(bf16[32,80,128]{2,1,0:T(8,128)(2,1)} %broadcast_in_dim.3), calls=%async_computation | async-start | bytes 1310720 | tf_op jit(solution)/shard_map/all_to_all | solution.py:216
  13.6 0.0 copy-start
  13.6 0.8 copy-done
  14.4 0.7 copy-done.9
  15.1 0.0 copy-start.10
  15.1 0.2 shard_map.132
  15.3 3.5 %collective-permute-start = (bf16[272,128]{1,0:T(8,128)(2,1)S(1)}, bf16[272,128]{1,0:T(8,128)(2,1)S(1)}, u32[]{:S(2)}, u32[]{:S(2)}) collective-permute-start(bf16[272,128]{1,0:T(8,128)(2,1)S(1)} %get-tuple-element.12), channel_id=1, source_target_pairs={{0,1},{1,2},{2,3},{3,4},{4,5},{5,6},{6,7},{7,8},{8,9},{9,10},{10,1... | collective-permute-start | bytes 208904 | tf_op jit(solution)/shard_map/ppermute | solution.py:220
  18.8 1.9 %collective-permute-start.1 = (bf16[272,128]{1,0:T(8,128)(2,1)S(1)}, bf16[272,128]{1,0:T(8,128)(2,1)S(1)}, u32[]{:S(2)}, u32[]{:S(2)}) collective-permute-start(bf16[272,128]{1,0:T(8,128)(2,1)S(1)} %get-tuple-element.13), channel_id=1, source_target_pairs={{0,511},{1,0},{2,1},{3,2},{4,3},{5,4},{6,5},{7,6},{8,7},{9,8},{10,... | collective-permute-start | bytes 208904 | tf_op jit(solution)/shard_map/ppermute | solution.py:220
  20.8 0.1 pad_add_fusion.1.places
  20.9 0.9 copy-done.2
  21.8 0.9 copy-done.3
  22.7 0.7 copy-done.5
  23.4 0.9 shard_map.131
  24.3 0.0 collective-permute-done.below
  24.3 0.5 collective-permute-done.1.above
  24.8 1.8 %all-to-all-done.got = bf16[32,80,128]{2,1,0:T(8,128)(2,1)S(1)} async-done(((bf16[32,80,128]{2,1,0:T(8,128)(2,1)}), bf16[32,80,128]{2,1,0:T(8,128)(2,1)S(1)}, u32[]{:S(2)}, u32[]{:S(2)}) %all-to-all-start) | async-done | bytes 655392 | tf_op jit(solution)/shard_map/all_to_all | solution.py:216
  26.6 4.5 %shard_map.133 = (bf16[512,4096]{1,0:T(8,128)(2,1)S(1)}, bf16[256,128]{1,0:T(8,128)(2,1)S(1)}) custom-call(bf16[32,80,128]{2,1,0:T(8,128)(2,1)S(1)} %all-to-all-done.got, f32[3,256,128]{2,1,0:T(8,128)S(1)} %get-tuple-element.11.columns, bf16[272,128]{1,0:T(8,128)(2,1)S(1)} %collective-permute-done.below, bf16[272,128]{1,0:T(8,128)(2,1)S(1)} %collective-permute-done.1.above, ...), custom_call_target="tpu_custom_call" | custom-call | tf_op jit(solution)/shard_map/pallas_call | solution.py:65
  31.1 25.0 %all_to_all.20.arrived = bf16[16,16,128]{2,1,0:T(8,128)(2,1)S(1)} all-to-all(bf16[16,16,128]{2,1,0:T(8,128)(2,1)S(1)} %bitcast.6), channel_id=1, replica_groups=mesh['yh'=2,'z'=16,'yl'=2,'x'=4,'c'=2] {'z'}, dimensions={0} | all-to-all | bytes 131072 | tf_op jit(solution)/shard_map/all_to_all | solution.py:216
  56.2 14.4 %all_to_all.21 = bf16[16,16,128]{2,1,0:T(8,128)(2,1)S(1)} all-to-all(bf16[16,16,128]{2,1,0:T(8,128)(2,1)S(1)} %shard_map.134), channel_id=1, replica_groups=mesh['yh'=2,'z'=16,'yl'=2,'x'=4,'c'=2] {'z'}, dimensions={0} | all-to-all | bytes 131072 | tf_op jit(solution)/shard_map/all_to_all | solution.py:216
  70.6 1.8 %shard_map.135.messages = bf16[32,64,128]{2,1,0:T(8,128)(2,1)} custom-call(bf16[256,128]{1,0:T(8,128)(2,1)S(1)} %bitcast.5, f32[64,256]{1,0:T(8,128)S(1)} %get-tuple-element.14.own_filter, bf16[64,64]{1,0:T(8,128)(2,1)S(1)} %get-tuple-element.16.weight, bf16[512,4096]{1,0:T(8,128)(2,1)S(1)} %get-tuple-element.17.table), custom_call_target="tpu_custom_call" | custom-call | tf_op jit(solution)/shard_map/pallas_call | solution.py:65
  72.4 9.1 %all-to-all-start.3 = ((bf16[32,64,128]{2,1,0:T(8,128)(2,1)}), bf16[32,64,128]{2,1,0:T(8,128)(2,1)S(1)}, u32[]{:S(2)}, u32[]{:S(2)}) async-start(bf16[32,64,128]{2,1,0:T(8,128)(2,1)} %shard_map.135.messages), calls=%async_computation.3 | async-start | bytes 1048576 | tf_op jit(solution)/shard_map/all_to_all | solution.py:216
  81.5 0.0 copy-done.8
  81.5 0.0 copy-done.1
  81.5 0.0 copy-done.4
  81.5 0.0 copy-done.6
  81.5 0.0 copy-done.7
  81.5 3.9 %shard_map.136 = (f32[64,128]{1,0:T(8,128)S(1)}, bf16[3,64,128]{2,1,0:T(8,128)(2,1)}) custom-call(bf16[80,128]{1,0:T(8,128)(2,1)S(1)} %pad_add_fusion.packed, bf16[3,64,128]{2,1,0:T(8,128)(2,1)S(1)} %copy-done.1, s32[16,128]{1,0:T(8,128)S(1)} %copy-done.8, bf16[272,128]{1,0:T(8,128)(2,1)S(1)} %collective-permute-done.below, ...), custom_call_target="tpu_custom_call" | custom-call | tf_op jit(solution)/shard_map/pallas_call | solution.py:65
  85.4 7.6 %all-to-all-done.3.arrived = bf16[32,64,128]{2,1,0:T(8,128)(2,1)S(1)} async-done(((bf16[32,64,128]{2,1,0:T(8,128)(2,1)}), bf16[32,64,128]{2,1,0:T(8,128)(2,1)S(1)}, u32[]{:S(2)}, u32[]{:S(2)}) %all-to-all-start.3) | async-done | bytes 524320 | tf_op jit(solution)/shard_map/all_to_all | solution.py:216
  93.0 0.7 shard_map.137
  (11 shorter events, 0.0 us)
Async XLA Ops:
  3.0 78.5 %copy-start.8 = (s32[16,128]{1,0:T(8,128)S(1)}, s32[16,128]{1,0:T(8,128)}, u32[]{:S(2)}) copy-start(s32[16,128]{1,0:T(8,128)} %ids.1) | copy-start | bytes 24580
  3.0 23.6 %all-to-all-start = ((bf16[32,80,128]{2,1,0:T(8,128)(2,1)}), bf16[32,80,128]{2,1,0:T(8,128)(2,1)S(1)}, u32[]{:S(2)}, u32[]{:S(2)}) async-start(bf16[32,80,128]{2,1,0:T(8,128)(2,1)} %broadcast_in_dim.3), calls=%async_computation | async-start | bytes 1310720 | tf_op jit(solution)/shard_map/all_to_all | solution.py:216
  13.6 0.8 copy-start
  14.4 0.7 copy-start.9
  15.0 66.4 %copy-start.1 = (bf16[3,64,128]{2,1,0:T(8,128)(2,1)S(1)}, bf16[3,64,128]{2,1,0:T(8,128)(2,1)}, u32[]{:S(2)}) copy-start(bf16[3,64,128]{2,1,0:T(8,128)(2,1)} %vec.3) | copy-start | bytes 147460
  15.0 66.5 %copy-start.4 = (bf16[64,192]{1,0:T(8,128)(2,1)S(1)}, bf16[64,192]{1,0:T(8,128)(2,1)}, u32[]{:S(2)}) copy-start(bf16[64,192]{1,0:T(8,128)(2,1)} %message_weight.1) | copy-start | bytes 73732
  15.0 66.5 %copy-start.6 = (bf16[64,64]{1,0:T(8,128)(2,1)S(1)}, bf16[64,64]{1,0:T(8,128)(2,1)}, u32[]{:S(2)}) copy-start(bf16[64,64]{1,0:T(8,128)(2,1)} %node_weight.1) | copy-start | bytes 24580
  15.1 66.5 %copy-start.7 = (bf16[20,192]{1,0:T(8,128)(2,1)S(1)}, bf16[20,192]{1,0:T(8,128)(2,1)}, u32[]{:S(2)}) copy-start(bf16[20,192]{1,0:T(8,128)(2,1)} %radial_weight.1) | copy-start | bytes 23044
  15.1 66.5 %copy-start.10 = (f32[64]{0:T(128)S(1)}, f32[64]{0:T(128)}, u32[]{:S(2)}) copy-start(f32[64]{0:T(128)} %param.20) | copy-start | bytes 772
  15.3 9.0 %collective-permute-start = (bf16[272,128]{1,0:T(8,128)(2,1)S(1)}, bf16[272,128]{1,0:T(8,128)(2,1)S(1)}, u32[]{:S(2)}, u32[]{:S(2)}) collective-permute-start(bf16[272,128]{1,0:T(8,128)(2,1)S(1)} %get-tuple-element.12), channel_id=1, source_target_pairs={{0,1},{1,2},{2,3},{3,4},{4,5},{5,6},{6,7},{7,8},{8,9},{9,10},{10,1... | collective-permute-start | bytes 208904 | tf_op jit(solution)/shard_map/ppermute | solution.py:220
  18.8 5.9 %collective-permute-start.1 = (bf16[272,128]{1,0:T(8,128)(2,1)S(1)}, bf16[272,128]{1,0:T(8,128)(2,1)S(1)}, u32[]{:S(2)}, u32[]{:S(2)}) collective-permute-start(bf16[272,128]{1,0:T(8,128)(2,1)S(1)} %get-tuple-element.13), channel_id=1, source_target_pairs={{0,511},{1,0},{2,1},{3,2},{4,3},{5,4},{6,5},{7,6},{8,7},{9,8},{10,... | collective-permute-start | bytes 208904 | tf_op jit(solution)/shard_map/ppermute | solution.py:220
  20.9 0.9 copy-start.2
  21.8 0.9 copy-start.3
  22.7 0.7 copy-start.5
  72.4 20.7 %all-to-all-start.3 = ((bf16[32,64,128]{2,1,0:T(8,128)(2,1)}), bf16[32,64,128]{2,1,0:T(8,128)(2,1)S(1)}, u32[]{:S(2)}, u32[]{:S(2)}) async-start(bf16[32,64,128]{2,1,0:T(8,128)(2,1)} %shard_map.135.messages), calls=%async_computation.3 | async-start | bytes 1048576 | tf_op jit(solution)/shard_map/all_to_all | solution.py:216

commit v4 on v3

--- a/solution.py
+++ b/solution.py
@@ -74,14 +74,11 @@
 
 
 def packed_rows(feat, pos):
-    first = lax.reduce_precision(pos, 8, 7)
-    second = lax.reduce_precision(pos - first, 8, 7)
-    third = (pos - first) - second
-    rows = jnp.pad(feat, ((0, PACK - F), (0, 0)))
-    for i, piece in enumerate((first, second, third)):
-        at = F + 3 * i
-        rows = rows + jnp.pad(piece.astype(jnp.bfloat16), ((at, PACK - at - 3), (0, 0)))
-    return rows
+    placed = [jnp.pad(pos, ((at, PACK - at - 3), (0, 0))) for at in (F, F + 3, F + 6)]
+    firsts = [lax.reduce_precision(value, 8, 7) for value in placed]
+    seconds = [lax.reduce_precision(value - first, 8, 7) for value, first in zip(placed[1:], firsts[1:])]
+    pieces = firsts[0] + seconds[0] + ((placed[2] - firsts[2]) - seconds[1])
+    return jnp.pad(feat, ((0, PACK - F), (0, 0))) + pieces.astype(jnp.bfloat16)
 
 
 def summed(pieces):
@@ -96,16 +93,10 @@
         out[...] = dot(rows, chosen, ((1,), (0,))).astype(jnp.bfloat16)
 
 
-def prepare_kernel(places, lattice, kfilter, weight, columns, own_filter, own_weight):
-    own_weight[...] = weight[...]
-    own = lattice[:, pl.ds(pl.multiple_of(places[0], KDEV), KDEV)].astype(jnp.float32)
-    turned = jnp.concatenate([own, jnp.zeros((5, KDEV), jnp.float32)], axis=0).T
+def table_kernel(got, lattice, below, above, own_filter, table, partial, columns, total):
+    turned = lattice[...].T
     for i in range(3):
         columns[i] = jnp.broadcast_to(turned[:, i : i + 1], (KDEV, ATOM))
-    own_filter[...] = kfilter[:, pl.ds(pl.multiple_of(places[1], KDEV), KDEV)] * norm_scale
-
-
-def table_kernel(got, columns, below, above, own_filter, table, partial, total):
     total[...] = jnp.zeros_like(total)
 
     @pl.loop(0, PLANE // GROUP)
@@ -143,9 +134,9 @@
         out[i] = total
 
 
-def project_kernel(got, own_filter, weight, table, out):
-    own = own_filter[...]
-    total = [dot(weight[...], got[:, part * F : (part + 1) * F], ((0,), (1,))) for part in range(2)]
+def project_kernel(got, own_filter, table, out):
+    own, weight = own_filter[:, :KDEV], own_filter[:, KDEV:].astype(jnp.bfloat16)
+    total = [dot(weight, got[:, part * F : (part + 1) * F], ((0,), (1,))) for part in range(2)]
     filtered = jnp.concatenate([own * total[0], own * total[1]], axis=1).astype(jnp.bfloat16)
     for first in range(0, PLANE, 8):
         message = dot(filtered, table[:, first * ATOM : (first + 8) * ATOM], ((1,), (0,))).astype(jnp.bfloat16)
@@ -227,30 +218,27 @@
     bf16, f32 = jnp.bfloat16, jnp.float32
     shape = jax.ShapeDtypeStruct
     half_at = lax.axis_index("yh") * KDEV
-    places = jnp.stack([lax.axis_index(kb_axes) * 2 * KDEV + half_at, half_at]).astype(jnp.int32)
+    k_at = lax.axis_index(kb_axes) * 2 * KDEV + half_at
     packed = packed_rows(features, positions)
     got = exchanged(jnp.broadcast_to(packed, (PLANE, PACK, ATOM)), plane_axes)
+    own_lattice = jnp.pad(lax.dynamic_slice_in_dim(lattice, k_at, KDEV, 1).astype(f32), ((0, 5), (0, 0)))
+    own_filter = jnp.pad(lax.dynamic_slice_in_dim(kspace_filter, half_at, KDEV, 1) * norm_scale, ((0, 0), (0, F)))
+    own_filter = own_filter + jnp.pad(ewald_weight.astype(f32), ((0, 0), (KDEV, 0)))
     halo = shape((HALO_ROWS, ATOM), bf16)
     up, down = call(halo_kernel, [VM] * 3, (halo, halo), packed, vectors, halo_lists)
     below, above = shifted(up, 1), shifted(down, -1)
-    columns, own_filter, own_weight = call(
-        prepare_kernel,
-        [SM, VM, VM, VM],
-        (shape((3, KDEV, ATOM), f32), shape((F, KDEV), f32), shape((F, F), bf16)),
-        places, lattice, kspace_filter, ewald_weight,
-    )
     table, partial = call(
         table_kernel,
         [VM, VM, ANY, ANY, ANY],
         (shape((2 * KDEV, PLANE * ATOM), bf16), shape((KDEV, 2 * F), bf16)),
-        got, columns, below, above, own_filter,
-        scratch=[VM((2 * KDEV, F), f32)],
+        got, own_lattice, below, above, own_filter,
+        scratch=[VM((3, KDEV, ATOM), f32), VM((2 * KDEV, F), f32)],
     )
     arrived = exchanged(partial.reshape(DEPTH, KDEV // DEPTH, 2 * F), "z")
     owned = call(sum_kernel, [VM], shape((DEPTH, KDEV // DEPTH, 2 * F), bf16), arrived)
     totals = exchanged(owned, "z").reshape(KDEV, 2 * F)
     messages = call(
-        project_kernel, [VM] * 4, shape((PLANE, F, ATOM), bf16), totals, own_filter, own_weight, table
+        project_kernel, [VM] * 3, shape((PLANE, F, ATOM), bf16), totals, own_filter, table
     )
     returned = exchanged(messages, plane_axes)
     scalar, new_vectors = call(

time: 94.4 us -> 92.9 us (0.984)
  local copies, waits for them, and re-layouts: 4.97 us -> 2.44 us
  starting transfers between devices: 25.1 us -> 22.9 us
  other arithmetic: 1.49 us -> 3.07 us
  waiting for transfers between devices: 9.89 us -> 11.1 us
  blocking collectives: 39.4 us -> 40.4 us
    unnamed x22 -> x16, local copies, waits for them, and re-layouts: 4.02 us -> 1.5 us
    all_to_all x2, starting transfers between devices: 19.7 us -> 17.5 us  [exchanged(): return lax.all_to_all(x, axes, split_axis=0, concat_axis=0, tiled=True)]
    ppermute x2, waiting for transfers between devices: 0.49 us -> 1.71 us  [shifted(): lax.ppermute(x, all_axes, [(i, (i + steps) % SLABS) for i in range(SLABS)])]
    all_to_all x2, blocking collectives: 39.4 us -> 40.4 us  [exchanged(): return lax.all_to_all(x, axes, split_axis=0, concat_axis=0, tiled=True)]
    pallas_call x7 -> x6, Pallas kernels: 12 us -> 11.5 us  [call(): pl.pallas_call(kernel, out_shape=outs, in_specs=[pl.BlockSpec(memory_spac...]
  transfers between devices with their start and end apart: 4 -> 4, of which waited for: 3 -> 3; matrix products, arithmetic and copies ran while one was open for 0% -> 2% of each run, Pallas kernels for 5% -> 4%
where the time goes in v4:
time: 92.9 us; the launch traced here: 92.2 us
  blocking collectives  40.4 us (43%)
  starting transfers between devices  22.9 us (25%)
  Pallas kernels  11.5 us (12%)
  waiting for transfers between devices  11.1 us (12%)
  other arithmetic  3.07 us (3%)
  local copies, waits for them, and re-layouts  2.44 us (3%)
    all_to_all x2, blocking collectives, exchanged(): return lax.all_to_all(x, axes, split_axis=0, concat_axis=0, tiled=True)  40.4 us
    all_to_all x2, starting transfers between devices, exchanged(): return lax.all_to_all(x, axes, split_axis=0, concat_axis=0, tiled=True)  17.5 us
    pallas_call x6, Pallas kernels, call(): pl.pallas_call(kernel, out_shape=outs, in_specs=[pl.BlockSpec(memory_spac...  11.5 us
    all_to_all x2, waiting for transfers between devices, exchanged(): return lax.all_to_all(x, axes, split_axis=0, concat_axis=0, tiled=True)  9.42 us
    ppermute x2, starting transfers between devices, shifted(): lax.ppermute(x, all_axes, [(i, (i + steps) % SLABS) for i in range(SLABS)])  5.47 us
  transfers between devices with their start and end apart: 4, of which 3 were waited for; matrix products, arithmetic and copies ran while one was open for 2% of the time, Pallas kernels for 4%

profile of v4, /device:TPU:1, one launch (start us, length us, event | category | flops | bytes accessed | tf_op | source)
XLA Modules:
  0.0 92.2 jit_solution(1489522037885711320)
XLA Ops:
  0.6 0.8 fusion.4.packed
  1.4 0.9 %broadcast_in_dim.3 = bf16[32,80,128]{2,1,0:T(8,128)(2,1)} broadcast(bf16[80,128]{1,0:T(8,128)(2,1)S(1)} %fusion.4.packed), dimensions={1,2} | broadcast | bytes 675840 | tf_op jit(solution)/shard_map/broadcast_in_dim | solution.py:223
  2.4 0.0 copy-start.1
  2.4 0.0 copy-start.5
  2.4 0.0 copy-start.7
  2.4 10.6 %all-to-all-start = ((bf16[32,80,128]{2,1,0:T(8,128)(2,1)}), bf16[32,80,128]{2,1,0:T(8,128)(2,1)S(1)}, u32[]{:S(2)}, u32[]{:S(2)}) async-start(bf16[32,80,128]{2,1,0:T(8,128)(2,1)} %broadcast_in_dim.3), calls=%async_computation | async-start | bytes 1310720 | tf_op jit(solution)/shard_map/all_to_all | solution.py:207
  13.0 0.0 copy-start
  13.0 0.8 copy-done
  13.8 0.7 copy-done.6
  14.5 0.2 shard_map.131
  14.7 3.5 %collective-permute-start = (bf16[272,128]{1,0:T(8,128)(2,1)S(1)}, bf16[272,128]{1,0:T(8,128)(2,1)S(1)}, u32[]{:S(2)}, u32[]{:S(2)}) collective-permute-start(bf16[272,128]{1,0:T(8,128)(2,1)S(1)} %get-tuple-element.8), channel_id=1, source_target_pairs={{0,1},{1,2},{2,3},{3,4},{4,5},{5,6},{6,7},{7,8},{8,9},{9,10},{10,1... | collective-permute-start | bytes 208904 | tf_op jit(solution)/shard_map/ppermute | solution.py:211
  18.2 1.9 %collective-permute-start.1 = (bf16[272,128]{1,0:T(8,128)(2,1)S(1)}, bf16[272,128]{1,0:T(8,128)(2,1)S(1)}, u32[]{:S(2)}, u32[]{:S(2)}) collective-permute-start(bf16[272,128]{1,0:T(8,128)(2,1)S(1)} %get-tuple-element.9), channel_id=1, source_target_pairs={{0,511},{1,0},{2,1},{3,2},{4,3},{5,4},{6,5},{7,6},{8,7},{9,8},{10,... | collective-permute-start | bytes 208904 | tf_op jit(solution)/shard_map/ppermute | solution.py:211
  20.2 0.7 dynamic-slice_convert_fusion
  20.9 0.8 dynamic-slice_multiply_fusion
  21.7 0.7 convert_add_fusion.own_filter
  22.5 0.0 collective-permute-done.below
  22.5 1.7 %collective-permute-done.1.above = bf16[272,128]{1,0:T(8,128)(2,1)S(1)} collective-permute-done((bf16[272,128]{1,0:T(8,128)(2,1)S(1)}, bf16[272,128]{1,0:T(8,128)(2,1)S(1)}, u32[]{:S(2)}, u32[]{:S(2)}) %collective-permute-start.1) | collective-permute-done | bytes 69664 | tf_op jit(solution)/shard_map/ppermute | solution.py:211
  24.2 1.8 %all-to-all-done.got = bf16[32,80,128]{2,1,0:T(8,128)(2,1)S(1)} async-done(((bf16[32,80,128]{2,1,0:T(8,128)(2,1)}), bf16[32,80,128]{2,1,0:T(8,128)(2,1)S(1)}, u32[]{:S(2)}, u32[]{:S(2)}) %all-to-all-start) | async-done | bytes 655392 | tf_op jit(solution)/shard_map/all_to_all | solution.py:207
  26.0 4.8 %shard_map.132 = (bf16[512,4096]{1,0:T(8,128)(2,1)S(1)}, bf16[256,128]{1,0:T(8,128)(2,1)S(1)}) custom-call(bf16[32,80,128]{2,1,0:T(8,128)(2,1)S(1)} %all-to-all-done.got, f32[8,256]{1,0:T(8,128)S(1)} %pad.35.lattice, bf16[272,128]{1,0:T(8,128)(2,1)S(1)} %collective-permute-done.below, bf16[272,128]{1,0:T(8,128)(2,1)S(1)} %collective-permute-done.1.above, ...), custom_call_target="tpu_custom_call" | custom-call | tf_op jit(solution)/shard_map/pallas_call | solution.py:65
  30.8 25.0 %all_to_all.20.arrived = bf16[16,16,128]{2,1,0:T(8,128)(2,1)S(1)} all-to-all(bf16[16,16,128]{2,1,0:T(8,128)(2,1)S(1)} %bitcast.4), channel_id=1, replica_groups=mesh['yh'=2,'z'=16,'yl'=2,'x'=4,'c'=2] {'z'}, dimensions={0} | all-to-all | bytes 131072 | tf_op jit(solution)/shard_map/all_to_all | solution.py:207
  55.9 15.4 %all_to_all.21 = bf16[16,16,128]{2,1,0:T(8,128)(2,1)S(1)} all-to-all(bf16[16,16,128]{2,1,0:T(8,128)(2,1)S(1)} %shard_map.133), channel_id=1, replica_groups=mesh['yh'=2,'z'=16,'yl'=2,'x'=4,'c'=2] {'z'}, dimensions={0} | all-to-all | bytes 131072 | tf_op jit(solution)/shard_map/all_to_all | solution.py:207
  71.3 1.8 %shard_map.134.messages = bf16[32,64,128]{2,1,0:T(8,128)(2,1)} custom-call(bf16[256,128]{1,0:T(8,128)(2,1)S(1)} %bitcast.3, f32[64,320]{1,0:T(8,128)S(1)} %convert_add_fusion.own_filter, bf16[512,4096]{1,0:T(8,128)(2,1)S(1)} %get-tuple-element.11.table), custom_call_target="tpu_custom_call" | custom-call | tf_op jit(solution)/shard_map/pallas_call | solution.py:65
  73.1 6.9 %all-to-all-start.3 = ((bf16[32,64,128]{2,1,0:T(8,128)(2,1)}), bf16[32,64,128]{2,1,0:T(8,128)(2,1)S(1)}, u32[]{:S(2)}, u32[]{:S(2)}) async-start(bf16[32,64,128]{2,1,0:T(8,128)(2,1)} %shard_map.134.messages), calls=%async_computation.3 | async-start | bytes 1048576 | tf_op jit(solution)/shard_map/all_to_all | solution.py:207
  80.0 0.0 copy-done.1
  80.0 0.0 copy-done.2
  80.0 0.0 copy-done.3
  80.0 0.0 copy-done.4
  80.0 0.0 copy-done.5
  80.0 0.0 copy-done.7
  80.0 3.9 %shard_map.135 = (f32[64,128]{1,0:T(8,128)S(1)}, bf16[3,64,128]{2,1,0:T(8,128)(2,1)}) custom-call(bf16[80,128]{1,0:T(8,128)(2,1)S(1)} %fusion.4.packed, bf16[3,64,128]{2,1,0:T(8,128)(2,1)S(1)} %copy-done.1, s32[16,128]{1,0:T(8,128)S(1)} %copy-done.5, bf16[272,128]{1,0:T(8,128)(2,1)S(1)} %collective-permute-done.below, ...), custom_call_target="tpu_custom_call" | custom-call | tf_op jit(solution)/shard_map/pallas_call | solution.py:65
  83.9 7.6 %all-to-all-done.3.arrived = bf16[32,64,128]{2,1,0:T(8,128)(2,1)S(1)} async-done(((bf16[32,64,128]{2,1,0:T(8,128)(2,1)}), bf16[32,64,128]{2,1,0:T(8,128)(2,1)S(1)}, u32[]{:S(2)}, u32[]{:S(2)}) %all-to-all-start.3) | async-done | bytes 524320 | tf_op jit(solution)/shard_map/all_to_all | solution.py:207
  91.5 0.7 shard_map.136
  (6 shorter events, 0.0 us)
Async XLA Ops:
  2.4 77.6 %copy-start.1 = (bf16[3,64,128]{2,1,0:T(8,128)(2,1)S(1)}, bf16[3,64,128]{2,1,0:T(8,128)(2,1)}, u32[]{:S(2)}) copy-start(bf16[3,64,128]{2,1,0:T(8,128)(2,1)} %vec.3) | copy-start | bytes 147460
  2.4 77.6 %copy-start.2 = (bf16[64,192]{1,0:T(8,128)(2,1)S(1)}, bf16[64,192]{1,0:T(8,128)(2,1)}, u32[]{:S(2)}) copy-start(bf16[64,192]{1,0:T(8,128)(2,1)} %message_weight.1) | copy-start | bytes 73732
  2.4 77.6 %copy-start.3 = (bf16[64,64]{1,0:T(8,128)(2,1)S(1)}, bf16[64,64]{1,0:T(8,128)(2,1)}, u32[]{:S(2)}) copy-start(bf16[64,64]{1,0:T(8,128)(2,1)} %node_weight.1) | copy-start | bytes 24580
  2.4 77.6 %copy-start.4 = (bf16[20,192]{1,0:T(8,128)(2,1)S(1)}, bf16[20,192]{1,0:T(8,128)(2,1)}, u32[]{:S(2)}) copy-start(bf16[20,192]{1,0:T(8,128)(2,1)} %radial_weight.1) | copy-start | bytes 23044
  2.4 77.6 %copy-start.5 = (s32[16,128]{1,0:T(8,128)S(1)}, s32[16,128]{1,0:T(8,128)}, u32[]{:S(2)}) copy-start(s32[16,128]{1,0:T(8,128)} %ids.1) | copy-start | bytes 24580
  2.4 77.6 %copy-start.7 = (f32[64]{0:T(128)S(1)}, f32[64]{0:T(128)}, u32[]{:S(2)}) copy-start(f32[64]{0:T(128)} %param.20) | copy-start | bytes 772
  2.4 23.6 %all-to-all-start = ((bf16[32,80,128]{2,1,0:T(8,128)(2,1)}), bf16[32,80,128]{2,1,0:T(8,128)(2,1)S(1)}, u32[]{:S(2)}, u32[]{:S(2)}) async-start(bf16[32,80,128]{2,1,0:T(8,128)(2,1)} %broadcast_in_dim.3), calls=%async_computation | async-start | bytes 1310720 | tf_op jit(solution)/shard_map/all_to_all | solution.py:207
  13.0 0.8 copy-start
  13.8 0.7 copy-start.6
  14.7 7.8 %collective-permute-start = (bf16[272,128]{1,0:T(8,128)(2,1)S(1)}, bf16[272,128]{1,0:T(8,128)(2,1)S(1)}, u32[]{:S(2)}, u32[]{:S(2)}) collective-permute-start(bf16[272,128]{1,0:T(8,128)(2,1)S(1)} %get-tuple-element.8), channel_id=1, source_target_pairs={{0,1},{1,2},{2,3},{3,4},{4,5},{5,6},{6,7},{7,8},{8,9},{9,10},{10,1... | collective-permute-start | bytes 208904 | tf_op jit(solution)/shard_map/ppermute | solution.py:211
  18.2 5.9 %collective-permute-start.1 = (bf16[272,128]{1,0:T(8,128)(2,1)S(1)}, bf16[272,128]{1,0:T(8,128)(2,1)S(1)}, u32[]{:S(2)}, u32[]{:S(2)}) collective-permute-start(bf16[272,128]{1,0:T(8,128)(2,1)S(1)} %get-tuple-element.9), channel_id=1, source_target_pairs={{0,511},{1,0},{2,1},{3,2},{4,3},{5,4},{6,5},{7,6},{8,7},{9,8},{10,... | collective-permute-start | bytes 208904 | tf_op jit(solution)/shard_map/ppermute | solution.py:211
  73.1 18.4 %all-to-all-start.3 = ((bf16[32,64,128]{2,1,0:T(8,128)(2,1)}), bf16[32,64,128]{2,1,0:T(8,128)(2,1)S(1)}, u32[]{:S(2)}, u32[]{:S(2)}) async-start(bf16[32,64,128]{2,1,0:T(8,128)(2,1)} %shard_map.134.messages), calls=%async_computation.3 | async-start | bytes 1048576 | tf_op jit(solution)/shard_map/all_to_all | solution.py:207

commit v5 on v4

--- a/solution.py
+++ b/solution.py
@@ -85,15 +85,14 @@
     return pieces[0:3] + pieces[3:6] + pieces[6:9]
 
 
-def halo_kernel(packed, vec, halo, up, down):
+def halo_kernel(row, packed, vec, halo, after, out):
     rows = jnp.concatenate([packed[...], vec[0], vec[1], vec[2]], axis=0)
     atom = lax.broadcasted_iota(jnp.int32, (ATOM, ATOM), 0)
-    for side, out in ((0, up), (1, down)):
-        chosen = jnp.where(atom == halo[side : side + 1, :], 1.0, 0.0).astype(jnp.bfloat16)
-        out[...] = dot(rows, chosen, ((1,), (0,))).astype(jnp.bfloat16)
-
-
-def table_kernel(got, lattice, below, above, own_filter, table, partial, columns, total):
+    chosen = jnp.where(atom == halo[pl.ds(row[0], 1), :], 1.0, 0.0).astype(jnp.bfloat16)
+    out[...] = dot(rows, chosen, ((1,), (0,))).astype(jnp.bfloat16)
+
+
+def table_kernel(got, lattice, far, own_filter, table, partial, columns, total):
     turned = lattice[...].T
     for i in range(3):
         columns[i] = jnp.broadcast_to(turned[:, i : i + 1], (KDEV, ATOM))
@@ -152,18 +151,21 @@
 
 
 def short_kernel(
-    packed, vec, ids, below, above, node_weight, bias, message_weight, radial_weight, messages,
-    scalar_out, vector_out, ext, chosen, filters, directions,
+    core, packed, vec, ids, near, far, node_weight, bias, message_weight, radial_weight,
+    scalar_out, vector_out, feats, ext, chosen, filters, directions,
 ):
     pos = summed(packed[F:].astype(jnp.float32))
+    feats[:, :ATOM] = packed[:F]
     ext[192:384, :ATOM] = jnp.concatenate([vec[0], vec[1], vec[2]], axis=0)
     ext[384:, :ATOM] = packed[F:]
-    for side, at in ((below, ATOM), (above, 2 * ATOM)):
-        ext[192:384, at : at + ATOM] = side[PACK:]
-        ext[384:, at : at + ATOM] = side[F:PACK]
-    ext_feat = jnp.concatenate([packed[:F], below[:F], above[:F]], axis=1)
+    near_at = pl.ds(pl.multiple_of((2 - core[0]) * ATOM, ATOM), ATOM)
+    far_at = pl.ds(pl.multiple_of((1 + core[0]) * ATOM, ATOM), ATOM)
+    for side, at in ((near, near_at), (far, far_at)):
+        feats[:, at] = side[:F]
+        ext[192:384, at] = side[PACK:]
+        ext[384:, at] = side[F:PACK]
     bias_column = jnp.broadcast_to(bias[...], (8, F)).T[:, 0:1]
-    hidden = dot(node_weight[...], ext_feat, ((0,), (0,))) + bias_column
+    hidden = dot(node_weight[...], feats[...], ((0,), (0,))) + bias_column
     hidden = (hidden / (1.0 + jnp.exp(-hidden))).astype(jnp.bfloat16)
     ext[:192] = dot(message_weight[...], hidden, ((0,), (0,))).astype(jnp.bfloat16)
 
@@ -207,8 +209,9 @@
     return lax.all_to_all(x, axes, split_axis=0, concat_axis=0, tiled=True)
 
 
-def shifted(x, steps):
-    return lax.ppermute(x, all_axes, [(i, (i + steps) % SLABS) for i in range(SLABS)])
+def swapped(x, first):
+    pairs = [((first + i) % SLABS, (first + (i ^ 1)) % SLABS) for i in range(SLABS)]
+    return lax.ppermute(x, all_axes, pairs)
 
 
 def shards(
@@ -224,14 +227,17 @@
     own_lattice = jnp.pad(lax.dynamic_slice_in_dim(lattice, k_at, KDEV, 1).astype(f32), ((0, 5), (0, 0)))
     own_filter = jnp.pad(lax.dynamic_slice_in_dim(kspace_filter, half_at, KDEV, 1) * norm_scale, ((0, 0), (0, F)))
     own_filter = own_filter + jnp.pad(ewald_weight.astype(f32), ((0, 0), (KDEV, 0)))
+    core = lax.axis_index("c").astype(jnp.int32).reshape(1)
     halo = shape((HALO_ROWS, ATOM), bf16)
-    up, down = call(halo_kernel, [VM] * 3, (halo, halo), packed, vectors, halo_lists)
-    below, above = shifted(up, 1), shifted(down, -1)
+    far = call(
+        halo_kernel, [SM, VM, VM, VM, ANY], halo, 1 - core, packed, vectors, halo_lists, own_lattice
+    )
+    far = swapped(far, 1)
     table, partial = call(
         table_kernel,
-        [VM, VM, ANY, ANY, ANY],
+        [VM, VM, ANY, ANY],
         (shape((2 * KDEV, PLANE * ATOM), bf16), shape((KDEV, 2 * F), bf16)),
-        got, own_lattice, below, above, own_filter,
+        got, own_lattice, far, own_filter,
         scratch=[VM((3, KDEV, ATOM), f32), VM((2 * KDEV, F), f32)],
     )
     arrived = exchanged(partial.reshape(DEPTH, KDEV // DEPTH, 2 * F), "z")
@@ -241,13 +247,16 @@
         project_kernel, [VM] * 3, shape((PLANE, F, ATOM), bf16), totals, own_filter, table
     )
     returned = exchanged(messages, plane_axes)
+    near = call(halo_kernel, [SM, VM, VM, VM, ANY], halo, core, packed, vectors, halo_lists, messages)
+    near = swapped(near, 0)
     scalar, new_vectors = call(
         short_kernel,
-        [VM] * 9 + [ANY],
+        [SM] + [VM] * 9,
         (shape((F, ATOM), f32), shape((3, F, ATOM), bf16)),
-        packed, vectors, neighbours, below, above,
-        node_weight, node_bias.reshape(1, F), message_weight, radial_weight, messages,
+        core, packed, vectors, neighbours, near, far,
+        node_weight, node_bias.reshape(1, F), message_weight, radial_weight,
         scratch=[
+            VM((F, 3 * ATOM), bf16),
             VM((400, 3 * ATOM), bf16),
             VM((3 * ATOM, NBR * ATOM), bf16),
             VM((192, NBR * ATOM), f32),

time: 92.9 us -> 92.3 us (level)
    all_to_all x2, waiting for transfers between devices: 9.42 us -> 6.78 us  [exchanged(): return lax.all_to_all(x, axes, split_axis=0, concat_axis=0, tiled=True)]
    ppermute x2, waiting for transfers between devices: 1.71 us -> 3.95 us  [swapped(): return lax.ppermute(x, all_axes, pairs)]
    pallas_call x6 -> x7, Pallas kernels: 11.5 us -> 11.6 us  [call(): pl.pallas_call(kernel, out_shape=outs, in_specs=[pl.BlockSpec(memory_spac...]
  transfers between devices with their start and end apart: 4 -> 4, of which waited for: 3 -> 4; matrix products, arithmetic and copies ran while one was open for 2% -> 2% of each run, Pallas kernels for 4% -> 5%
where the time goes in v5:
time: 92.3 us; the launch traced here: 91.6 us
  blocking collectives  40 us (43%)
  starting transfers between devices  23 us (25%)
  Pallas kernels  11.6 us (13%)
  waiting for transfers between devices  10.7 us (12%)
  other arithmetic  3.08 us (3%)
  local copies, waits for them, and re-layouts  2.45 us (3%)
    all_to_all x2, blocking collectives, exchanged(): return lax.all_to_all(x, axes, split_axis=0, concat_axis=0, tiled=True)  40 us
    all_to_all x2, starting transfers between devices, exchanged(): return lax.all_to_all(x, axes, split_axis=0, concat_axis=0, tiled=True)  17.3 us
    pallas_call x7, Pallas kernels, call(): pl.pallas_call(kernel, out_shape=outs, in_specs=[pl.BlockSpec(memory_spac...  11.6 us
    all_to_all x2, waiting for transfers between devices, exchanged(): return lax.all_to_all(x, axes, split_axis=0, concat_axis=0, tiled=True)  6.78 us
    ppermute x2, starting transfers between devices, swapped(): return lax.ppermute(x, all_axes, pairs)  5.69 us
    ppermute x2, waiting for transfers between devices, swapped(): return lax.ppermute(x, all_axes, pairs)  3.95 us
  transfers between devices with their start and end apart: 4, of which 4 were waited for; matrix products, arithmetic and copies ran while one was open for 2% of the time, Pallas kernels for 5%

profile of v5, /device:TPU:1, one launch (start us, length us, event | category | flops | bytes accessed | tf_op | source)
XLA Modules:
  0.0 91.6 jit_solution(13670297592141685738)
XLA Ops:
  0.6 0.8 fusion.4.packed
  1.4 0.9 %broadcast_in_dim.3 = bf16[32,80,128]{2,1,0:T(8,128)(2,1)} broadcast(bf16[80,128]{1,0:T(8,128)(2,1)S(1)} %fusion.4.packed), dimensions={1,2} | broadcast | bytes 675840 | tf_op jit(solution)/shard_map/broadcast_in_dim | solution.py:226
  2.4 10.6 %all-to-all-start = ((bf16[32,80,128]{2,1,0:T(8,128)(2,1)}), bf16[32,80,128]{2,1,0:T(8,128)(2,1)S(1)}, u32[]{:S(2)}, u32[]{:S(2)}) async-start(bf16[32,80,128]{2,1,0:T(8,128)(2,1)} %broadcast_in_dim.3), calls=%async_computation | async-start | bytes 1310720 | tf_op jit(solution)/shard_map/all_to_all | solution.py:209
  12.9 0.0 copy-start.2
  13.0 0.0 copy-start.3
  13.0 0.0 copy-start.4
  13.0 0.0 copy-start.8
  13.0 0.7 dynamic-slice_convert_fusion
  13.7 0.8 copy-done
  14.5 0.7 copy-done.6
  15.2 0.2 shard_map.131
  15.4 3.5 %collective-permute-start = (bf16[272,128]{1,0:T(8,128)(2,1)S(1)}, bf16[272,128]{1,0:T(8,128)(2,1)S(1)}, u32[]{:S(2)}, u32[]{:S(2)}) collective-permute-start(bf16[272,128]{1,0:T(8,128)(2,1)S(1)} %shard_map.131), channel_id=1, source_target_pairs={{1,2},{2,1},{3,4},{4,3},{5,6},{6,5},{7,8},{8,7},{9,10},{10,9},{11,... | collective-permute-start | bytes 208904 | tf_op jit(solution)/shard_map/ppermute | solution.py:214
  18.9 0.9 dynamic-slice_multiply_fusion
  19.8 0.7 convert_add_fusion.own_filter
  20.5 2.9 %collective-permute-done.far = bf16[272,128]{1,0:T(8,128)(2,1)S(1)} collective-permute-done((bf16[272,128]{1,0:T(8,128)(2,1)S(1)}, bf16[272,128]{1,0:T(8,128)(2,1)S(1)}, u32[]{:S(2)}, u32[]{:S(2)}) %collective-permute-start) | collective-permute-done | bytes 69664 | tf_op jit(solution)/shard_map/ppermute | solution.py:214
  23.4 2.5 %all-to-all-done.got = bf16[32,80,128]{2,1,0:T(8,128)(2,1)S(1)} async-done(((bf16[32,80,128]{2,1,0:T(8,128)(2,1)}), bf16[32,80,128]{2,1,0:T(8,128)(2,1)S(1)}, u32[]{:S(2)}, u32[]{:S(2)}) %all-to-all-start) | async-done | bytes 655392 | tf_op jit(solution)/shard_map/all_to_all | solution.py:209
  26.0 4.8 %shard_map.132 = (bf16[512,4096]{1,0:T(8,128)(2,1)S(1)}, bf16[256,128]{1,0:T(8,128)(2,1)S(1)}) custom-call(bf16[32,80,128]{2,1,0:T(8,128)(2,1)S(1)} %all-to-all-done.got, f32[8,256]{1,0:T(8,128)S(1)} %pad.35.after.lattice, bf16[272,128]{1,0:T(8,128)(2,1)S(1)} %collective-permute-done.far, f32[64,320]{1,0:T(8,128)S(1)} %convert_add_fusion.own_filter), custom_call_target="tpu_custom_call" | custom-call | tf_op jit(solution)/shard_map/pallas_call | solution.py:65
  30.8 24.6 %all_to_all.20.arrived = bf16[16,16,128]{2,1,0:T(8,128)(2,1)S(1)} all-to-all(bf16[16,16,128]{2,1,0:T(8,128)(2,1)S(1)} %bitcast.5), channel_id=1, replica_groups=mesh['yh'=2,'z'=16,'yl'=2,'x'=4,'c'=2] {'z'}, dimensions={0} | all-to-all | bytes 131072 | tf_op jit(solution)/shard_map/all_to_all | solution.py:209
  55.4 15.3 %all_to_all.21 = bf16[16,16,128]{2,1,0:T(8,128)(2,1)S(1)} all-to-all(bf16[16,16,128]{2,1,0:T(8,128)(2,1)S(1)} %shard_map.133), channel_id=1, replica_groups=mesh['yh'=2,'z'=16,'yl'=2,'x'=4,'c'=2] {'z'}, dimensions={0} | all-to-all | bytes 131072 | tf_op jit(solution)/shard_map/all_to_all | solution.py:209
  70.8 1.8 %shard_map.134.after = bf16[32,64,128]{2,1,0:T(8,128)(2,1)} custom-call(bf16[256,128]{1,0:T(8,128)(2,1)S(1)} %bitcast.4, f32[64,320]{1,0:T(8,128)S(1)} %convert_add_fusion.own_filter, bf16[512,4096]{1,0:T(8,128)(2,1)S(1)} %get-tuple-element.7.table), custom_call_target="tpu_custom_call" | custom-call | tf_op jit(solution)/shard_map/pallas_call | solution.py:65
  72.6 6.7 %all-to-all-start.3 = ((bf16[32,64,128]{2,1,0:T(8,128)(2,1)}), bf16[32,64,128]{2,1,0:T(8,128)(2,1)S(1)}, u32[]{:S(2)}, u32[]{:S(2)}) async-start(bf16[32,64,128]{2,1,0:T(8,128)(2,1)} %shard_map.134.after), calls=%async_computation.3 | async-start | bytes 1048576 | tf_op jit(solution)/shard_map/all_to_all | solution.py:209
  79.3 0.0 copy-done.1
  79.4 0.0 copy-done.7
  79.4 0.2 shard_map.135
  79.5 2.1 %collective-permute-start.1 = (bf16[272,128]{1,0:T(8,128)(2,1)S(1)}, bf16[272,128]{1,0:T(8,128)(2,1)S(1)}, u32[]{:S(2)}, u32[]{:S(2)}) collective-permute-start(bf16[272,128]{1,0:T(8,128)(2,1)S(1)} %shard_map.135), channel_id=1, source_target_pairs={{0,1},{1,0},{2,3},{3,2},{4,5},{5,4},{6,7},{7,6},{8,9},{9,8},{10,11... | collective-permute-start | bytes 208904 | tf_op jit(solution)/shard_map/ppermute | solution.py:214
  81.7 1.0 %collective-permute-done.1.near = bf16[272,128]{1,0:T(8,128)(2,1)S(1)} collective-permute-done((bf16[272,128]{1,0:T(8,128)(2,1)S(1)}, bf16[272,128]{1,0:T(8,128)(2,1)S(1)}, u32[]{:S(2)}, u32[]{:S(2)}) %collective-permute-start.1) | collective-permute-done | bytes 69664 | tf_op jit(solution)/shard_map/ppermute | solution.py:214
  82.7 0.0 copy-done.5
  82.7 0.0 copy-done.2
  82.7 0.0 copy-done.3
  82.7 3.9 %shard_map.136 = (f32[64,128]{1,0:T(8,128)S(1)}, bf16[3,64,128]{2,1,0:T(8,128)(2,1)}) custom-call(s32[1]{0:T(128)} %bitcast.row.core, bf16[80,128]{1,0:T(8,128)(2,1)S(1)} %fusion.4.packed, bf16[3,64,128]{2,1,0:T(8,128)(2,1)S(1)} %copy-done.1, s32[16,128]{1,0:T(8,128)S(1)} %copy-done.5, bf16[272,128]{1,0:T(8,128)(2,1)S(1)} %collective-permute-done.1.near, ...), custom_call_target="tpu_custom_call" | custom-call | tf_op jit(solution)/shard_map/pallas_call | solution.py:65
  86.6 4.3 %all-to-all-done.3.arrived = bf16[32,64,128]{2,1,0:T(8,128)(2,1)S(1)} async-done(((bf16[32,64,128]{2,1,0:T(8,128)(2,1)}), bf16[32,64,128]{2,1,0:T(8,128)(2,1)S(1)}, u32[]{:S(2)}, u32[]{:S(2)}) %all-to-all-start.3) | async-done | bytes 524320 | tf_op jit(solution)/shard_map/all_to_all | solution.py:209
  90.9 0.7 shard_map.137
  (9 shorter events, 0.0 us)
Async XLA Ops:
  2.4 77.0 %copy-start.1 = (bf16[3,64,128]{2,1,0:T(8,128)(2,1)S(1)}, bf16[3,64,128]{2,1,0:T(8,128)(2,1)}, u32[]{:S(2)}) copy-start(bf16[3,64,128]{2,1,0:T(8,128)(2,1)} %vec.5) | copy-start | bytes 147460
  2.4 77.0 %copy-start.7 = (s32[2,128]{1,0:T(2,128)S(1)}, s32[2,128]{1,0:T(2,128)}, u32[]{:S(2)}) copy-start(s32[2,128]{1,0:T(2,128)} %halo.3) | copy-start | bytes 3076
  2.4 80.3 %copy-start.5 = (s32[16,128]{1,0:T(8,128)S(1)}, s32[16,128]{1,0:T(8,128)}, u32[]{:S(2)}) copy-start(s32[16,128]{1,0:T(8,128)} %ids.1) | copy-start | bytes 24580
  2.4 23.6 %all-to-all-start = ((bf16[32,80,128]{2,1,0:T(8,128)(2,1)}), bf16[32,80,128]{2,1,0:T(8,128)(2,1)S(1)}, u32[]{:S(2)}, u32[]{:S(2)}) async-start(bf16[32,80,128]{2,1,0:T(8,128)(2,1)} %broadcast_in_dim.3), calls=%async_computation | async-start | bytes 1310720 | tf_op jit(solution)/shard_map/all_to_all | solution.py:209
  12.9 69.8 %copy-start.2 = (bf16[64,192]{1,0:T(8,128)(2,1)S(1)}, bf16[64,192]{1,0:T(8,128)(2,1)}, u32[]{:S(2)}) copy-start(bf16[64,192]{1,0:T(8,128)(2,1)} %message_weight.1) | copy-start | bytes 73732
  13.0 69.7 %copy-start.3 = (bf16[64,64]{1,0:T(8,128)(2,1)S(1)}, bf16[64,64]{1,0:T(8,128)(2,1)}, u32[]{:S(2)}) copy-start(bf16[64,64]{1,0:T(8,128)(2,1)} %node_weight.1) | copy-start | bytes 24580
  13.0 69.7 %copy-start.4 = (bf16[20,192]{1,0:T(8,128)(2,1)S(1)}, bf16[20,192]{1,0:T(8,128)(2,1)}, u32[]{:S(2)}) copy-start(bf16[20,192]{1,0:T(8,128)(2,1)} %radial_weight.1) | copy-start | bytes 23044
  13.0 69.7 %copy-start.8 = (f32[64]{0:T(128)S(1)}, f32[64]{0:T(128)}, u32[]{:S(2)}) copy-start(f32[64]{0:T(128)} %param.20) | copy-start | bytes 772
  13.7 0.8 copy-start
  14.5 0.7 copy-start.6
  15.4 8.1 %collective-permute-start = (bf16[272,128]{1,0:T(8,128)(2,1)S(1)}, bf16[272,128]{1,0:T(8,128)(2,1)S(1)}, u32[]{:S(2)}, u32[]{:S(2)}) collective-permute-start(bf16[272,128]{1,0:T(8,128)(2,1)S(1)} %shard_map.131), channel_id=1, source_target_pairs={{1,2},{2,1},{3,4},{4,3},{5,6},{6,5},{7,8},{8,7},{9,10},{10,9},{11,... | collective-permute-start | bytes 208904 | tf_op jit(solution)/shard_map/ppermute | solution.py:214
  72.6 18.3 %all-to-all-start.3 = ((bf16[32,64,128]{2,1,0:T(8,128)(2,1)}), bf16[32,64,128]{2,1,0:T(8,128)(2,1)S(1)}, u32[]{:S(2)}, u32[]{:S(2)}) async-start(bf16[32,64,128]{2,1,0:T(8,128)(2,1)} %shard_map.134.after), calls=%async_computation.3 | async-start | bytes 1048576 | tf_op jit(solution)/shard_map/all_to_all | solution.py:209
  79.5 3.2 %collective-permute-start.1 = (bf16[272,128]{1,0:T(8,128)(2,1)S(1)}, bf16[272,128]{1,0:T(8,128)(2,1)S(1)}, u32[]{:S(2)}, u32[]{:S(2)}) collective-permute-start(bf16[272,128]{1,0:T(8,128)(2,1)S(1)} %shard_map.135), channel_id=1, source_target_pairs={{0,1},{1,0},{2,3},{3,2},{4,5},{5,4},{6,7},{7,6},{8,9},{9,8},{10,11... | collective-permute-start | bytes 208904 | tf_op jit(solution)/shard_map/ppermute | solution.py:214

commit v6 on v5

--- a/solution.py
+++ b/solution.py
@@ -20,7 +20,8 @@
 ATOMS = 65536
 PACK = 80
 HALO_ROWS = 272
-GROUP = 8
+GROUP = 4
+SPARE = 11
 
 plane_axes = ("yh", "yl", "x", "c")
 kb_axes = ("yl", "x", "c")
@@ -61,12 +62,15 @@
 VM, SM, ANY = pltpu.VMEM, pltpu.SMEM, pl.ANY
 
 
-def call(kernel, places, outs, *operands, scratch=()):
+def call(kernel, places, outs, *operands, scratch=(), kept=None, far_outs=()):
     return pl.pallas_call(
         kernel,
         out_shape=outs,
         in_specs=[pl.BlockSpec(memory_space=place) for place in places],
-        out_specs=jax.tree.map(lambda _: pl.BlockSpec(memory_space=VM), outs),
+        out_specs=jax.tree.map(lambda _: pl.BlockSpec(memory_space=VM), outs)
+        if kept is None
+        else [pl.BlockSpec(memory_space=ANY if i in far_outs else VM) for i in range(len(outs))],
+        input_output_aliases=kept or {},
         scratch_shapes=list(scratch),
         compiler_params=pltpu.CompilerParams(vmem_limit_bytes=VMEM_LIMIT),
         cost_estimate=pl.CostEstimate(flops=0, bytes_accessed=0, transcendentals=0),
@@ -85,18 +89,23 @@
     return pieces[0:3] + pieces[3:6] + pieces[6:9]
 
 
-def halo_kernel(row, packed, vec, halo, after, out):
+def halo_kernel(core, packed, vec, halo, far, near):
     rows = jnp.concatenate([packed[...], vec[0], vec[1], vec[2]], axis=0)
     atom = lax.broadcasted_iota(jnp.int32, (ATOM, ATOM), 0)
-    chosen = jnp.where(atom == halo[pl.ds(row[0], 1), :], 1.0, 0.0).astype(jnp.bfloat16)
-    out[...] = dot(rows, chosen, ((1,), (0,))).astype(jnp.bfloat16)
-
-
-def table_kernel(got, lattice, far, own_filter, table, partial, columns, total):
+    for row, out in ((1 - core[0], far), (core[0], near)):
+        chosen = jnp.where(atom == halo[pl.ds(row, 1), :], 1.0, 0.0).astype(jnp.bfloat16)
+        out[...] = dot(rows, chosen, ((1,), (0,))).astype(jnp.bfloat16)
+
+
+def table_kernel(got, lattice, far, own_filter, table_at, partial, far_kept, table, columns, total, done):
     turned = lattice[...].T
     for i in range(3):
         columns[i] = jnp.broadcast_to(turned[:, i : i + 1], (KDEV, ATOM))
     total[...] = jnp.zeros_like(total)
+
+    def stored(step):
+        atoms = pl.ds(pl.multiple_of(step * GROUP * ATOM, GROUP * ATOM), GROUP * ATOM)
+        return pltpu.make_async_copy(table.at[:, atoms], table_at.at[0, :, atoms], done.at[step])
 
     @pl.loop(0, PLANE // GROUP)
     def _(step):
@@ -120,11 +129,14 @@
                 sums = dot(jnp.concatenate([cosines, sines], axis=0), both[:F], ((1,), (1,)))
                 total[k : k + 64] += sums[:64]
                 total[KDEV + k : KDEV + k + 64] += sums[64:]
+        stored(step).start()
 
     partial[...] = jnp.concatenate([total[:KDEV], total[KDEV:]], axis=1).astype(jnp.bfloat16)
-
-
-def sum_kernel(arrived, out):
+    for step in range(PLANE // GROUP):
+        stored(step).wait()
+
+
+def sum_kernel(arrived, near, out, near_kept):
     total = arrived[0].astype(jnp.float32)
     for i in range(1, DEPTH):
         total = total + arrived[i].astype(jnp.float32)
@@ -133,13 +145,21 @@
         out[i] = total
 
 
-def project_kernel(got, own_filter, table, out):
+def project_kernel(got, own_filter, table_at, near, out, table, done):
+    parts = ((0, 4), (4, 12), (12, 20), (20, 28), (28, 32))
+    loads = []
+    for i, (first, last) in enumerate(parts):
+        atoms = slice(first * ATOM, last * ATOM)
+        loads.append(pltpu.make_async_copy(table_at.at[0, :, atoms], table.at[:, atoms], done.at[i]))
+    for load in loads:
+        load.start()
     own, weight = own_filter[:, :KDEV], own_filter[:, KDEV:].astype(jnp.bfloat16)
     total = [dot(weight, got[:, part * F : (part + 1) * F], ((0,), (1,))) for part in range(2)]
     filtered = jnp.concatenate([own * total[0], own * total[1]], axis=1).astype(jnp.bfloat16)
-    for first in range(0, PLANE, 8):
-        message = dot(filtered, table[:, first * ATOM : (first + 8) * ATOM], ((1,), (0,))).astype(jnp.bfloat16)
-        for p in range(8):
+    for (first, last), load in zip(parts, loads):
+        load.wait()
+        message = dot(filtered, table[:, first * ATOM : last * ATOM], ((1,), (0,))).astype(jnp.bfloat16)
+        for p in range(last - first):
             out[first + p] = message[:, p * ATOM : (p + 1) * ATOM]
 
 
@@ -151,7 +171,7 @@
 
 
 def short_kernel(
-    core, packed, vec, ids, near, far, node_weight, bias, message_weight, radial_weight,
+    core, packed, vec, ids, near, far, node_weight, bias, message_weight, radial_weight, messages,
     scalar_out, vector_out, feats, ext, chosen, filters, directions,
 ):
     pos = summed(packed[F:].astype(jnp.float32))
@@ -229,32 +249,47 @@
     own_filter = own_filter + jnp.pad(ewald_weight.astype(f32), ((0, 0), (KDEV, 0)))
     core = lax.axis_index("c").astype(jnp.int32).reshape(1)
     halo = shape((HALO_ROWS, ATOM), bf16)
-    far = call(
-        halo_kernel, [SM, VM, VM, VM, ANY], halo, 1 - core, packed, vectors, halo_lists, own_lattice
-    )
-    far = swapped(far, 1)
-    table, partial = call(
+    far, near = call(halo_kernel, [SM, VM, VM, VM], (halo, halo), core, packed, vectors, halo_lists)
+    table, partial, far = call(
         table_kernel,
         [VM, VM, ANY, ANY],
-        (shape((2 * KDEV, PLANE * ATOM), bf16), shape((KDEV, 2 * F), bf16)),
+        (shape((SPARE, 2 * KDEV, PLANE * ATOM), bf16), shape((KDEV, 2 * F), bf16), halo),
         got, own_lattice, far, own_filter,
-        scratch=[VM((3, KDEV, ATOM), f32), VM((2 * KDEV, F), f32)],
+        scratch=[
+            VM((2 * KDEV, PLANE * ATOM), bf16),
+            VM((3, KDEV, ATOM), f32),
+            VM((2 * KDEV, F), f32),
+            pltpu.SemaphoreType.DMA((PLANE // GROUP,)),
+        ],
+        kept={2: 2},
+        far_outs=(0, 2),
     )
     arrived = exchanged(partial.reshape(DEPTH, KDEV // DEPTH, 2 * F), "z")
-    owned = call(sum_kernel, [VM], shape((DEPTH, KDEV // DEPTH, 2 * F), bf16), arrived)
+    far = swapped(far, 1)
+    owned, near = call(
+        sum_kernel,
+        [VM, ANY],
+        (shape((DEPTH, KDEV // DEPTH, 2 * F), bf16), halo),
+        arrived, near,
+        kept={1: 1},
+        far_outs=(1,),
+    )
+    near = swapped(near, 0)
     totals = exchanged(owned, "z").reshape(KDEV, 2 * F)
     messages = call(
-        project_kernel, [VM] * 3, shape((PLANE, F, ATOM), bf16), totals, own_filter, table
+        project_kernel,
+        [VM, VM, ANY, ANY],
+        shape((PLANE, F, ATOM), bf16),
+        totals, own_filter, table, near,
+        scratch=[VM((2 * KDEV, PLANE * ATOM), bf16), pltpu.SemaphoreType.DMA((5,))],
     )
     returned = exchanged(messages, plane_axes)
-    near = call(halo_kernel, [SM, VM, VM, VM, ANY], halo, core, packed, vectors, halo_lists, messages)
-    near = swapped(near, 0)
     scalar, new_vectors = call(
         short_kernel,
-        [SM] + [VM] * 9,
+        [SM] + [VM] * 9 + [ANY],
         (shape((F, ATOM), f32), shape((3, F, ATOM), bf16)),
         core, packed, vectors, neighbours, near, far,
-        node_weight, node_bias.reshape(1, F), message_weight, radial_weight,
+        node_weight, node_bias.reshape(1, F), message_weight, radial_weight, messages,
         scratch=[
             VM((F, 3 * ATOM), bf16),
             VM((400, 3 * ATOM), bf16),

time: 92.3 us -> 96.9 us (1.050)
  blocking collectives: 40 us -> 24.3 us
  waiting for transfers between devices: 10.7 us -> 22.4 us
  starting transfers between devices: 23 us -> 28.2 us
  Pallas kernels: 11.6 us -> 14.9 us
    all_to_all x2 -> x1, blocking collectives: 40 us -> 24.3 us  [exchanged(): return lax.all_to_all(x, axes, split_axis=0, concat_axis=0, tiled=True)]
    all_to_all x2 -> x3, waiting for transfers between devices: 6.78 us -> 15.9 us  [exchanged(): return lax.all_to_all(x, axes, split_axis=0, concat_axis=0, tiled=True)]
    all_to_all x2 -> x3, starting transfers between devices: 17.3 us -> 20.9 us  [exchanged(): return lax.all_to_all(x, axes, split_axis=0, concat_axis=0, tiled=True)]
    pallas_call x7 -> x6, Pallas kernels: 11.6 us -> 14.9 us  [call(): pl.pallas_call(kernel, out_shape=outs, in_specs=[pl.BlockSpec(memory_spac...]
    ppermute x2, waiting for transfers between devices: 3.95 us -> 6.43 us  [swapped(): return lax.ppermute(x, all_axes, pairs)]
    ppermute x2, starting transfers between devices: 5.69 us -> 7.3 us  [swapped(): return lax.ppermute(x, all_axes, pairs)]
  transfers between devices with their start and end apart: 4 -> 5, of which waited for: 4 -> 4; matrix products, arithmetic and copies ran while one was open for 2% -> 2% of each run, Pallas kernels for 5% -> 4%
where the time goes in v6:
time: 96.9 us; the launch traced here: 96 us
  starting transfers between devices  28.2 us (29%)
  blocking collectives  24.3 us (25%)
  waiting for transfers between devices  22.4 us (23%)
  Pallas kernels  14.9 us (15%)
  other arithmetic  3.09 us (3%)
  local copies, waits for them, and re-layouts  2.45 us (3%)
    all_to_all x1, blocking collectives, exchanged(): return lax.all_to_all(x, axes, split_axis=0, concat_axis=0, tiled=True)  24.3 us
    all_to_all x3, starting transfers between devices, exchanged(): return lax.all_to_all(x, axes, split_axis=0, concat_axis=0, tiled=True)  20.9 us
    all_to_all x3, waiting for transfers between devices, exchanged(): return lax.all_to_all(x, axes, split_axis=0, concat_axis=0, tiled=True)  15.9 us
    pallas_call x6, Pallas kernels, call(): pl.pallas_call(kernel, out_shape=outs, in_specs=[pl.BlockSpec(memory_spac...  14.9 us
    ppermute x2, starting transfers between devices, swapped(): return lax.ppermute(x, all_axes, pairs)  7.3 us
    ppermute x2, waiting for transfers between devices, swapped(): return lax.ppermute(x, all_axes, pairs)  6.43 us
  transfers between devices with their start and end apart: 5, of which 4 were waited for; matrix products, arithmetic and copies ran while one was open for 2% of the time, Pallas kernels for 4%

profile of v6, /device:TPU:1, one launch (start us, length us, event | category | flops | bytes accessed | tf_op | source)
XLA Modules:
  0.0 96.0 jit_solution(1777488059905206176)
XLA Ops:
  0.6 0.0 copy-start.1
  0.6 0.0 copy-start.4
  0.7 0.0 copy-start.2
  0.7 0.0 copy-start.7
  0.7 0.0 copy-start.3
  0.7 0.0 copy-start.5
  0.7 0.8 fusion.4.packed
  1.5 0.9 broadcast_in_dim.3
  2.5 10.4 %all-to-all-start = ((bf16[32,80,128]{2,1,0:T(8,128)(2,1)}), bf16[32,80,128]{2,1,0:T(8,128)(2,1)S(1)}, u32[]{:S(2)}, u32[]{:S(2)}) async-start(bf16[32,80,128]{2,1,0:T(8,128)(2,1)} %broadcast_in_dim.3), calls=%async_computation | async-start | bytes 1310720 | tf_op jit(solution)/shard_map/all_to_all | solution.py:229
  12.9 0.7 dynamic-slice_convert_fusion
  13.6 0.8 copy-done
  14.4 0.7 copy-done.6
  15.1 0.2 shard_map.131
  15.3 0.9 dynamic-slice_multiply_fusion
  16.2 0.7 convert_add_fusion.own_filter
  16.9 9.0 %all-to-all-done.got = bf16[32,80,128]{2,1,0:T(8,128)(2,1)S(1)} async-done(((bf16[32,80,128]{2,1,0:T(8,128)(2,1)}), bf16[32,80,128]{2,1,0:T(8,128)(2,1)S(1)}, u32[]{:S(2)}, u32[]{:S(2)}) %all-to-all-start) | async-done | bytes 655392 | tf_op jit(solution)/shard_map/all_to_all | solution.py:229
  25.9 6.0 %shard_map.132 = (bf16[11,512,4096]{2,1,0:T(8,128)(2,1)}, bf16[256,128]{1,0:T(8,128)(2,1)S(1)}, bf16[272,128]{1,0:T(8,128)(2,1)S(1)}) custom-call(bf16[32,80,128]{2,1,0:T(8,128)(2,1)S(1)} %all-to-all-done.got, f32[8,256]{1,0:T(8,128)S(1)} %pad.35.lattice, bf16[272,128]{1,0:T(8,128)(2,1)S(1)} %get-tuple-element.11.far, ...), custom_call_target="tpu_custom_call", output_to_operand_aliasing={{2}: (2, {})} | custom-call | tf_op jit(solution)/shard_map/pallas_call | solution.py:66
  31.9 24.3 %all_to_all.20.arrived = bf16[16,16,128]{2,1,0:T(8,128)(2,1)S(1)} all-to-all(bf16[16,16,128]{2,1,0:T(8,128)(2,1)S(1)} %bitcast.5), channel_id=1, replica_groups=mesh['yh'=2,'z'=16,'yl'=2,'x'=4,'c'=2] {'z'}, dimensions={0} | all-to-all | bytes 131072 | tf_op jit(solution)/shard_map/all_to_all | solution.py:229
  56.3 0.6 shard_map.133
  56.9 3.8 %all-to-all-start.2 = ((bf16[16,16,128]{2,1,0:T(8,128)(2,1)}), bf16[16,16,128]{2,1,0:T(8,128)(2,1)S(1)}, u32[]{:S(2)}, u32[]{:S(2)}) async-start(bf16[16,16,128]{2,1,0:T(8,128)(2,1)} %get-tuple-element.14), calls=%async_computation.2 | async-start | bytes 131072 | tf_op jit(solution)/shard_map/all_to_all | solution.py:229
  60.7 3.8 %collective-permute-start = (bf16[272,128]{1,0:T(8,128)(2,1)S(1)}, bf16[272,128]{1,0:T(8,128)(2,1)S(1)}, u32[]{:S(2)}, u32[]{:S(2)}) collective-permute-start(bf16[272,128]{1,0:T(8,128)(2,1)S(1)} %get-tuple-element.16), channel_id=1, source_target_pairs={{0,1},{1,0},{2,3},{3,2},{4,5},{5,4},{6,7},{7,6},{8,9},{9,8},{10,11... | collective-permute-start | bytes 208904 | tf_op jit(solution)/shard_map/ppermute | solution.py:234
  64.5 0.9 collective-permute-done.near
  65.4 6.9 %all-to-all-done.2 = bf16[16,16,128]{2,1,0:T(8,128)(2,1)S(1)} async-done(((bf16[16,16,128]{2,1,0:T(8,128)(2,1)}), bf16[16,16,128]{2,1,0:T(8,128)(2,1)S(1)}, u32[]{:S(2)}, u32[]{:S(2)}) %all-to-all-start.2) | async-done | bytes 65568 | tf_op jit(solution)/shard_map/all_to_all | solution.py:229
  72.3 3.4 %shard_map.134.messages = bf16[32,64,128]{2,1,0:T(8,128)(2,1)} custom-call(bf16[256,128]{1,0:T(8,128)(2,1)S(1)} %bitcast.4, f32[64,320]{1,0:T(8,128)S(1)} %convert_add_fusion.own_filter, bf16[11,512,4096]{2,1,0:T(8,128)(2,1)} %get-tuple-element.15.table_at, bf16[272,128]{1,0:T(8,128)(2,1)S(1)} %collective-permute-done.near), custom_call_target="tpu_custom_call" | custom-call | tf_op jit(solution)/shard_map/pallas_call | solution.py:66
  75.7 6.6 %all-to-all-start.3 = ((bf16[32,64,128]{2,1,0:T(8,128)(2,1)}), bf16[32,64,128]{2,1,0:T(8,128)(2,1)S(1)}, u32[]{:S(2)}, u32[]{:S(2)}) async-start(bf16[32,64,128]{2,1,0:T(8,128)(2,1)} %shard_map.134.messages), calls=%async_computation.3 | async-start | bytes 1048576 | tf_op jit(solution)/shard_map/all_to_all | solution.py:229
  82.3 3.5 %collective-permute-start.1 = (bf16[272,128]{1,0:T(8,128)(2,1)S(1)}, bf16[272,128]{1,0:T(8,128)(2,1)S(1)}, u32[]{:S(2)}, u32[]{:S(2)}) collective-permute-start(bf16[272,128]{1,0:T(8,128)(2,1)S(1)} %get-tuple-element.17), channel_id=1, source_target_pairs={{1,2},{2,1},{3,4},{4,3},{5,6},{6,5},{7,8},{8,7},{9,10},{10,9},{11,... | collective-permute-start | bytes 208904 | tf_op jit(solution)/shard_map/ppermute | solution.py:234
  85.9 5.5 %collective-permute-done.1.far = bf16[272,128]{1,0:T(8,128)(2,1)S(1)} collective-permute-done((bf16[272,128]{1,0:T(8,128)(2,1)S(1)}, bf16[272,128]{1,0:T(8,128)(2,1)S(1)}, u32[]{:S(2)}, u32[]{:S(2)}) %collective-permute-start.1) | collective-permute-done | bytes 69664 | tf_op jit(solution)/shard_map/ppermute | solution.py:234
  91.4 0.0 copy-done.1
  91.4 0.0 copy-done.4
  91.4 3.9 %shard_map.135 = (f32[64,128]{1,0:T(8,128)S(1)}, bf16[3,64,128]{2,1,0:T(8,128)(2,1)}) custom-call(s32[1]{0:T(128)} %bitcast.core, bf16[80,128]{1,0:T(8,128)(2,1)S(1)} %fusion.4.packed, bf16[3,64,128]{2,1,0:T(8,128)(2,1)S(1)} %copy-done.1, s32[16,128]{1,0:T(8,128)S(1)} %copy-done.5, bf16[272,128]{1,0:T(8,128)(2,1)S(1)} %collective-permute-done.near, ...), custom_call_target="tpu_custom_call" | custom-call | tf_op jit(solution)/shard_map/pallas_call | solution.py:66
  95.4 0.0 all-to-all-done.3.arrived
  95.4 0.7 shard_map.136
  (7 shorter events, 0.0 us)
Async XLA Ops:
  0.6 90.8 %copy-start.1 = (bf16[3,64,128]{2,1,0:T(8,128)(2,1)S(1)}, bf16[3,64,128]{2,1,0:T(8,128)(2,1)}, u32[]{:S(2)}) copy-start(bf16[3,64,128]{2,1,0:T(8,128)(2,1)} %vec.3) | copy-start | bytes 147460
  0.6 90.8 %copy-start.4 = (bf16[20,192]{1,0:T(8,128)(2,1)S(1)}, bf16[20,192]{1,0:T(8,128)(2,1)}, u32[]{:S(2)}) copy-start(bf16[20,192]{1,0:T(8,128)(2,1)} %radial_weight.1) | copy-start | bytes 23044
  0.7 90.8 %copy-start.2 = (bf16[64,192]{1,0:T(8,128)(2,1)S(1)}, bf16[64,192]{1,0:T(8,128)(2,1)}, u32[]{:S(2)}) copy-start(bf16[64,192]{1,0:T(8,128)(2,1)} %message_weight.1) | copy-start | bytes 73732
  0.7 90.8 %copy-start.7 = (f32[64]{0:T(128)S(1)}, f32[64]{0:T(128)}, u32[]{:S(2)}) copy-start(f32[64]{0:T(128)} %param.20) | copy-start | bytes 772
  0.7 90.8 %copy-start.3 = (bf16[64,64]{1,0:T(8,128)(2,1)S(1)}, bf16[64,64]{1,0:T(8,128)(2,1)}, u32[]{:S(2)}) copy-start(bf16[64,64]{1,0:T(8,128)(2,1)} %node_weight.1) | copy-start | bytes 24580
  0.7 90.8 %copy-start.5 = (s32[16,128]{1,0:T(8,128)S(1)}, s32[16,128]{1,0:T(8,128)}, u32[]{:S(2)}) copy-start(s32[16,128]{1,0:T(8,128)} %ids.1) | copy-start | bytes 24580
  2.5 23.5 %all-to-all-start = ((bf16[32,80,128]{2,1,0:T(8,128)(2,1)}), bf16[32,80,128]{2,1,0:T(8,128)(2,1)S(1)}, u32[]{:S(2)}, u32[]{:S(2)}) async-start(bf16[32,80,128]{2,1,0:T(8,128)(2,1)} %broadcast_in_dim.3), calls=%async_computation | async-start | bytes 1310720 | tf_op jit(solution)/shard_map/all_to_all | solution.py:229
  13.6 0.8 copy-start
  14.4 0.7 copy-start.6
  56.9 15.4 %all-to-all-start.2 = ((bf16[16,16,128]{2,1,0:T(8,128)(2,1)}), bf16[16,16,128]{2,1,0:T(8,128)(2,1)S(1)}, u32[]{:S(2)}, u32[]{:S(2)}) async-start(bf16[16,16,128]{2,1,0:T(8,128)(2,1)} %get-tuple-element.14), calls=%async_computation.2 | async-start | bytes 131072 | tf_op jit(solution)/shard_map/all_to_all | solution.py:229
  60.7 4.7 %collective-permute-start = (bf16[272,128]{1,0:T(8,128)(2,1)S(1)}, bf16[272,128]{1,0:T(8,128)(2,1)S(1)}, u32[]{:S(2)}, u32[]{:S(2)}) collective-permute-start(bf16[272,128]{1,0:T(8,128)(2,1)S(1)} %get-tuple-element.16), channel_id=1, source_target_pairs={{0,1},{1,0},{2,3},{3,2},{4,5},{5,4},{6,7},{7,6},{8,9},{9,8},{10,11... | collective-permute-start | bytes 208904 | tf_op jit(solution)/shard_map/ppermute | solution.py:234
  75.7 19.7 %all-to-all-start.3 = ((bf16[32,64,128]{2,1,0:T(8,128)(2,1)}), bf16[32,64,128]{2,1,0:T(8,128)(2,1)S(1)}, u32[]{:S(2)}, u32[]{:S(2)}) async-start(bf16[32,64,128]{2,1,0:T(8,128)(2,1)} %shard_map.134.messages), calls=%async_computation.3 | async-start | bytes 1048576 | tf_op jit(solution)/shard_map/all_to_all | solution.py:229
  82.3 9.1 %collective-permute-start.1 = (bf16[272,128]{1,0:T(8,128)(2,1)S(1)}, bf16[272,128]{1,0:T(8,128)(2,1)S(1)}, u32[]{:S(2)}, u32[]{:S(2)}) collective-permute-start(bf16[272,128]{1,0:T(8,128)(2,1)S(1)} %get-tuple-element.17), channel_id=1, source_target_pairs={{1,2},{2,1},{3,4},{4,3},{5,6},{6,5},{7,8},{8,7},{9,10},{10,9},{11,... | collective-permute-start | bytes 208904 | tf_op jit(solution)/shard_map/ppermute | solution.py:234

commit v7 on v5

--- a/solution.py
+++ b/solution.py
@@ -14,6 +14,7 @@
 ATOM = 128
 KDEV = 256
 PLANE = 32
+SAME = 16
 DEPTH = 16
 SLABS = 512
 KVEC = 8192
@@ -22,7 +23,7 @@
 HALO_ROWS = 272
 GROUP = 8
 
-plane_axes = ("yh", "yl", "x", "c")
+same_axes = ("yh", "yl", "x")
 kb_axes = ("yl", "x", "c")
 all_axes = ("yh", "z", "yl", "x", "c")
 
@@ -85,41 +86,44 @@
     return pieces[0:3] + pieces[3:6] + pieces[6:9]
 
 
-def halo_kernel(row, packed, vec, halo, after, out):
+def halo_kernel(core, packed, vec, halo, far, near):
     rows = jnp.concatenate([packed[...], vec[0], vec[1], vec[2]], axis=0)
     atom = lax.broadcasted_iota(jnp.int32, (ATOM, ATOM), 0)
-    chosen = jnp.where(atom == halo[pl.ds(row[0], 1), :], 1.0, 0.0).astype(jnp.bfloat16)
-    out[...] = dot(rows, chosen, ((1,), (0,))).astype(jnp.bfloat16)
-
-
-def table_kernel(got, lattice, far, own_filter, table, partial, columns, total):
+    for row, out in ((1 - core[0], far), (core[0], near)):
+        chosen = jnp.where(atom == halo[pl.ds(row, 1), :], 1.0, 0.0).astype(jnp.bfloat16)
+        out[...] = dot(rows, chosen, ((1,), (0,))).astype(jnp.bfloat16)
+
+
+def table_kernel(own, other, lattice, far, own_filter, table, partial, columns, total):
     turned = lattice[...].T
     for i in range(3):
         columns[i] = jnp.broadcast_to(turned[:, i : i + 1], (KDEV, ATOM))
     total[...] = jnp.zeros_like(total)
 
-    @pl.loop(0, PLANE // GROUP)
-    def _(step):
-        for pair in range(0, GROUP, 2):
-            first = step * GROUP + pair
-            both = jnp.concatenate([got[first], got[first + 1]], axis=1)
-            pos = summed(both[F:].astype(jnp.float32))
-            at = pl.ds(pl.multiple_of(first * ATOM, 2 * ATOM), 2 * ATOM)
-            for k in range(0, KDEV, 64):
-                rows = slice(k, k + 64)
-                halves = []
-                for lanes in (slice(0, ATOM), slice(ATOM, 2 * ATOM)):
-                    halves.append(
-                        (columns[0, rows] * pos[0:1, lanes] + columns[1, rows] * pos[1:2, lanes])
-                        + columns[2, rows] * pos[2:3, lanes]
-                    )
-                cosines, sines = cosine_and_sine(jnp.concatenate(halves, axis=1))
-                cosines, sines = cosines.astype(jnp.bfloat16), sines.astype(jnp.bfloat16)
-                table[k : k + 64, at] = cosines
-                table[KDEV + k : KDEV + k + 64, at] = sines
-                sums = dot(jnp.concatenate([cosines, sines], axis=0), both[:F], ((1,), (1,)))
-                total[k : k + 64] += sums[:64]
-                total[KDEV + k : KDEV + k + 64] += sums[64:]
+    for part, got in enumerate((own, other)):
+
+        @pl.loop(0, SAME // GROUP)
+        def _(step):
+            for pair in range(0, GROUP, 2):
+                first = step * GROUP + pair
+                both = jnp.concatenate([got[first], got[first + 1]], axis=1)
+                pos = summed(both[F:].astype(jnp.float32))
+                at = pl.ds(pl.multiple_of((part * SAME + first) * ATOM, 2 * ATOM), 2 * ATOM)
+                for k in range(0, KDEV, 64):
+                    rows = slice(k, k + 64)
+                    halves = []
+                    for lanes in (slice(0, ATOM), slice(ATOM, 2 * ATOM)):
+                        halves.append(
+                            (columns[0, rows] * pos[0:1, lanes] + columns[1, rows] * pos[1:2, lanes])
+                            + columns[2, rows] * pos[2:3, lanes]
+                        )
+                    cosines, sines = cosine_and_sine(jnp.concatenate(halves, axis=1))
+                    cosines, sines = cosines.astype(jnp.bfloat16), sines.astype(jnp.bfloat16)
+                    table[k : k + 64, at] = cosines
+                    table[KDEV + k : KDEV + k + 64, at] = sines
+                    sums = dot(jnp.concatenate([cosines, sines], axis=0), both[:F], ((1,), (1,)))
+                    total[k : k + 64] += sums[:64]
+                    total[KDEV + k : KDEV + k + 64] += sums[64:]
 
     partial[...] = jnp.concatenate([total[:KDEV], total[KDEV:]], axis=1).astype(jnp.bfloat16)
 
@@ -133,25 +137,40 @@
         out[i] = total
 
 
-def project_kernel(got, own_filter, table, out):
+def filtered_sums(got, own_filter):
     own, weight = own_filter[:, :KDEV], own_filter[:, KDEV:].astype(jnp.bfloat16)
     total = [dot(weight, got[:, part * F : (part + 1) * F], ((0,), (1,))) for part in range(2)]
-    filtered = jnp.concatenate([own * total[0], own * total[1]], axis=1).astype(jnp.bfloat16)
-    for first in range(0, PLANE, 8):
-        message = dot(filtered, table[:, first * ATOM : (first + 8) * ATOM], ((1,), (0,))).astype(jnp.bfloat16)
+    return jnp.concatenate([own * total[0], own * total[1]], axis=1).astype(jnp.bfloat16)
+
+
+def project_other_kernel(got, own_filter, table, near, out):
+    filtered = filtered_sums(got, own_filter)
+    for first in range(0, SAME, 8):
+        atoms = slice((SAME + first) * ATOM, (SAME + first + 8) * ATOM)
+        message = dot(filtered, table[:, atoms], ((1,), (0,))).astype(jnp.bfloat16)
         for p in range(8):
-            out[first + p] = message[:, p * ATOM : (p + 1) * ATOM]
+            out[(first + p) * F : (first + p + 1) * F] = message[:, p * ATOM : (p + 1) * ATOM]
+    out[SAME * F :] = near[...]
+
+
+def project_own_kernel(got, own_filter, table, received, out):
+    filtered = filtered_sums(got, own_filter)
+    for first in range(0, SAME, 8):
+        message = dot(filtered, table[:, first * ATOM : (first + 8) * ATOM], ((1,), (0,)))
+        for p in range(first, first + 8):
+            there = received[p * F : (p + 1) * F].astype(jnp.float32)
+            out[p] = (message[:, (p - first) * ATOM : (p - first + 1) * ATOM] + there).astype(jnp.bfloat16)
 
 
 def finish_kernel(arrived, scalar, out):
     total = arrived[0].astype(jnp.float32)
-    for i in range(1, PLANE):
+    for i in range(1, SAME):
         total = total + arrived[i].astype(jnp.float32)
     out[...] = (scalar[...] + total).astype(jnp.bfloat16)
 
 
 def short_kernel(
-    core, packed, vec, ids, near, far, node_weight, bias, message_weight, radial_weight,
+    core, packed, vec, ids, near, far, node_weight, bias, message_weight, radial_weight, messages,
     scalar_out, vector_out, feats, ext, chosen, filters, directions,
 ):
     pos = summed(packed[F:].astype(jnp.float32))
@@ -160,10 +179,10 @@
     ext[384:, :ATOM] = packed[F:]
     near_at = pl.ds(pl.multiple_of((2 - core[0]) * ATOM, ATOM), ATOM)
     far_at = pl.ds(pl.multiple_of((1 + core[0]) * ATOM, ATOM), ATOM)
-    for side, at in ((near, near_at), (far, far_at)):
-        feats[:, at] = side[:F]
-        ext[192:384, at] = side[PACK:]
-        ext[384:, at] = side[F:PACK]
+    for side, start, at in ((near, SAME * F, near_at), (far, 0, far_at)):
+        feats[:, at] = side[start : start + F]
+        ext[192:384, at] = side[start + PACK : start + HALO_ROWS]
+        ext[384:, at] = side[start + F : start + PACK]
     bias_column = jnp.broadcast_to(bias[...], (8, F)).T[:, 0:1]
     hidden = dot(node_weight[...], feats[...], ((0,), (0,))) + bias_column
     hidden = (hidden / (1.0 + jnp.exp(-hidden))).astype(jnp.bfloat16)
@@ -223,38 +242,42 @@
     half_at = lax.axis_index("yh") * KDEV
     k_at = lax.axis_index(kb_axes) * 2 * KDEV + half_at
     packed = packed_rows(features, positions)
-    got = exchanged(jnp.broadcast_to(packed, (PLANE, PACK, ATOM)), plane_axes)
+    own = exchanged(jnp.broadcast_to(packed, (SAME, PACK, ATOM)), same_axes)
+    other = swapped(own, 0)
     own_lattice = jnp.pad(lax.dynamic_slice_in_dim(lattice, k_at, KDEV, 1).astype(f32), ((0, 5), (0, 0)))
     own_filter = jnp.pad(lax.dynamic_slice_in_dim(kspace_filter, half_at, KDEV, 1) * norm_scale, ((0, 0), (0, F)))
     own_filter = own_filter + jnp.pad(ewald_weight.astype(f32), ((0, 0), (KDEV, 0)))
     core = lax.axis_index("c").astype(jnp.int32).reshape(1)
     halo = shape((HALO_ROWS, ATOM), bf16)
-    far = call(
-        halo_kernel, [SM, VM, VM, VM, ANY], halo, 1 - core, packed, vectors, halo_lists, own_lattice
-    )
+    far, near = call(halo_kernel, [SM, VM, VM, VM], (halo, halo), core, packed, vectors, halo_lists)
     far = swapped(far, 1)
     table, partial = call(
         table_kernel,
-        [VM, VM, ANY, ANY],
+        [VM, VM, VM, ANY, ANY],
         (shape((2 * KDEV, PLANE * ATOM), bf16), shape((KDEV, 2 * F), bf16)),
-        got, own_lattice, far, own_filter,
+        own, other, own_lattice, far, own_filter,
         scratch=[VM((3, KDEV, ATOM), f32), VM((2 * KDEV, F), f32)],
     )
     arrived = exchanged(partial.reshape(DEPTH, KDEV // DEPTH, 2 * F), "z")
     owned = call(sum_kernel, [VM], shape((DEPTH, KDEV // DEPTH, 2 * F), bf16), arrived)
     totals = exchanged(owned, "z").reshape(KDEV, 2 * F)
+    for_other = call(
+        project_other_kernel,
+        [VM] * 4,
+        shape((SAME * F + HALO_ROWS, ATOM), bf16),
+        totals, own_filter, table, near,
+    )
+    received = swapped(for_other, 0)
     messages = call(
-        project_kernel, [VM] * 3, shape((PLANE, F, ATOM), bf16), totals, own_filter, table
-    )
-    returned = exchanged(messages, plane_axes)
-    near = call(halo_kernel, [SM, VM, VM, VM, ANY], halo, core, packed, vectors, halo_lists, messages)
-    near = swapped(near, 0)
+        project_own_kernel, [VM] * 4, shape((SAME, F, ATOM), bf16), totals, own_filter, table, received
+    )
+    returned = exchanged(messages, same_axes)
     scalar, new_vectors = call(
         short_kernel,
-        [SM] + [VM] * 9,
+        [SM] + [VM] * 9 + [ANY],
         (shape((F, ATOM), f32), shape((3, F, ATOM), bf16)),
-        core, packed, vectors, neighbours, near, far,
-        node_weight, node_bias.reshape(1, F), message_weight, radial_weight,
+        core, packed, vectors, neighbours, received, far,
+        node_weight, node_bias.reshape(1, F), message_weight, radial_weight, messages,
         scratch=[
             VM((F, 3 * ATOM), bf16),
             VM((400, 3 * ATOM), bf16),

time: 92.3 us -> 91.6 us (level)
  starting transfers between devices: 23 us -> 33.1 us
  blocking collectives: 40 us -> 34.4 us
  waiting for transfers between devices: 10.7 us -> 5.69 us
    ppermute x2 -> x3, starting transfers between devices: 5.69 us -> 21.9 us  [swapped(): return lax.ppermute(x, all_axes, pairs)]
    all_to_all x2, starting transfers between devices: 17.3 us -> 11.1 us  [exchanged(): return lax.all_to_all(x, axes, split_axis=0, concat_axis=0, tiled=True)]
    all_to_all x2, blocking collectives: 40 us -> 34.4 us  [exchanged(): return lax.all_to_all(x, axes, split_axis=0, concat_axis=0, tiled=True)]
    ppermute x2 -> x3, waiting for transfers between devices: 3.95 us -> 1.24 us  [swapped(): return lax.ppermute(x, all_axes, pairs)]
    all_to_all x2, waiting for transfers between devices: 6.78 us -> 4.45 us  [exchanged(): return lax.all_to_all(x, axes, split_axis=0, concat_axis=0, tiled=True)]
  transfers between devices with their start and end apart: 4 -> 5, of which waited for: 4 -> 2; matrix products, arithmetic and copies ran while one was open for 2% -> 2% of each run, Pallas kernels for 5% -> 5%
where the time goes in v7:
time: 91.6 us; the launch traced here: 90.9 us
  blocking collectives  34.4 us (38%)
  starting transfers between devices  33.1 us (36%)
  Pallas kernels  11.6 us (13%)
  waiting for transfers between devices  5.69 us (6%)
  other arithmetic  3.07 us (3%)
  local copies, waits for them, and re-layouts  2.27 us (2%)
    all_to_all x2, blocking collectives, exchanged(): return lax.all_to_all(x, axes, split_axis=0, concat_axis=0, tiled=True)  34.4 us
    ppermute x3, starting transfers between devices, swapped(): return lax.ppermute(x, all_axes, pairs)  21.9 us
    pallas_call x7, Pallas kernels, call(): pl.pallas_call(kernel, out_shape=outs, in_specs=[pl.BlockSpec(memory_spac...  11.6 us
    all_to_all x2, starting transfers between devices, exchanged(): return lax.all_to_all(x, axes, split_axis=0, concat_axis=0, tiled=True)  11.1 us
    all_to_all x2, waiting for transfers between devices, exchanged(): return lax.all_to_all(x, axes, split_axis=0, concat_axis=0, tiled=True)  4.45 us
  transfers between devices with their start and end apart: 5, of which 2 were waited for; matrix products, arithmetic and copies ran while one was open for 2% of the time, Pallas kernels for 5%

profile of v7, /device:TPU:1, one launch (start us, length us, event | category | flops | bytes accessed | tf_op | source)
XLA Modules:
  0.0 90.9 jit_solution(2479096619990029145)
XLA Ops:
  0.6 0.8 fusion.4.packed
  1.4 0.8 broadcast_in_dim.3
  2.2 7.6 %all-to-all-start = ((bf16[16,80,128]{2,1,0:T(8,128)(2,1)}), bf16[16,80,128]{2,1,0:T(8,128)(2,1)S(1)}, u32[]{:S(2)}, u32[]{:S(2)}) async-start(bf16[16,80,128]{2,1,0:T(8,128)(2,1)} %broadcast_in_dim.3), calls=%async_computation | async-start | bytes 655360 | tf_op jit(solution)/shard_map/all_to_all | solution.py:228
  9.8 0.0 copy-start
  9.8 0.8 copy-done
  10.6 0.7 copy-done.6
  11.3 0.2 shard_map.131
  11.5 6.1 %collective-permute-start.1 = (bf16[272,128]{1,0:T(8,128)(2,1)S(1)}, bf16[272,128]{1,0:T(8,128)(2,1)S(1)}, u32[]{:S(2)}, u32[]{:S(2)}) collective-permute-start(bf16[272,128]{1,0:T(8,128)(2,1)S(1)} %get-tuple-element.8), channel_id=1, source_target_pairs={{1,2},{2,1},{3,4},{4,3},{5,6},{6,5},{7,8},{8,7},{9,10},{10,9},{11,... | collective-permute-start | bytes 208904 | tf_op jit(solution)/shard_map/ppermute | solution.py:233
  17.7 0.0 all-to-all-done.own
  17.7 11.7 %collective-permute-start = (bf16[16,80,128]{2,1,0:T(8,128)(2,1)S(1)}, bf16[16,80,128]{2,1,0:T(8,128)(2,1)S(1)}, u32[]{:S(2)}, u32[]{:S(2)}) collective-permute-start(bf16[16,80,128]{2,1,0:T(8,128)(2,1)S(1)} %all-to-all-done.own), channel_id=1, source_target_pairs={{0,1},{1,0},{2,3},{3,2},{4,5},{5,4},{6,7},{7,6},{8,9},{9,8},{10,11... | collective-permute-start | bytes 983048 | tf_op jit(solution)/shard_map/ppermute | solution.py:233
  29.4 0.7 dynamic-slice_convert_fusion
  30.1 0.8 dynamic-slice_multiply_fusion
  30.9 0.7 convert_add_fusion.own_filter
  31.6 0.0 collective-permute-done.1.far
  31.6 0.0 collective-permute-done.other
  31.7 4.8 %shard_map.132 = (bf16[512,4096]{1,0:T(8,128)(2,1)S(1)}, bf16[256,128]{1,0:T(8,128)(2,1)S(1)}) custom-call(bf16[16,80,128]{2,1,0:T(8,128)(2,1)S(1)} %all-to-all-done.own, bf16[16,80,128]{2,1,0:T(8,128)(2,1)S(1)} %collective-permute-done.other, f32[8,256]{1,0:T(8,128)S(1)} %pad.35.lattice, bf16[272,128]{1,0:T(8,128)(2,1)S(1)} %collective-permute-done.1.far, ...), custom_call_target="tpu_custom_call" | custom-call | tf_op jit(solution)/shard_map/pallas_call | solution.py:66
  36.5 19.0 %all_to_all.20.arrived = bf16[16,16,128]{2,1,0:T(8,128)(2,1)S(1)} all-to-all(bf16[16,16,128]{2,1,0:T(8,128)(2,1)S(1)} %bitcast.6), channel_id=1, replica_groups=mesh['yh'=2,'z'=16,'yl'=2,'x'=4,'c'=2] {'z'}, dimensions={0} | all-to-all | bytes 131072 | tf_op jit(solution)/shard_map/all_to_all | solution.py:228
  55.5 15.3 %all_to_all.21 = bf16[16,16,128]{2,1,0:T(8,128)(2,1)S(1)} all-to-all(bf16[16,16,128]{2,1,0:T(8,128)(2,1)S(1)} %shard_map.133), channel_id=1, replica_groups=mesh['yh'=2,'z'=16,'yl'=2,'x'=4,'c'=2] {'z'}, dimensions={0} | all-to-all | bytes 131072 | tf_op jit(solution)/shard_map/all_to_all | solution.py:228
  70.9 0.0 copy-start.5
  70.9 0.0 copy-start.7
  70.9 0.6 shard_map.134
  71.6 4.1 %collective-permute-start.2 = (bf16[1296,128]{1,0:T(8,128)(2,1)S(1)}, bf16[1296,128]{1,0:T(8,128)(2,1)S(1)}, u32[]{:S(2)}, u32[]{:S(2)}) collective-permute-start(bf16[1296,128]{1,0:T(8,128)(2,1)S(1)} %shard_map.134), channel_id=1, source_target_pairs={{0,1},{1,0},{2,3},{3,2},{4,5},{5,4},{6,7},{7,6},{8,9},{9,8},{10,11... | collective-permute-start | bytes 995336 | tf_op jit(solution)/shard_map/ppermute | solution.py:233
  75.7 1.2 %collective-permute-done.2.received.near = bf16[1296,128]{1,0:T(8,128)(2,1)S(1)} collective-permute-done((bf16[1296,128]{1,0:T(8,128)(2,1)S(1)}, bf16[1296,128]{1,0:T(8,128)(2,1)S(1)}, u32[]{:S(2)}, u32[]{:S(2)}) %collective-permute-start.2) | collective-permute-done | bytes 331808 | tf_op jit(solution)/shard_map/ppermute | solution.py:233
  77.0 1.3 %shard_map.135.messages = bf16[16,64,128]{2,1,0:T(8,128)(2,1)} custom-call(bf16[256,128]{1,0:T(8,128)(2,1)S(1)} %bitcast.5, f32[64,320]{1,0:T(8,128)S(1)} %convert_add_fusion.own_filter, bf16[512,4096]{1,0:T(8,128)(2,1)S(1)} %get-tuple-element.10.table, bf16[1296,128]{1,0:T(8,128)(2,1)S(1)} %collective-permute-done.2.received.near), custom_call_target="tpu_custom_call" | custom-call | tf_op jit(solution)/shard_map/pallas_call | solution.py:66
  78.3 3.5 %all-to-all-start.3 = ((bf16[16,64,128]{2,1,0:T(8,128)(2,1)}), bf16[16,64,128]{2,1,0:T(8,128)(2,1)S(1)}, u32[]{:S(2)}, u32[]{:S(2)}) async-start(bf16[16,64,128]{2,1,0:T(8,128)(2,1)} %shard_map.135.messages), calls=%async_computation.3 | async-start | bytes 524288 | tf_op jit(solution)/shard_map/all_to_all | solution.py:228
  81.8 0.0 copy-done.1
  81.8 0.0 copy-done.2
  81.9 0.0 copy-done.3
  81.9 0.0 copy-done.4
  81.9 3.9 %shard_map.136 = (f32[64,128]{1,0:T(8,128)S(1)}, bf16[3,64,128]{2,1,0:T(8,128)(2,1)}) custom-call(s32[1]{0:T(128)} %bitcast.core, bf16[80,128]{1,0:T(8,128)(2,1)S(1)} %fusion.4.packed, bf16[3,64,128]{2,1,0:T(8,128)(2,1)S(1)} %copy-done.1, s32[16,128]{1,0:T(8,128)S(1)} %copy-done.5, bf16[1296,128]{1,0:T(8,128)(2,1)S(1)} %collective-permute-done.2.received.near, ...), custom_call_target="tpu_custom_call" | custom-call | tf_op jit(solution)/shard_map/pallas_call | solution.py:66
  85.8 4.4 %all-to-all-done.3.arrived = bf16[16,64,128]{2,1,0:T(8,128)(2,1)S(1)} async-done(((bf16[16,64,128]{2,1,0:T(8,128)(2,1)}), bf16[16,64,128]{2,1,0:T(8,128)(2,1)S(1)}, u32[]{:S(2)}, u32[]{:S(2)}) %all-to-all-start.3) | async-done | bytes 262176 | tf_op jit(solution)/shard_map/all_to_all | solution.py:228
  90.2 0.6 shard_map.137
  (9 shorter events, 0.0 us)
Async XLA Ops:
  2.2 15.5 %all-to-all-start = ((bf16[16,80,128]{2,1,0:T(8,128)(2,1)}), bf16[16,80,128]{2,1,0:T(8,128)(2,1)S(1)}, u32[]{:S(2)}, u32[]{:S(2)}) async-start(bf16[16,80,128]{2,1,0:T(8,128)(2,1)} %broadcast_in_dim.3), calls=%async_computation | async-start | bytes 655360 | tf_op jit(solution)/shard_map/all_to_all | solution.py:228
  9.8 0.8 copy-start
  10.6 0.7 copy-start.6
  11.5 20.1 %collective-permute-start.1 = (bf16[272,128]{1,0:T(8,128)(2,1)S(1)}, bf16[272,128]{1,0:T(8,128)(2,1)S(1)}, u32[]{:S(2)}, u32[]{:S(2)}) collective-permute-start(bf16[272,128]{1,0:T(8,128)(2,1)S(1)} %get-tuple-element.8), channel_id=1, source_target_pairs={{1,2},{2,1},{3,4},{4,3},{5,6},{6,5},{7,8},{8,7},{9,10},{10,9},{11,... | collective-permute-start | bytes 208904 | tf_op jit(solution)/shard_map/ppermute | solution.py:233
  17.7 13.9 %collective-permute-start = (bf16[16,80,128]{2,1,0:T(8,128)(2,1)S(1)}, bf16[16,80,128]{2,1,0:T(8,128)(2,1)S(1)}, u32[]{:S(2)}, u32[]{:S(2)}) collective-permute-start(bf16[16,80,128]{2,1,0:T(8,128)(2,1)S(1)} %all-to-all-done.own), channel_id=1, source_target_pairs={{0,1},{1,0},{2,3},{3,2},{4,5},{5,4},{6,7},{7,6},{8,9},{9,8},{10,11... | collective-permute-start | bytes 983048 | tf_op jit(solution)/shard_map/ppermute | solution.py:233
  70.9 11.0 %copy-start.1 = (bf16[3,64,128]{2,1,0:T(8,128)(2,1)S(1)}, bf16[3,64,128]{2,1,0:T(8,128)(2,1)}, u32[]{:S(2)}) copy-start(bf16[3,64,128]{2,1,0:T(8,128)(2,1)} %vec.3) | copy-start | bytes 147460
  70.9 11.0 %copy-start.2 = (bf16[64,192]{1,0:T(8,128)(2,1)S(1)}, bf16[64,192]{1,0:T(8,128)(2,1)}, u32[]{:S(2)}) copy-start(bf16[64,192]{1,0:T(8,128)(2,1)} %message_weight.1) | copy-start | bytes 73732
  70.9 11.0 %copy-start.3 = (bf16[64,64]{1,0:T(8,128)(2,1)S(1)}, bf16[64,64]{1,0:T(8,128)(2,1)}, u32[]{:S(2)}) copy-start(bf16[64,64]{1,0:T(8,128)(2,1)} %node_weight.1) | copy-start | bytes 24580
  70.9 11.0 %copy-start.4 = (bf16[20,192]{1,0:T(8,128)(2,1)S(1)}, bf16[20,192]{1,0:T(8,128)(2,1)}, u32[]{:S(2)}) copy-start(bf16[20,192]{1,0:T(8,128)(2,1)} %radial_weight.1) | copy-start | bytes 23044
  70.9 11.0 %copy-start.5 = (s32[16,128]{1,0:T(8,128)S(1)}, s32[16,128]{1,0:T(8,128)}, u32[]{:S(2)}) copy-start(s32[16,128]{1,0:T(8,128)} %ids.1) | copy-start | bytes 24580
  70.9 11.0 %copy-start.7 = (f32[64]{0:T(128)S(1)}, f32[64]{0:T(128)}, u32[]{:S(2)}) copy-start(f32[64]{0:T(128)} %param.20) | copy-start | bytes 772
  71.6 5.4 %collective-permute-start.2 = (bf16[1296,128]{1,0:T(8,128)(2,1)S(1)}, bf16[1296,128]{1,0:T(8,128)(2,1)S(1)}, u32[]{:S(2)}, u32[]{:S(2)}) collective-permute-start(bf16[1296,128]{1,0:T(8,128)(2,1)S(1)} %shard_map.134), channel_id=1, source_target_pairs={{0,1},{1,0},{2,3},{3,2},{4,5},{5,4},{6,7},{7,6},{8,9},{9,8},{10,11... | collective-permute-start | bytes 995336 | tf_op jit(solution)/shard_map/ppermute | solution.py:233
  78.3 11.9 %all-to-all-start.3 = ((bf16[16,64,128]{2,1,0:T(8,128)(2,1)}), bf16[16,64,128]{2,1,0:T(8,128)(2,1)S(1)}, u32[]{:S(2)}, u32[]{:S(2)}) async-start(bf16[16,64,128]{2,1,0:T(8,128)(2,1)} %shard_map.135.messages), calls=%async_computation.3 | async-start | bytes 524288 | tf_op jit(solution)/shard_map/all_to_all | solution.py:228

commit v8 on v7

--- a/solution.py
+++ b/solution.py
@@ -21,7 +21,8 @@
 ATOMS = 65536
 PACK = 80
 HALO_ROWS = 272
-GROUP = 8
+GROUP = 4
+SPARE = 22
 
 same_axes = ("yh", "yl", "x")
 kb_axes = ("yl", "x", "c")
@@ -62,15 +63,17 @@
 VM, SM, ANY = pltpu.VMEM, pltpu.SMEM, pl.ANY
 
 
-def call(kernel, places, outs, *operands, scratch=()):
+def call(kernel, places, outs, *operands, scratch=(), far_outs=(), flops=0):
     return pl.pallas_call(
         kernel,
         out_shape=outs,
         in_specs=[pl.BlockSpec(memory_space=place) for place in places],
-        out_specs=jax.tree.map(lambda _: pl.BlockSpec(memory_space=VM), outs),
+        out_specs=tuple(pl.BlockSpec(memory_space=ANY if i in far_outs else VM) for i in range(len(outs)))
+        if isinstance(outs, tuple)
+        else pl.BlockSpec(memory_space=VM),
         scratch_shapes=list(scratch),
         compiler_params=pltpu.CompilerParams(vmem_limit_bytes=VMEM_LIMIT),
-        cost_estimate=pl.CostEstimate(flops=0, bytes_accessed=0, transcendentals=0),
+        cost_estimate=pl.CostEstimate(flops=flops, bytes_accessed=0, transcendentals=0),
     )(*operands)
 
 
@@ -86,7 +89,7 @@
     return pieces[0:3] + pieces[3:6] + pieces[6:9]
 
 
-def halo_kernel(core, packed, vec, halo, far, near):
+def halo_kernel(core, packed, vec, halo, after, far, near):
     rows = jnp.concatenate([packed[...], vec[0], vec[1], vec[2]], axis=0)
     atom = lax.broadcasted_iota(jnp.int32, (ATOM, ATOM), 0)
     for row, out in ((1 - core[0], far), (core[0], near)):
@@ -94,41 +97,63 @@
         out[...] = dot(rows, chosen, ((1,), (0,))).astype(jnp.bfloat16)
 
 
-def table_kernel(own, other, lattice, far, own_filter, table, partial, columns, total):
+def make_columns(lattice, columns):
     turned = lattice[...].T
     for i in range(3):
         columns[i] = jnp.broadcast_to(turned[:, i : i + 1], (KDEV, ATOM))
+
+
+def add_atoms(got, first, columns, table, total):
+    for pair in range(0, GROUP, 2):
+        both = jnp.concatenate([got[first + pair], got[first + pair + 1]], axis=1)
+        pos = summed(both[F:].astype(jnp.float32))
+        at = pl.ds(pl.multiple_of((first + pair) * ATOM, 2 * ATOM), 2 * ATOM)
+        for k in range(0, KDEV, 64):
+            rows = slice(k, k + 64)
+            halves = []
+            for lanes in (slice(0, ATOM), slice(ATOM, 2 * ATOM)):
+                halves.append(
+                    (columns[0, rows] * pos[0:1, lanes] + columns[1, rows] * pos[1:2, lanes])
+                    + columns[2, rows] * pos[2:3, lanes]
+                )
+            cosines, sines = cosine_and_sine(jnp.concatenate(halves, axis=1))
+            cosines, sines = cosines.astype(jnp.bfloat16), sines.astype(jnp.bfloat16)
+            table[k : k + 64, at] = cosines
+            table[KDEV + k : KDEV + k + 64, at] = sines
+            sums = dot(jnp.concatenate([cosines, sines], axis=0), both[:F], ((1,), (1,)))
+            total[k : k + 64] += sums[:64]
+            total[KDEV + k : KDEV + k + 64] += sums[64:]
+
+
+def own_table_kernel(got, lattice, own_filter, table_at, total, table, columns, done):
+    make_columns(lattice, columns)
     total[...] = jnp.zeros_like(total)
 
-    for part, got in enumerate((own, other)):
-
-        @pl.loop(0, SAME // GROUP)
-        def _(step):
-            for pair in range(0, GROUP, 2):
-                first = step * GROUP + pair
-                both = jnp.concatenate([got[first], got[first + 1]], axis=1)
-                pos = summed(both[F:].astype(jnp.float32))
-                at = pl.ds(pl.multiple_of((part * SAME + first) * ATOM, 2 * ATOM), 2 * ATOM)
-                for k in range(0, KDEV, 64):
-                    rows = slice(k, k + 64)
-                    halves = []
-                    for lanes in (slice(0, ATOM), slice(ATOM, 2 * ATOM)):
-                        halves.append(
-                            (columns[0, rows] * pos[0:1, lanes] + columns[1, rows] * pos[1:2, lanes])
-                            + columns[2, rows] * pos[2:3, lanes]
-                        )
-                    cosines, sines = cosine_and_sine(jnp.concatenate(halves, axis=1))
-                    cosines, sines = cosines.astype(jnp.bfloat16), sines.astype(jnp.bfloat16)
-                    table[k : k + 64, at] = cosines
-                    table[KDEV + k : KDEV + k + 64, at] = sines
-                    sums = dot(jnp.concatenate([cosines, sines], axis=0), both[:F], ((1,), (1,)))
-                    total[k : k + 64] += sums[:64]
-                    total[KDEV + k : KDEV + k + 64] += sums[64:]
+    def stored(step):
+        atoms = pl.ds(pl.multiple_of(step * GROUP * ATOM, GROUP * ATOM), GROUP * ATOM)
+        return pltpu.make_async_copy(table.at[:, atoms], table_at.at[0, :, atoms], done.at[step])
+
+    @pl.loop(0, SAME // GROUP)
+    def _(step):
+        add_atoms(got, step * GROUP, columns, table, total)
+        stored(step).start()
+
+    for step in range(SAME // GROUP):
+        stored(step).wait()
+
+
+def other_table_kernel(got, lattice, own_total, table, partial, columns, total):
+    make_columns(lattice, columns)
+    total[...] = own_total[...]
+
+    @pl.loop(0, SAME // GROUP)
+    def _(step):
+        add_atoms(got, step * GROUP, columns, table, total)
 
     partial[...] = jnp.concatenate([total[:KDEV], total[KDEV:]], axis=1).astype(jnp.bfloat16)
 
 
-def sum_kernel(arrived, out):
+def sum_kernel(arrived, far, out):
     total = arrived[0].astype(jnp.float32)
     for i in range(1, DEPTH):
         total = total + arrived[i].astype(jnp.float32)
@@ -146,18 +171,24 @@
 def project_other_kernel(got, own_filter, table, near, out):
     filtered = filtered_sums(got, own_filter)
     for first in range(0, SAME, 8):
-        atoms = slice((SAME + first) * ATOM, (SAME + first + 8) * ATOM)
-        message = dot(filtered, table[:, atoms], ((1,), (0,))).astype(jnp.bfloat16)
+        message = dot(filtered, table[:, first * ATOM : (first + 8) * ATOM], ((1,), (0,))).astype(jnp.bfloat16)
         for p in range(8):
             out[(first + p) * F : (first + p + 1) * F] = message[:, p * ATOM : (p + 1) * ATOM]
     out[SAME * F :] = near[...]
 
 
-def project_own_kernel(got, own_filter, table, received, out):
+def project_own_kernel(got, own_filter, table_at, received, out, table, done):
+    loads = []
+    for i, first in enumerate(range(0, SAME, 4)):
+        atoms = slice(first * ATOM, (first + 4) * ATOM)
+        loads.append(pltpu.make_async_copy(table_at.at[0, :, atoms], table.at[:, atoms], done.at[i]))
+    for load in loads:
+        load.start()
     filtered = filtered_sums(got, own_filter)
-    for first in range(0, SAME, 8):
-        message = dot(filtered, table[:, first * ATOM : (first + 8) * ATOM], ((1,), (0,)))
-        for p in range(first, first + 8):
+    for first, load in zip(range(0, SAME, 4), loads):
+        load.wait()
+        message = dot(filtered, table[:, first * ATOM : (first + 4) * ATOM], ((1,), (0,)))
+        for p in range(first, first + 4):
             there = received[p * F : (p + 1) * F].astype(jnp.float32)
             out[p] = (message[:, (p - first) * ATOM : (p - first + 1) * ATOM] + there).astype(jnp.bfloat16)
 
@@ -249,27 +280,46 @@
     own_filter = own_filter + jnp.pad(ewald_weight.astype(f32), ((0, 0), (KDEV, 0)))
     core = lax.axis_index("c").astype(jnp.int32).reshape(1)
     halo = shape((HALO_ROWS, ATOM), bf16)
-    far, near = call(halo_kernel, [SM, VM, VM, VM], (halo, halo), core, packed, vectors, halo_lists)
+    own_table, own_total = call(
+        own_table_kernel,
+        [VM, VM, ANY],
+        (shape((SPARE, 2 * KDEV, SAME * ATOM), bf16), shape((2 * KDEV, F), f32)),
+        own, own_lattice, own_filter,
+        scratch=[
+            VM((2 * KDEV, SAME * ATOM), bf16),
+            VM((3, KDEV, ATOM), f32),
+            pltpu.SemaphoreType.DMA((SAME // GROUP,)),
+        ],
+        far_outs=(0,),
+        flops=10**11,
+    )
+    other_table, partial = call(
+        other_table_kernel,
+        [VM] * 3,
+        (shape((2 * KDEV, SAME * ATOM), bf16), shape((KDEV, 2 * F), bf16)),
+        other, own_lattice, own_total,
+        scratch=[VM((3, KDEV, ATOM), f32), VM((2 * KDEV, F), f32)],
+    )
+    arrived = exchanged(partial.reshape(DEPTH, KDEV // DEPTH, 2 * F), "z")
+    far, near = call(
+        halo_kernel, [SM, VM, VM, VM, ANY], (halo, halo), core, packed, vectors, halo_lists, partial
+    )
     far = swapped(far, 1)
-    table, partial = call(
-        table_kernel,
-        [VM, VM, VM, ANY, ANY],
-        (shape((2 * KDEV, PLANE * ATOM), bf16), shape((KDEV, 2 * F), bf16)),
-        own, other, own_lattice, far, own_filter,
-        scratch=[VM((3, KDEV, ATOM), f32), VM((2 * KDEV, F), f32)],
-    )
-    arrived = exchanged(partial.reshape(DEPTH, KDEV // DEPTH, 2 * F), "z")
-    owned = call(sum_kernel, [VM], shape((DEPTH, KDEV // DEPTH, 2 * F), bf16), arrived)
+    owned = call(sum_kernel, [VM, ANY], shape((DEPTH, KDEV // DEPTH, 2 * F), bf16), arrived, far)
     totals = exchanged(owned, "z").reshape(KDEV, 2 * F)
     for_other = call(
         project_other_kernel,
         [VM] * 4,
         shape((SAME * F + HALO_ROWS, ATOM), bf16),
-        totals, own_filter, table, near,
+        totals, own_filter, other_table, near,
     )
     received = swapped(for_other, 0)
     messages = call(
-        project_own_kernel, [VM] * 4, shape((SAME, F, ATOM), bf16), totals, own_filter, table, received
+        project_own_kernel,
+        [VM, VM, ANY, VM],
+        shape((SAME, F, ATOM), bf16),
+        totals, own_filter, own_table, received,
+        scratch=[VM((2 * KDEV, SAME * ATOM), bf16), pltpu.SemaphoreType.DMA((SAME // 4,))],
     )
     returned = exchanged(messages, same_axes)
     scalar, new_vectors = call(

time: 91.6 us -> 98.9 us (1.080)
  blocking collectives: 34.4 us -> 17 us
  waiting for transfers between devices: 5.69 us -> 20.3 us
  starting transfers between devices: 33.1 us -> 41 us
  Pallas kernels: 11.6 us -> 15.2 us
  local copies, waits for them, and re-layouts: 2.27 us -> 0.82 us
    all_to_all x2 -> x1, blocking collectives: 34.4 us -> 17 us  [exchanged(): return lax.all_to_all(x, axes, split_axis=0, concat_axis=0, tiled=True)]
    all_to_all x2 -> x3, starting transfers between devices: 11.1 us -> 24.5 us  [exchanged(): return lax.all_to_all(x, axes, split_axis=0, concat_axis=0, tiled=True)]
    all_to_all x2 -> x3, waiting for transfers between devices: 4.45 us -> 15.5 us  [exchanged(): return lax.all_to_all(x, axes, split_axis=0, concat_axis=0, tiled=True)]
    ppermute x3, starting transfers between devices: 21.9 us -> 16.4 us  [swapped(): return lax.ppermute(x, all_axes, pairs)]
    pallas_call x7 -> x8, Pallas kernels: 11.6 us -> 15.2 us  [call(): pl.pallas_call(kernel, out_shape=outs, in_specs=[pl.BlockSpec(memory_spac...]
    ppermute x3, waiting for transfers between devices: 1.24 us -> 4.79 us  [swapped(): return lax.ppermute(x, all_axes, pairs)]
    unnamed x16 -> x14, local copies, waits for them, and re-layouts: 1.5 us -> 0.04 us
  transfers between devices with their start and end apart: 5 -> 6, of which waited for: 2 -> 5; matrix products, arithmetic and copies ran while one was open for 2% -> 2% of each run, Pallas kernels for 5% -> 8%
where the time goes in v8:
time: 98.9 us; the launch traced here: 98.3 us
  starting transfers between devices  41 us (41%)
  waiting for transfers between devices  20.3 us (21%)
  blocking collectives  17 us (17%)
  Pallas kernels  15.2 us (15%)
  other arithmetic  3.07 us (3%)
    all_to_all x3, starting transfers between devices, exchanged(): return lax.all_to_all(x, axes, split_axis=0, concat_axis=0, tiled=True)  24.5 us
    all_to_all x1, blocking collectives, exchanged(): return lax.all_to_all(x, axes, split_axis=0, concat_axis=0, tiled=True)  17 us
    ppermute x3, starting transfers between devices, swapped(): return lax.ppermute(x, all_axes, pairs)  16.4 us
    all_to_all x3, waiting for transfers between devices, exchanged(): return lax.all_to_all(x, axes, split_axis=0, concat_axis=0, tiled=True)  15.5 us
    pallas_call x8, Pallas kernels, call(): pl.pallas_call(kernel, out_shape=outs, in_specs=[pl.BlockSpec(memory_spac...  15.2 us
    ppermute x3, waiting for transfers between devices, swapped(): return lax.ppermute(x, all_axes, pairs)  4.79 us
  transfers between devices with their start and end apart: 6, of which 5 were waited for; matrix products, arithmetic and copies ran while one was open for 2% of the time, Pallas kernels for 8%

profile of v8, /device:TPU:1, one launch (start us, length us, event | category | flops | bytes accessed | tf_op | source)
XLA Modules:
  0.0 98.3 jit_solution(1341918744759126443)
XLA Ops:
  0.6 0.8 fusion.4.packed
  1.4 0.8 broadcast_in_dim.3
  2.2 7.6 %all-to-all-start = ((bf16[16,80,128]{2,1,0:T(8,128)(2,1)}), bf16[16,80,128]{2,1,0:T(8,128)(2,1)S(1)}, u32[]{:S(2)}, u32[]{:S(2)}) async-start(bf16[16,80,128]{2,1,0:T(8,128)(2,1)} %broadcast_in_dim.3), calls=%async_computation | async-start | bytes 655360 | tf_op jit(solution)/shard_map/all_to_all | solution.py:259
  9.8 0.7 dynamic-slice_convert_fusion
  10.5 0.8 dynamic-slice_multiply_fusion
  11.4 0.7 convert_add_fusion.own_filter
  12.1 0.0 copy-start.5
  12.1 5.6 %all-to-all-done.got = bf16[16,80,128]{2,1,0:T(8,128)(2,1)S(1)} async-done(((bf16[16,80,128]{2,1,0:T(8,128)(2,1)}), bf16[16,80,128]{2,1,0:T(8,128)(2,1)S(1)}, u32[]{:S(2)}, u32[]{:S(2)}) %all-to-all-start) | async-done | bytes 327712 | tf_op jit(solution)/shard_map/all_to_all | solution.py:259
  17.7 5.8 %collective-permute-start = (bf16[16,80,128]{2,1,0:T(8,128)(2,1)S(1)}, bf16[16,80,128]{2,1,0:T(8,128)(2,1)S(1)}, u32[]{:S(2)}, u32[]{:S(2)}) collective-permute-start(bf16[16,80,128]{2,1,0:T(8,128)(2,1)S(1)} %all-to-all-done.got), channel_id=1, source_target_pairs={{0,1},{1,0},{2,3},{3,2},{4,5},{5,4},{6,7},{7,6},{8,9},{9,8},{10,11... | collective-permute-start | bytes 983048 | tf_op jit(solution)/shard_map/ppermute | solution.py:264
  23.5 3.6 %shard_map.131 = (bf16[22,512,2048]{2,1,0:T(8,128)(2,1)}, f32[512,64]{1,0:T(8,128)S(1)}) custom-call(bf16[16,80,128]{2,1,0:T(8,128)(2,1)S(1)} %all-to-all-done.got, f32[8,256]{1,0:T(8,128)S(1)} %pad.35.lattice, f32[64,320]{1,0:T(8,128)S(1)} %convert_add_fusion.own_filter), custom_call_target="tpu_custom_call" | custom-call | flops 99999997952 | tf_op jit(solution)/shard_map/pallas_call | solution.py:67
  27.2 0.0 copy-start.1
  27.2 0.0 copy-start.2
  27.2 0.0 copy-start.3
  27.2 0.0 copy-start.4
  27.2 0.0 copy-start.6
  27.2 0.0 collective-permute-done.got
  27.2 3.5 %shard_map.132 = (bf16[512,2048]{1,0:T(8,128)(2,1)S(1)}, bf16[256,128]{1,0:T(8,128)(2,1)}) custom-call(bf16[16,80,128]{2,1,0:T(8,128)(2,1)S(1)} %collective-permute-done.got, f32[8,256]{1,0:T(8,128)S(1)} %pad.35.lattice, f32[512,64]{1,0:T(8,128)S(1)} %get-tuple-element.10.own_total), custom_call_target="tpu_custom_call" | custom-call | tf_op jit(solution)/shard_map/pallas_call | solution.py:67
  30.7 13.4 %all-to-all-start.1 = ((bf16[16,16,128]{2,1,0:T(8,128)(2,1)}), bf16[16,16,128]{2,1,0:T(8,128)(2,1)S(1)}, u32[]{:S(2)}, u32[]{:S(2)}) async-start(bf16[16,16,128]{2,1,0:T(8,128)(2,1)} %bitcast), calls=%async_computation.1 | async-start | bytes 131072 | tf_op jit(solution)/shard_map/all_to_all | solution.py:259
  44.1 0.0 copy-done
  44.2 0.2 shard_map.133
  44.4 2.4 %collective-permute-start.1 = (bf16[272,128]{1,0:T(8,128)(2,1)S(1)}, bf16[272,128]{1,0:T(8,128)(2,1)S(1)}, u32[]{:S(2)}, u32[]{:S(2)}) collective-permute-start(bf16[272,128]{1,0:T(8,128)(2,1)S(1)} %get-tuple-element.12), channel_id=1, source_target_pairs={{1,2},{2,1},{3,4},{4,3},{5,6},{6,5},{7,8},{8,7},{9,10},{10,9},{11,... | collective-permute-start | bytes 208904 | tf_op jit(solution)/shard_map/ppermute | solution.py:264
  46.8 3.5 %collective-permute-done.1.far = bf16[272,128]{1,0:T(8,128)(2,1)S(1)} collective-permute-done((bf16[272,128]{1,0:T(8,128)(2,1)S(1)}, bf16[272,128]{1,0:T(8,128)(2,1)S(1)}, u32[]{:S(2)}, u32[]{:S(2)}) %collective-permute-start.1) | collective-permute-done | bytes 69664 | tf_op jit(solution)/shard_map/ppermute | solution.py:264
  50.3 5.5 %all-to-all-done.1.arrived = bf16[16,16,128]{2,1,0:T(8,128)(2,1)S(1)} async-done(((bf16[16,16,128]{2,1,0:T(8,128)(2,1)}), bf16[16,16,128]{2,1,0:T(8,128)(2,1)S(1)}, u32[]{:S(2)}, u32[]{:S(2)}) %all-to-all-start.1) | async-done | bytes 65568 | tf_op jit(solution)/shard_map/all_to_all | solution.py:259
  55.8 17.0 %all_to_all.20 = bf16[16,16,128]{2,1,0:T(8,128)(2,1)S(1)} all-to-all(bf16[16,16,128]{2,1,0:T(8,128)(2,1)S(1)} %shard_map.134), channel_id=1, replica_groups=mesh['yh'=2,'z'=16,'yl'=2,'x'=4,'c'=2] {'z'}, dimensions={0} | all-to-all | bytes 131072 | tf_op jit(solution)/shard_map/all_to_all | solution.py:259
  72.9 0.6 shard_map.135
  73.5 8.2 %collective-permute-start.2 = (bf16[1296,128]{1,0:T(8,128)(2,1)S(1)}, bf16[1296,128]{1,0:T(8,128)(2,1)S(1)}, u32[]{:S(2)}, u32[]{:S(2)}) collective-permute-start(bf16[1296,128]{1,0:T(8,128)(2,1)S(1)} %shard_map.135), channel_id=1, source_target_pairs={{0,1},{1,0},{2,3},{3,2},{4,5},{5,4},{6,7},{7,6},{8,9},{9,8},{10,11... | collective-permute-start | bytes 995336 | tf_op jit(solution)/shard_map/ppermute | solution.py:264
  81.8 1.2 %collective-permute-done.2.received.near = bf16[1296,128]{1,0:T(8,128)(2,1)S(1)} collective-permute-done((bf16[1296,128]{1,0:T(8,128)(2,1)S(1)}, bf16[1296,128]{1,0:T(8,128)(2,1)S(1)}, u32[]{:S(2)}, u32[]{:S(2)}) %collective-permute-start.2) | collective-permute-done | bytes 331808 | tf_op jit(solution)/shard_map/ppermute | solution.py:264
  83.0 2.6 %shard_map.136.messages = bf16[16,64,128]{2,1,0:T(8,128)(2,1)} custom-call(bf16[256,128]{1,0:T(8,128)(2,1)S(1)} %bitcast.5, f32[64,320]{1,0:T(8,128)S(1)} %convert_add_fusion.own_filter, bf16[22,512,2048]{2,1,0:T(8,128)(2,1)} %get-tuple-element.13.table_at, bf16[1296,128]{1,0:T(8,128)(2,1)S(1)} %collective-permute-done.2.received.near), custom_call_target="tpu_custom_call" | custom-call | tf_op jit(solution)/shard_map/pallas_call | solution.py:67
  85.7 3.5 %all-to-all-start.3 = ((bf16[16,64,128]{2,1,0:T(8,128)(2,1)}), bf16[16,64,128]{2,1,0:T(8,128)(2,1)S(1)}, u32[]{:S(2)}, u32[]{:S(2)}) async-start(bf16[16,64,128]{2,1,0:T(8,128)(2,1)} %shard_map.136.messages), calls=%async_computation.3 | async-start | bytes 524288 | tf_op jit(solution)/shard_map/all_to_all | solution.py:259
  89.3 3.9 %shard_map.137 = (f32[64,128]{1,0:T(8,128)S(1)}, bf16[3,64,128]{2,1,0:T(8,128)(2,1)}) custom-call(s32[1]{0:T(128)} %bitcast.1.core, bf16[80,128]{1,0:T(8,128)(2,1)S(1)} %fusion.4.packed, bf16[3,64,128]{2,1,0:T(8,128)(2,1)S(1)} %copy-done, s32[16,128]{1,0:T(8,128)S(1)} %copy-done.4, bf16[1296,128]{1,0:T(8,128)(2,1)S(1)} %collective-permute-done.2.received.near, ...), custom_call_target="tpu_custom_call" | custom-call | tf_op jit(solution)/shard_map/pallas_call | solution.py:67
  93.2 4.4 %all-to-all-done.3.arrived = bf16[16,64,128]{2,1,0:T(8,128)(2,1)S(1)} async-done(((bf16[16,64,128]{2,1,0:T(8,128)(2,1)}), bf16[16,64,128]{2,1,0:T(8,128)(2,1)S(1)}, u32[]{:S(2)}, u32[]{:S(2)}) %all-to-all-start.3) | async-done | bytes 262176 | tf_op jit(solution)/shard_map/all_to_all | solution.py:259
  97.6 0.6 shard_map.138
  (9 shorter events, 0.0 us)
Async XLA Ops:
  2.2 15.5 %all-to-all-start = ((bf16[16,80,128]{2,1,0:T(8,128)(2,1)}), bf16[16,80,128]{2,1,0:T(8,128)(2,1)S(1)}, u32[]{:S(2)}, u32[]{:S(2)}) async-start(bf16[16,80,128]{2,1,0:T(8,128)(2,1)} %broadcast_in_dim.3), calls=%async_computation | async-start | bytes 655360 | tf_op jit(solution)/shard_map/all_to_all | solution.py:259
  12.1 32.1 %copy-start = (bf16[3,64,128]{2,1,0:T(8,128)(2,1)S(1)}, bf16[3,64,128]{2,1,0:T(8,128)(2,1)}, u32[]{:S(2)}) copy-start(bf16[3,64,128]{2,1,0:T(8,128)(2,1)} %vec.3) | copy-start | bytes 147460
  12.1 32.1 %copy-start.5 = (s32[2,128]{1,0:T(2,128)S(1)}, s32[2,128]{1,0:T(2,128)}, u32[]{:S(2)}) copy-start(s32[2,128]{1,0:T(2,128)} %halo.1) | copy-start | bytes 3076
  17.7 9.5 %collective-permute-start = (bf16[16,80,128]{2,1,0:T(8,128)(2,1)S(1)}, bf16[16,80,128]{2,1,0:T(8,128)(2,1)S(1)}, u32[]{:S(2)}, u32[]{:S(2)}) collective-permute-start(bf16[16,80,128]{2,1,0:T(8,128)(2,1)S(1)} %all-to-all-done.got), channel_id=1, source_target_pairs={{0,1},{1,0},{2,3},{3,2},{4,5},{5,4},{6,7},{7,6},{8,9},{9,8},{10,11... | collective-permute-start | bytes 983048 | tf_op jit(solution)/shard_map/ppermute | solution.py:264
  27.2 62.1 %copy-start.1 = (bf16[64,192]{1,0:T(8,128)(2,1)S(1)}, bf16[64,192]{1,0:T(8,128)(2,1)}, u32[]{:S(2)}) copy-start(bf16[64,192]{1,0:T(8,128)(2,1)} %message_weight.1) | copy-start | bytes 73732
  27.2 62.0 %copy-start.2 = (bf16[64,64]{1,0:T(8,128)(2,1)S(1)}, bf16[64,64]{1,0:T(8,128)(2,1)}, u32[]{:S(2)}) copy-start(bf16[64,64]{1,0:T(8,128)(2,1)} %node_weight.1) | copy-start | bytes 24580
  27.2 62.0 %copy-start.3 = (bf16[20,192]{1,0:T(8,128)(2,1)S(1)}, bf16[20,192]{1,0:T(8,128)(2,1)}, u32[]{:S(2)}) copy-start(bf16[20,192]{1,0:T(8,128)(2,1)} %radial_weight.1) | copy-start | bytes 23044
  27.2 62.0 %copy-start.4 = (s32[16,128]{1,0:T(8,128)S(1)}, s32[16,128]{1,0:T(8,128)}, u32[]{:S(2)}) copy-start(s32[16,128]{1,0:T(8,128)} %ids.1) | copy-start | bytes 24580
  27.2 62.0 %copy-start.6 = (f32[64]{0:T(128)S(1)}, f32[64]{0:T(128)}, u32[]{:S(2)}) copy-start(f32[64]{0:T(128)} %param.20) | copy-start | bytes 772
  30.7 25.1 %all-to-all-start.1 = ((bf16[16,16,128]{2,1,0:T(8,128)(2,1)}), bf16[16,16,128]{2,1,0:T(8,128)(2,1)S(1)}, u32[]{:S(2)}, u32[]{:S(2)}) async-start(bf16[16,16,128]{2,1,0:T(8,128)(2,1)} %bitcast), calls=%async_computation.1 | async-start | bytes 131072 | tf_op jit(solution)/shard_map/all_to_all | solution.py:259
  44.4 5.9 %collective-permute-start.1 = (bf16[272,128]{1,0:T(8,128)(2,1)S(1)}, bf16[272,128]{1,0:T(8,128)(2,1)S(1)}, u32[]{:S(2)}, u32[]{:S(2)}) collective-permute-start(bf16[272,128]{1,0:T(8,128)(2,1)S(1)} %get-tuple-element.12), channel_id=1, source_target_pairs={{1,2},{2,1},{3,4},{4,3},{5,6},{6,5},{7,8},{8,7},{9,10},{10,9},{11,... | collective-permute-start | bytes 208904 | tf_op jit(solution)/shard_map/ppermute | solution.py:264
  73.5 9.5 %collective-permute-start.2 = (bf16[1296,128]{1,0:T(8,128)(2,1)S(1)}, bf16[1296,128]{1,0:T(8,128)(2,1)S(1)}, u32[]{:S(2)}, u32[]{:S(2)}) collective-permute-start(bf16[1296,128]{1,0:T(8,128)(2,1)S(1)} %shard_map.135), channel_id=1, source_target_pairs={{0,1},{1,0},{2,3},{3,2},{4,5},{5,4},{6,7},{7,6},{8,9},{9,8},{10,11... | collective-permute-start | bytes 995336 | tf_op jit(solution)/shard_map/ppermute | solution.py:264
  85.7 11.9 %all-to-all-start.3 = ((bf16[16,64,128]{2,1,0:T(8,128)(2,1)}), bf16[16,64,128]{2,1,0:T(8,128)(2,1)S(1)}, u32[]{:S(2)}, u32[]{:S(2)}) async-start(bf16[16,64,128]{2,1,0:T(8,128)(2,1)} %shard_map.136.messages), calls=%async_computation.3 | async-start | bytes 524288 | tf_op jit(solution)/shard_map/all_to_all | solution.py:259

commit v9 on v7

--- a/solution.py
+++ b/solution.py
@@ -21,7 +21,6 @@
 ATOMS = 65536
 PACK = 80
 HALO_ROWS = 272
-GROUP = 8
 
 same_axes = ("yh", "yl", "x")
 kb_axes = ("yl", "x", "c")
@@ -62,7 +61,7 @@
 VM, SM, ANY = pltpu.VMEM, pltpu.SMEM, pl.ANY
 
 
-def call(kernel, places, outs, *operands, scratch=()):
+def call(kernel, places, outs, *operands, scratch=(), flops=0):
     return pl.pallas_call(
         kernel,
         out_shape=outs,
@@ -70,7 +69,7 @@
         out_specs=jax.tree.map(lambda _: pl.BlockSpec(memory_space=VM), outs),
         scratch_shapes=list(scratch),
         compiler_params=pltpu.CompilerParams(vmem_limit_bytes=VMEM_LIMIT),
-        cost_estimate=pl.CostEstimate(flops=0, bytes_accessed=0, transcendentals=0),
+        cost_estimate=pl.CostEstimate(flops=flops, bytes_accessed=0, transcendentals=0),
     )(*operands)
 
 
@@ -94,37 +93,39 @@
         out[...] = dot(rows, chosen, ((1,), (0,))).astype(jnp.bfloat16)
 
 
-def table_kernel(own, other, lattice, far, own_filter, table, partial, columns, total):
-    turned = lattice[...].T
+def add_atoms(got, constants, table, columns, total):
+    turned = constants[F:, :KDEV].T
     for i in range(3):
         columns[i] = jnp.broadcast_to(turned[:, i : i + 1], (KDEV, ATOM))
+    for first in range(0, SAME, 2):
+        both = jnp.concatenate([got[first], got[first + 1]], axis=1)
+        pos = summed(both[F:].astype(jnp.float32))
+        at = slice(first * ATOM, (first + 2) * ATOM)
+        for k in range(0, KDEV, 64):
+            rows = slice(k, k + 64)
+            halves = []
+            for lanes in (slice(0, ATOM), slice(ATOM, 2 * ATOM)):
+                halves.append(
+                    (columns[0, rows] * pos[0:1, lanes] + columns[1, rows] * pos[1:2, lanes])
+                    + columns[2, rows] * pos[2:3, lanes]
+                )
+            cosines, sines = cosine_and_sine(jnp.concatenate(halves, axis=1))
+            cosines, sines = cosines.astype(jnp.bfloat16), sines.astype(jnp.bfloat16)
+            table[k : k + 64, at] = cosines
+            table[KDEV + k : KDEV + k + 64, at] = sines
+            sums = dot(jnp.concatenate([cosines, sines], axis=0), both[:F], ((1,), (1,)))
+            total[k : k + 64] += sums[:64]
+            total[KDEV + k : KDEV + k + 64] += sums[64:]
+
+
+def own_table_kernel(got, constants, table, total, columns):
     total[...] = jnp.zeros_like(total)
-
-    for part, got in enumerate((own, other)):
-
-        @pl.loop(0, SAME // GROUP)
-        def _(step):
-            for pair in range(0, GROUP, 2):
-                first = step * GROUP + pair
-                both = jnp.concatenate([got[first], got[first + 1]], axis=1)
-                pos = summed(both[F:].astype(jnp.float32))
-                at = pl.ds(pl.multiple_of((part * SAME + first) * ATOM, 2 * ATOM), 2 * ATOM)
-                for k in range(0, KDEV, 64):
-                    rows = slice(k, k + 64)
-                    halves = []
-                    for lanes in (slice(0, ATOM), slice(ATOM, 2 * ATOM)):
-                        halves.append(
-                            (columns[0, rows] * pos[0:1, lanes] + columns[1, rows] * pos[1:2, lanes])
-                            + columns[2, rows] * pos[2:3, lanes]
-                        )
-                    cosines, sines = cosine_and_sine(jnp.concatenate(halves, axis=1))
-                    cosines, sines = cosines.astype(jnp.bfloat16), sines.astype(jnp.bfloat16)
-                    table[k : k + 64, at] = cosines
-                    table[KDEV + k : KDEV + k + 64, at] = sines
-                    sums = dot(jnp.concatenate([cosines, sines], axis=0), both[:F], ((1,), (1,)))
-                    total[k : k + 64] += sums[:64]
-                    total[KDEV + k : KDEV + k + 64] += sums[64:]
-
+    add_atoms(got, constants, table, columns, total)
+
+
+def other_table_kernel(got, constants, own_total, far, table, partial, columns, total):
+    total[...] = own_total[...]
+    add_atoms(got, constants, table, columns, total)
     partial[...] = jnp.concatenate([total[:KDEV], total[KDEV:]], axis=1).astype(jnp.bfloat16)
 
 
@@ -137,24 +138,23 @@
         out[i] = total
 
 
-def filtered_sums(got, own_filter):
-    own, weight = own_filter[:, :KDEV], own_filter[:, KDEV:].astype(jnp.bfloat16)
+def filtered_sums(got, constants):
+    own, weight = constants[:F, :KDEV], constants[:F, KDEV:].astype(jnp.bfloat16)
     total = [dot(weight, got[:, part * F : (part + 1) * F], ((0,), (1,))) for part in range(2)]
     return jnp.concatenate([own * total[0], own * total[1]], axis=1).astype(jnp.bfloat16)
 
 
-def project_other_kernel(got, own_filter, table, near, out):
-    filtered = filtered_sums(got, own_filter)
+def project_other_kernel(got, constants, table, near, out):
+    filtered = filtered_sums(got, constants)
     for first in range(0, SAME, 8):
-        atoms = slice((SAME + first) * ATOM, (SAME + first + 8) * ATOM)
-        message = dot(filtered, table[:, atoms], ((1,), (0,))).astype(jnp.bfloat16)
+        message = dot(filtered, table[:, first * ATOM : (first + 8) * ATOM], ((1,), (0,))).astype(jnp.bfloat16)
         for p in range(8):
             out[(first + p) * F : (first + p + 1) * F] = message[:, p * ATOM : (p + 1) * ATOM]
     out[SAME * F :] = near[...]
 
 
-def project_own_kernel(got, own_filter, table, received, out):
-    filtered = filtered_sums(got, own_filter)
+def project_own_kernel(got, constants, table, received, out):
+    filtered = filtered_sums(got, constants)
     for first in range(0, SAME, 8):
         message = dot(filtered, table[:, first * ATOM : (first + 8) * ATOM], ((1,), (0,)))
         for p in range(first, first + 8):
@@ -244,18 +244,28 @@
     packed = packed_rows(features, positions)
     own = exchanged(jnp.broadcast_to(packed, (SAME, PACK, ATOM)), same_axes)
     other = swapped(own, 0)
-    own_lattice = jnp.pad(lax.dynamic_slice_in_dim(lattice, k_at, KDEV, 1).astype(f32), ((0, 5), (0, 0)))
-    own_filter = jnp.pad(lax.dynamic_slice_in_dim(kspace_filter, half_at, KDEV, 1) * norm_scale, ((0, 0), (0, F)))
-    own_filter = own_filter + jnp.pad(ewald_weight.astype(f32), ((0, 0), (KDEV, 0)))
+    own_lattice = lax.dynamic_slice_in_dim(lattice, k_at, KDEV, 1).astype(f32)
+    own_filter = lax.dynamic_slice_in_dim(kspace_filter, half_at, KDEV, 1) * norm_scale
+    constants = jnp.pad(own_filter, ((0, 8), (0, F))) + jnp.pad(own_lattice, ((F, 5), (0, F)))
+    constants = constants + jnp.pad(ewald_weight.astype(f32), ((0, 8), (KDEV, 0)))
     core = lax.axis_index("c").astype(jnp.int32).reshape(1)
     halo = shape((HALO_ROWS, ATOM), bf16)
     far, near = call(halo_kernel, [SM, VM, VM, VM], (halo, halo), core, packed, vectors, halo_lists)
     far = swapped(far, 1)
-    table, partial = call(
-        table_kernel,
-        [VM, VM, VM, ANY, ANY],
-        (shape((2 * KDEV, PLANE * ATOM), bf16), shape((KDEV, 2 * F), bf16)),
-        own, other, own_lattice, far, own_filter,
+    half_table = shape((2 * KDEV, SAME * ATOM), bf16)
+    own_table, own_total = call(
+        own_table_kernel,
+        [VM, VM],
+        (half_table, shape((2 * KDEV, F), f32)),
+        own, constants,
+        scratch=[VM((3, KDEV, ATOM), f32)],
+        flops=3 * 10**9,
+    )
+    other_table, partial = call(
+        other_table_kernel,
+        [VM, VM, VM, ANY],
+        (half_table, shape((KDEV, 2 * F), bf16)),
+        other, constants, own_total, far,
         scratch=[VM((3, KDEV, ATOM), f32), VM((2 * KDEV, F), f32)],
     )
     arrived = exchanged(partial.reshape(DEPTH, KDEV // DEPTH, 2 * F), "z")
@@ -265,11 +275,11 @@
         project_other_kernel,
         [VM] * 4,
         shape((SAME * F + HALO_ROWS, ATOM), bf16),
-        totals, own_filter, table, near,
+        totals, constants, other_table, near,
     )
     received = swapped(for_other, 0)
     messages = call(
-        project_own_kernel, [VM] * 4, shape((SAME, F, ATOM), bf16), totals, own_filter, table, received
+        project_own_kernel, [VM] * 4, shape((SAME, F, ATOM), bf16), totals, constants, own_table, received
     )
     returned = exchanged(messages, same_axes)
     scalar, new_vectors = call(

time: 91.6 us -> 89.7 us (0.979)
  blocking collectives: 34.4 us -> 32.8 us
    all_to_all x2, blocking collectives: 34.4 us -> 32.8 us  [exchanged(): return lax.all_to_all(x, axes, split_axis=0, concat_axis=0, tiled=True)]
    pallas_call x7 -> x8, Pallas kernels: 11.6 us -> 11.3 us  [call(): pl.pallas_call(kernel, out_shape=outs, in_specs=[pl.BlockSpec(memory_spac...]
  transfers between devices with their start and end apart: 5 -> 5, of which waited for: 2 -> 2; matrix products, arithmetic and copies ran while one was open for 2% -> 3% of each run, Pallas kernels for 5% -> 7%
where the time goes in v9:
time: 89.7 us; the launch traced here: 89 us
  starting transfers between devices  33.2 us (37%)
  blocking collectives  32.8 us (37%)
  Pallas kernels  11.3 us (13%)
  waiting for transfers between devices  5.39 us (6%)
  other arithmetic  3.08 us (3%)
  local copies, waits for them, and re-layouts  2.28 us (3%)
    all_to_all x2, blocking collectives, exchanged(): return lax.all_to_all(x, axes, split_axis=0, concat_axis=0, tiled=True)  32.8 us
    ppermute x3, starting transfers between devices, swapped(): return lax.ppermute(x, all_axes, pairs)  22.1 us
    pallas_call x8, Pallas kernels, call(): pl.pallas_call(kernel, out_shape=outs, in_specs=[pl.BlockSpec(memory_spac...  11.3 us
    all_to_all x2, starting transfers between devices, exchanged(): return lax.all_to_all(x, axes, split_axis=0, concat_axis=0, tiled=True)  11.1 us
    all_to_all x2, waiting for transfers between devices, exchanged(): return lax.all_to_all(x, axes, split_axis=0, concat_axis=0, tiled=True)  4.14 us
  transfers between devices with their start and end apart: 5, of which 2 were waited for; matrix products, arithmetic and copies ran while one was open for 3% of the time, Pallas kernels for 7%

profile of v9, /device:TPU:1, one launch (start us, length us, event | category | flops | bytes accessed | tf_op | source)
XLA Modules:
  0.0 89.0 jit_solution(16294075721568760792)
XLA Ops:
  0.6 0.8 fusion.4.packed
  1.4 0.8 broadcast_in_dim.3
  2.2 7.6 %all-to-all-start = ((bf16[16,80,128]{2,1,0:T(8,128)(2,1)}), bf16[16,80,128]{2,1,0:T(8,128)(2,1)S(1)}, u32[]{:S(2)}, u32[]{:S(2)}) async-start(bf16[16,80,128]{2,1,0:T(8,128)(2,1)} %broadcast_in_dim.3), calls=%async_computation | async-start | bytes 655360 | tf_op jit(solution)/shard_map/all_to_all | solution.py:228
  9.8 0.0 copy-start
  9.8 0.8 copy-done
  10.6 0.7 copy-done.6
  11.3 0.2 shard_map.132
  11.5 6.2 %collective-permute-start.1 = (bf16[272,128]{1,0:T(8,128)(2,1)S(1)}, bf16[272,128]{1,0:T(8,128)(2,1)S(1)}, u32[]{:S(2)}, u32[]{:S(2)}) collective-permute-start(bf16[272,128]{1,0:T(8,128)(2,1)S(1)} %get-tuple-element.11), channel_id=1, source_target_pairs={{1,2},{2,1},{3,4},{4,3},{5,6},{6,5},{7,8},{8,7},{9,10},{10,9},{11,... | collective-permute-start | bytes 208904 | tf_op jit(solution)/shard_map/ppermute | solution.py:233
  17.7 0.7 dynamic-slice_convert_fusion
  18.4 0.8 dynamic-slice_multiply_fusion
  19.2 0.0 all-to-all-done.got
  19.2 11.7 %collective-permute-start = (bf16[16,80,128]{2,1,0:T(8,128)(2,1)S(1)}, bf16[16,80,128]{2,1,0:T(8,128)(2,1)S(1)}, u32[]{:S(2)}, u32[]{:S(2)}) collective-permute-start(bf16[16,80,128]{2,1,0:T(8,128)(2,1)S(1)} %all-to-all-done.got), channel_id=1, source_target_pairs={{0,1},{1,0},{2,3},{3,2},{4,5},{5,4},{6,7},{7,6},{8,9},{9,8},{10,11... | collective-permute-start | bytes 983048 | tf_op jit(solution)/shard_map/ppermute | solution.py:233
  30.9 0.7 convert_add_fusion.constants
  31.6 2.2 %shard_map.131 = (bf16[512,2048]{1,0:T(8,128)(2,1)S(1)}, f32[512,64]{1,0:T(8,128)S(1)}) custom-call(bf16[16,80,128]{2,1,0:T(8,128)(2,1)S(1)} %all-to-all-done.got, f32[72,320]{1,0:T(8,128)S(1)} %convert_add_fusion.constants), custom_call_target="tpu_custom_call" | custom-call | flops 3000000000 | tf_op jit(solution)/shard_map/pallas_call | solution.py:65
  33.9 0.0 collective-permute-done.1.far
  33.9 2.3 %shard_map.133 = (bf16[512,2048]{1,0:T(8,128)(2,1)S(1)}, bf16[256,128]{1,0:T(8,128)(2,1)S(1)}) custom-call(bf16[16,80,128]{2,1,0:T(8,128)(2,1)S(1)} %collective-permute-done.got, f32[72,320]{1,0:T(8,128)S(1)} %convert_add_fusion.constants, f32[512,64]{1,0:T(8,128)S(1)} %get-tuple-element.10.own_total, bf16[272,128]{1,0:T(8,128)(2,1)S(1)} %collective-permute-done.1.far), custom_call_target="tpu_custom_call" | custom-call | tf_op jit(solution)/shard_map/pallas_call | solution.py:65
  36.2 17.5 %all_to_all.20.arrived = bf16[16,16,128]{2,1,0:T(8,128)(2,1)S(1)} all-to-all(bf16[16,16,128]{2,1,0:T(8,128)(2,1)S(1)} %bitcast.6), channel_id=1, replica_groups=mesh['yh'=2,'z'=16,'yl'=2,'x'=4,'c'=2] {'z'}, dimensions={0} | all-to-all | bytes 131072 | tf_op jit(solution)/shard_map/all_to_all | solution.py:228
  53.7 15.3 %all_to_all.21 = bf16[16,16,128]{2,1,0:T(8,128)(2,1)S(1)} all-to-all(bf16[16,16,128]{2,1,0:T(8,128)(2,1)S(1)} %shard_map.134), channel_id=1, replica_groups=mesh['yh'=2,'z'=16,'yl'=2,'x'=4,'c'=2] {'z'}, dimensions={0} | all-to-all | bytes 131072 | tf_op jit(solution)/shard_map/all_to_all | solution.py:228
  69.1 0.6 shard_map.135
  69.7 0.0 copy-start.1
  69.7 0.0 copy-start.2
  69.7 0.0 copy-start.3
  69.8 0.0 copy-start.4
  69.8 0.0 copy-start.5
  69.8 0.0 copy-start.7
  69.8 4.3 %collective-permute-start.2 = (bf16[1296,128]{1,0:T(8,128)(2,1)S(1)}, bf16[1296,128]{1,0:T(8,128)(2,1)S(1)}, u32[]{:S(2)}, u32[]{:S(2)}) collective-permute-start(bf16[1296,128]{1,0:T(8,128)(2,1)S(1)} %shard_map.135), channel_id=1, source_target_pairs={{0,1},{1,0},{2,3},{3,2},{4,5},{5,4},{6,7},{7,6},{8,9},{9,8},{10,11... | collective-permute-start | bytes 995336 | tf_op jit(solution)/shard_map/ppermute | solution.py:233
  74.1 1.2 %collective-permute-done.2.received.near = bf16[1296,128]{1,0:T(8,128)(2,1)S(1)} collective-permute-done((bf16[1296,128]{1,0:T(8,128)(2,1)S(1)}, bf16[1296,128]{1,0:T(8,128)(2,1)S(1)}, u32[]{:S(2)}, u32[]{:S(2)}) %collective-permute-start.2) | collective-permute-done | bytes 331808 | tf_op jit(solution)/shard_map/ppermute | solution.py:233
  75.3 1.4 %shard_map.136.messages = bf16[16,64,128]{2,1,0:T(8,128)(2,1)} custom-call(bf16[256,128]{1,0:T(8,128)(2,1)S(1)} %bitcast.5, f32[72,320]{1,0:T(8,128)S(1)} %convert_add_fusion.constants, bf16[512,2048]{1,0:T(8,128)(2,1)S(1)} %get-tuple-element.13.table, bf16[1296,128]{1,0:T(8,128)(2,1)S(1)} %collective-permute-done.2.received.near), custom_call_target="tpu_custom_call" | custom-call | tf_op jit(solution)/shard_map/pallas_call | solution.py:65
  76.7 3.5 %all-to-all-start.3 = ((bf16[16,64,128]{2,1,0:T(8,128)(2,1)}), bf16[16,64,128]{2,1,0:T(8,128)(2,1)S(1)}, u32[]{:S(2)}, u32[]{:S(2)}) async-start(bf16[16,64,128]{2,1,0:T(8,128)(2,1)} %shard_map.136.messages), calls=%async_computation.3 | async-start | bytes 524288 | tf_op jit(solution)/shard_map/all_to_all | solution.py:228
  80.3 3.9 %shard_map.137 = (f32[64,128]{1,0:T(8,128)S(1)}, bf16[3,64,128]{2,1,0:T(8,128)(2,1)}) custom-call(s32[1]{0:T(128)} %bitcast.core, bf16[80,128]{1,0:T(8,128)(2,1)S(1)} %fusion.4.packed, bf16[3,64,128]{2,1,0:T(8,128)(2,1)S(1)} %copy-done.1, s32[16,128]{1,0:T(8,128)S(1)} %copy-done.5, bf16[1296,128]{1,0:T(8,128)(2,1)S(1)} %collective-permute-done.2.received.near, ...), custom_call_target="tpu_custom_call" | custom-call | tf_op jit(solution)/shard_map/pallas_call | solution.py:65
  84.2 4.1 %all-to-all-done.3.arrived = bf16[16,64,128]{2,1,0:T(8,128)(2,1)S(1)} async-done(((bf16[16,64,128]{2,1,0:T(8,128)(2,1)}), bf16[16,64,128]{2,1,0:T(8,128)(2,1)S(1)}, u32[]{:S(2)}, u32[]{:S(2)}) %all-to-all-start.3) | async-done | bytes 262176 | tf_op jit(solution)/shard_map/all_to_all | solution.py:228
  88.3 0.6 shard_map.138
  (9 shorter events, 0.0 us)
Async XLA Ops:
  2.2 17.0 %all-to-all-start = ((bf16[16,80,128]{2,1,0:T(8,128)(2,1)}), bf16[16,80,128]{2,1,0:T(8,128)(2,1)S(1)}, u32[]{:S(2)}, u32[]{:S(2)}) async-start(bf16[16,80,128]{2,1,0:T(8,128)(2,1)} %broadcast_in_dim.3), calls=%async_computation | async-start | bytes 655360 | tf_op jit(solution)/shard_map/all_to_all | solution.py:228
  9.8 0.8 copy-start
  10.6 0.7 copy-start.6
  11.5 22.4 %collective-permute-start.1 = (bf16[272,128]{1,0:T(8,128)(2,1)S(1)}, bf16[272,128]{1,0:T(8,128)(2,1)S(1)}, u32[]{:S(2)}, u32[]{:S(2)}) collective-permute-start(bf16[272,128]{1,0:T(8,128)(2,1)S(1)} %get-tuple-element.11), channel_id=1, source_target_pairs={{1,2},{2,1},{3,4},{4,3},{5,6},{6,5},{7,8},{8,7},{9,10},{10,9},{11,... | collective-permute-start | bytes 208904 | tf_op jit(solution)/shard_map/ppermute | solution.py:233
  19.2 14.7 %collective-permute-start = (bf16[16,80,128]{2,1,0:T(8,128)(2,1)S(1)}, bf16[16,80,128]{2,1,0:T(8,128)(2,1)S(1)}, u32[]{:S(2)}, u32[]{:S(2)}) collective-permute-start(bf16[16,80,128]{2,1,0:T(8,128)(2,1)S(1)} %all-to-all-done.got), channel_id=1, source_target_pairs={{0,1},{1,0},{2,3},{3,2},{4,5},{5,4},{6,7},{7,6},{8,9},{9,8},{10,11... | collective-permute-start | bytes 983048 | tf_op jit(solution)/shard_map/ppermute | solution.py:233
  69.7 10.5 %copy-start.1 = (bf16[3,64,128]{2,1,0:T(8,128)(2,1)S(1)}, bf16[3,64,128]{2,1,0:T(8,128)(2,1)}, u32[]{:S(2)}) copy-start(bf16[3,64,128]{2,1,0:T(8,128)(2,1)} %vec.3) | copy-start | bytes 147460
  69.7 10.5 %copy-start.2 = (bf16[64,192]{1,0:T(8,128)(2,1)S(1)}, bf16[64,192]{1,0:T(8,128)(2,1)}, u32[]{:S(2)}) copy-start(bf16[64,192]{1,0:T(8,128)(2,1)} %message_weight.1) | copy-start | bytes 73732
  69.7 10.5 %copy-start.3 = (bf16[64,64]{1,0:T(8,128)(2,1)S(1)}, bf16[64,64]{1,0:T(8,128)(2,1)}, u32[]{:S(2)}) copy-start(bf16[64,64]{1,0:T(8,128)(2,1)} %node_weight.1) | copy-start | bytes 24580
  69.8 10.5 %copy-start.4 = (bf16[20,192]{1,0:T(8,128)(2,1)S(1)}, bf16[20,192]{1,0:T(8,128)(2,1)}, u32[]{:S(2)}) copy-start(bf16[20,192]{1,0:T(8,128)(2,1)} %radial_weight.1) | copy-start | bytes 23044
  69.8 10.5 %copy-start.5 = (s32[16,128]{1,0:T(8,128)S(1)}, s32[16,128]{1,0:T(8,128)}, u32[]{:S(2)}) copy-start(s32[16,128]{1,0:T(8,128)} %ids.1) | copy-start | bytes 24580
  69.8 10.5 %copy-start.7 = (f32[64]{0:T(128)S(1)}, f32[64]{0:T(128)}, u32[]{:S(2)}) copy-start(f32[64]{0:T(128)} %param.20) | copy-start | bytes 772
  69.8 5.5 %collective-permute-start.2 = (bf16[1296,128]{1,0:T(8,128)(2,1)S(1)}, bf16[1296,128]{1,0:T(8,128)(2,1)S(1)}, u32[]{:S(2)}, u32[]{:S(2)}) collective-permute-start(bf16[1296,128]{1,0:T(8,128)(2,1)S(1)} %shard_map.135), channel_id=1, source_target_pairs={{0,1},{1,0},{2,3},{3,2},{4,5},{5,4},{6,7},{7,6},{8,9},{9,8},{10,11... | collective-permute-start | bytes 995336 | tf_op jit(solution)/shard_map/ppermute | solution.py:233
  76.7 11.7 %all-to-all-start.3 = ((bf16[16,64,128]{2,1,0:T(8,128)(2,1)}), bf16[16,64,128]{2,1,0:T(8,128)(2,1)S(1)}, u32[]{:S(2)}, u32[]{:S(2)}) async-start(bf16[16,64,128]{2,1,0:T(8,128)(2,1)} %shard_map.136.messages), calls=%async_computation.3 | async-start | bytes 524288 | tf_op jit(solution)/shard_map/all_to_all | solution.py:228

commit v10 on v9

--- a/solution.py
+++ b/solution.py
@@ -153,13 +153,17 @@
     out[SAME * F :] = near[...]
 
 
-def project_own_kernel(got, constants, table, received, out):
+def project_own_kernel(got, constants, table, out):
     filtered = filtered_sums(got, constants)
     for first in range(0, SAME, 8):
         message = dot(filtered, table[:, first * ATOM : (first + 8) * ATOM], ((1,), (0,)))
-        for p in range(first, first + 8):
-            there = received[p * F : (p + 1) * F].astype(jnp.float32)
-            out[p] = (message[:, (p - first) * ATOM : (p - first + 1) * ATOM] + there).astype(jnp.bfloat16)
+        for p in range(8):
+            out[first + p] = message[:, p * ATOM : (p + 1) * ATOM]
+
+
+def join_kernel(own, received, out):
+    for p in range(SAME):
+        out[p] = (own[p] + received[p * F : (p + 1) * F].astype(jnp.float32)).astype(jnp.bfloat16)
 
 
 def finish_kernel(arrived, scalar, out):
@@ -278,9 +282,11 @@
         totals, constants, other_table, near,
     )
     received = swapped(for_other, 0)
-    messages = call(
-        project_own_kernel, [VM] * 4, shape((SAME, F, ATOM), bf16), totals, constants, own_table, received
-    )
+    own_messages = call(
+        project_own_kernel, [VM] * 3, shape((SAME, F, ATOM), f32), totals, constants, own_table,
+        flops=10**9,
+    )
+    messages = call(join_kernel, [VM] * 2, shape((SAME, F, ATOM), bf16), own_messages, received)
     returned = exchanged(messages, same_axes)
     scalar, new_vectors = call(
         short_kernel,

time: 89.7 us -> 88.9 us (level)
    pallas_call x8 -> x9, Pallas kernels: 11.3 us -> 11.4 us  [call(): pl.pallas_call(kernel, out_shape=outs, in_specs=[pl.BlockSpec(memory_spac...]
  transfers between devices with their start and end apart: 5 -> 5, of which waited for: 2 -> 2; matrix products, arithmetic and copies ran while one was open for 3% -> 3% of each run, Pallas kernels for 7% -> 8%
where the time goes in v10:
time: 88.9 us; the launch traced here: 88.2 us
  starting transfers between devices  33.1 us (37%)
  blocking collectives  32.8 us (37%)
  Pallas kernels  11.4 us (13%)
  waiting for transfers between devices  4.67 us (5%)
  other arithmetic  3.08 us (3%)
  local copies, waits for them, and re-layouts  2.28 us (3%)
    all_to_all x2, blocking collectives, exchanged(): return lax.all_to_all(x, axes, split_axis=0, concat_axis=0, tiled=True)  32.8 us
    ppermute x3, starting transfers between devices, swapped(): return lax.ppermute(x, all_axes, pairs)  22 us
    pallas_call x9, Pallas kernels, call(): pl.pallas_call(kernel, out_shape=outs, in_specs=[pl.BlockSpec(memory_spac...  11.4 us
    all_to_all x2, starting transfers between devices, exchanged(): return lax.all_to_all(x, axes, split_axis=0, concat_axis=0, tiled=True)  11.1 us
    all_to_all x2, waiting for transfers between devices, exchanged(): return lax.all_to_all(x, axes, split_axis=0, concat_axis=0, tiled=True)  4.14 us
  transfers between devices with their start and end apart: 5, of which 2 were waited for; matrix products, arithmetic and copies ran while one was open for 3% of the time, Pallas kernels for 8%

profile of v10, /device:TPU:1, one launch (start us, length us, event | category | flops | bytes accessed | tf_op | source)
XLA Modules:
  0.0 88.2 jit_solution(5101586006922525404)
XLA Ops:
  0.6 0.8 fusion.4.packed
  1.4 0.8 broadcast_in_dim.3
  2.2 7.6 %all-to-all-start = ((bf16[16,80,128]{2,1,0:T(8,128)(2,1)}), bf16[16,80,128]{2,1,0:T(8,128)(2,1)S(1)}, u32[]{:S(2)}, u32[]{:S(2)}) async-start(bf16[16,80,128]{2,1,0:T(8,128)(2,1)} %broadcast_in_dim.3), calls=%async_computation | async-start | bytes 655360 | tf_op jit(solution)/shard_map/all_to_all | solution.py:232
  9.8 0.0 copy-start
  9.8 0.8 copy-done
  10.6 0.7 copy-done.6
  11.3 0.2 shard_map.132
  11.5 6.2 %collective-permute-start.1 = (bf16[272,128]{1,0:T(8,128)(2,1)S(1)}, bf16[272,128]{1,0:T(8,128)(2,1)S(1)}, u32[]{:S(2)}, u32[]{:S(2)}) collective-permute-start(bf16[272,128]{1,0:T(8,128)(2,1)S(1)} %get-tuple-element.11), channel_id=1, source_target_pairs={{1,2},{2,1},{3,4},{4,3},{5,6},{6,5},{7,8},{8,7},{9,10},{10,9},{11,... | collective-permute-start | bytes 208904 | tf_op jit(solution)/shard_map/ppermute | solution.py:237
  17.7 0.7 dynamic-slice_convert_fusion
  18.4 0.8 dynamic-slice_multiply_fusion
  19.2 0.0 all-to-all-done.got
  19.2 11.7 %collective-permute-start = (bf16[16,80,128]{2,1,0:T(8,128)(2,1)S(1)}, bf16[16,80,128]{2,1,0:T(8,128)(2,1)S(1)}, u32[]{:S(2)}, u32[]{:S(2)}) collective-permute-start(bf16[16,80,128]{2,1,0:T(8,128)(2,1)S(1)} %all-to-all-done.got), channel_id=1, source_target_pairs={{0,1},{1,0},{2,3},{3,2},{4,5},{5,4},{6,7},{7,6},{8,9},{9,8},{10,11... | collective-permute-start | bytes 983048 | tf_op jit(solution)/shard_map/ppermute | solution.py:237
  30.9 0.7 convert_add_fusion.constants
  31.6 2.2 %shard_map.131 = (bf16[512,2048]{1,0:T(8,128)(2,1)S(1)}, f32[512,64]{1,0:T(8,128)S(1)}) custom-call(bf16[16,80,128]{2,1,0:T(8,128)(2,1)S(1)} %all-to-all-done.got, f32[72,320]{1,0:T(8,128)S(1)} %convert_add_fusion.constants), custom_call_target="tpu_custom_call" | custom-call | flops 3000000000 | tf_op jit(solution)/shard_map/pallas_call | solution.py:65
  33.9 2.3 %shard_map.133 = (bf16[512,2048]{1,0:T(8,128)(2,1)S(1)}, bf16[256,128]{1,0:T(8,128)(2,1)S(1)}) custom-call(bf16[16,80,128]{2,1,0:T(8,128)(2,1)S(1)} %collective-permute-done.got, f32[72,320]{1,0:T(8,128)S(1)} %convert_add_fusion.constants, f32[512,64]{1,0:T(8,128)S(1)} %get-tuple-element.10.own_total, bf16[272,128]{1,0:T(8,128)(2,1)S(1)} %collective-permute-done.1.far), custom_call_target="tpu_custom_call" | custom-call | tf_op jit(solution)/shard_map/pallas_call | solution.py:65
  36.2 17.5 %all_to_all.20.arrived = bf16[16,16,128]{2,1,0:T(8,128)(2,1)S(1)} all-to-all(bf16[16,16,128]{2,1,0:T(8,128)(2,1)S(1)} %bitcast.6), channel_id=1, replica_groups=mesh['yh'=2,'z'=16,'yl'=2,'x'=4,'c'=2] {'z'}, dimensions={0} | all-to-all | bytes 131072 | tf_op jit(solution)/shard_map/all_to_all | solution.py:232
  53.7 15.3 %all_to_all.21 = bf16[16,16,128]{2,1,0:T(8,128)(2,1)S(1)} all-to-all(bf16[16,16,128]{2,1,0:T(8,128)(2,1)S(1)} %shard_map.134), channel_id=1, replica_groups=mesh['yh'=2,'z'=16,'yl'=2,'x'=4,'c'=2] {'z'}, dimensions={0} | all-to-all | bytes 131072 | tf_op jit(solution)/shard_map/all_to_all | solution.py:232
  69.1 0.6 shard_map.136
  69.7 4.1 %collective-permute-start.2 = (bf16[1296,128]{1,0:T(8,128)(2,1)S(1)}, bf16[1296,128]{1,0:T(8,128)(2,1)S(1)}, u32[]{:S(2)}, u32[]{:S(2)}) collective-permute-start(bf16[1296,128]{1,0:T(8,128)(2,1)S(1)} %shard_map.136), channel_id=1, source_target_pairs={{0,1},{1,0},{2,3},{3,2},{4,5},{5,4},{6,7},{7,6},{8,9},{9,8},{10,11... | collective-permute-start | bytes 995336 | tf_op jit(solution)/shard_map/ppermute | solution.py:237
  73.9 0.0 copy-start.1
  73.9 0.0 copy-start.2
  73.9 0.0 copy-start.3
  73.9 0.0 copy-start.4
  73.9 0.0 copy-start.5
  73.9 0.0 copy-start.7
  73.9 0.6 shard_map.135.own
  74.6 0.5 collective-permute-done.2.received.near
  75.1 0.8 shard_map.137.messages
  75.9 3.5 %all-to-all-start.3 = ((bf16[16,64,128]{2,1,0:T(8,128)(2,1)}), bf16[16,64,128]{2,1,0:T(8,128)(2,1)S(1)}, u32[]{:S(2)}, u32[]{:S(2)}) async-start(bf16[16,64,128]{2,1,0:T(8,128)(2,1)} %shard_map.137.messages), calls=%async_computation.3 | async-start | bytes 524288 | tf_op jit(solution)/shard_map/all_to_all | solution.py:232
  79.5 3.9 %shard_map.138 = (f32[64,128]{1,0:T(8,128)S(1)}, bf16[3,64,128]{2,1,0:T(8,128)(2,1)}) custom-call(s32[1]{0:T(128)} %bitcast.core, bf16[80,128]{1,0:T(8,128)(2,1)S(1)} %fusion.4.packed, bf16[3,64,128]{2,1,0:T(8,128)(2,1)S(1)} %copy-done.1, s32[16,128]{1,0:T(8,128)S(1)} %copy-done.5, bf16[1296,128]{1,0:T(8,128)(2,1)S(1)} %collective-permute-done.2.received.near, ...), custom_call_target="tpu_custom_call" | custom-call | tf_op jit(solution)/shard_map/pallas_call | solution.py:65
  83.4 4.1 %all-to-all-done.3.arrived = bf16[16,64,128]{2,1,0:T(8,128)(2,1)S(1)} async-done(((bf16[16,64,128]{2,1,0:T(8,128)(2,1)}), bf16[16,64,128]{2,1,0:T(8,128)(2,1)S(1)}, u32[]{:S(2)}, u32[]{:S(2)}) %all-to-all-start.3) | async-done | bytes 262176 | tf_op jit(solution)/shard_map/all_to_all | solution.py:232
  87.5 0.6 shard_map.139
  (10 shorter events, 0.0 us)
Async XLA Ops:
  2.2 17.0 %all-to-all-start = ((bf16[16,80,128]{2,1,0:T(8,128)(2,1)}), bf16[16,80,128]{2,1,0:T(8,128)(2,1)S(1)}, u32[]{:S(2)}, u32[]{:S(2)}) async-start(bf16[16,80,128]{2,1,0:T(8,128)(2,1)} %broadcast_in_dim.3), calls=%async_computation | async-start | bytes 655360 | tf_op jit(solution)/shard_map/all_to_all | solution.py:232
  9.8 0.8 copy-start
  10.6 0.7 copy-start.6
  11.5 22.4 %collective-permute-start.1 = (bf16[272,128]{1,0:T(8,128)(2,1)S(1)}, bf16[272,128]{1,0:T(8,128)(2,1)S(1)}, u32[]{:S(2)}, u32[]{:S(2)}) collective-permute-start(bf16[272,128]{1,0:T(8,128)(2,1)S(1)} %get-tuple-element.11), channel_id=1, source_target_pairs={{1,2},{2,1},{3,4},{4,3},{5,6},{6,5},{7,8},{8,7},{9,10},{10,9},{11,... | collective-permute-start | bytes 208904 | tf_op jit(solution)/shard_map/ppermute | solution.py:237
  19.2 14.7 %collective-permute-start = (bf16[16,80,128]{2,1,0:T(8,128)(2,1)S(1)}, bf16[16,80,128]{2,1,0:T(8,128)(2,1)S(1)}, u32[]{:S(2)}, u32[]{:S(2)}) collective-permute-start(bf16[16,80,128]{2,1,0:T(8,128)(2,1)S(1)} %all-to-all-done.got), channel_id=1, source_target_pairs={{0,1},{1,0},{2,3},{3,2},{4,5},{5,4},{6,7},{7,6},{8,9},{9,8},{10,11... | collective-permute-start | bytes 983048 | tf_op jit(solution)/shard_map/ppermute | solution.py:237
  69.7 5.4 %collective-permute-start.2 = (bf16[1296,128]{1,0:T(8,128)(2,1)S(1)}, bf16[1296,128]{1,0:T(8,128)(2,1)S(1)}, u32[]{:S(2)}, u32[]{:S(2)}) collective-permute-start(bf16[1296,128]{1,0:T(8,128)(2,1)S(1)} %shard_map.136), channel_id=1, source_target_pairs={{0,1},{1,0},{2,3},{3,2},{4,5},{5,4},{6,7},{7,6},{8,9},{9,8},{10,11... | collective-permute-start | bytes 995336 | tf_op jit(solution)/shard_map/ppermute | solution.py:237
  73.9 5.6 %copy-start.1 = (bf16[3,64,128]{2,1,0:T(8,128)(2,1)S(1)}, bf16[3,64,128]{2,1,0:T(8,128)(2,1)}, u32[]{:S(2)}) copy-start(bf16[3,64,128]{2,1,0:T(8,128)(2,1)} %vec.3) | copy-start | bytes 147460
  73.9 5.6 %copy-start.2 = (bf16[64,192]{1,0:T(8,128)(2,1)S(1)}, bf16[64,192]{1,0:T(8,128)(2,1)}, u32[]{:S(2)}) copy-start(bf16[64,192]{1,0:T(8,128)(2,1)} %message_weight.1) | copy-start | bytes 73732
  73.9 5.6 %copy-start.3 = (bf16[64,64]{1,0:T(8,128)(2,1)S(1)}, bf16[64,64]{1,0:T(8,128)(2,1)}, u32[]{:S(2)}) copy-start(bf16[64,64]{1,0:T(8,128)(2,1)} %node_weight.1) | copy-start | bytes 24580
  73.9 5.6 %copy-start.4 = (bf16[20,192]{1,0:T(8,128)(2,1)S(1)}, bf16[20,192]{1,0:T(8,128)(2,1)}, u32[]{:S(2)}) copy-start(bf16[20,192]{1,0:T(8,128)(2,1)} %radial_weight.1) | copy-start | bytes 23044
  73.9 5.5 %copy-start.5 = (s32[16,128]{1,0:T(8,128)S(1)}, s32[16,128]{1,0:T(8,128)}, u32[]{:S(2)}) copy-start(s32[16,128]{1,0:T(8,128)} %ids.1) | copy-start | bytes 24580
  73.9 5.5 %copy-start.7 = (f32[64]{0:T(128)S(1)}, f32[64]{0:T(128)}, u32[]{:S(2)}) copy-start(f32[64]{0:T(128)} %param.20) | copy-start | bytes 772
  75.9 11.7 %all-to-all-start.3 = ((bf16[16,64,128]{2,1,0:T(8,128)(2,1)}), bf16[16,64,128]{2,1,0:T(8,128)(2,1)S(1)}, u32[]{:S(2)}, u32[]{:S(2)}) async-start(bf16[16,64,128]{2,1,0:T(8,128)(2,1)} %shard_map.137.messages), calls=%async_computation.3 | async-start | bytes 524288 | tf_op jit(solution)/shard_map/all_to_all | solution.py:232

commit v11 on v10

--- a/solution.py
+++ b/solution.py
@@ -93,10 +93,7 @@
         out[...] = dot(rows, chosen, ((1,), (0,))).astype(jnp.bfloat16)
 
 
-def add_atoms(got, constants, table, columns, total):
-    turned = constants[F:, :KDEV].T
-    for i in range(3):
-        columns[i] = jnp.broadcast_to(turned[:, i : i + 1], (KDEV, ATOM))
+def add_atoms(got, table, columns, total):
     for first in range(0, SAME, 2):
         both = jnp.concatenate([got[first], got[first + 1]], axis=1)
         pos = summed(both[F:].astype(jnp.float32))
@@ -118,14 +115,17 @@
             total[KDEV + k : KDEV + k + 64] += sums[64:]
 
 
-def own_table_kernel(got, constants, table, total, columns):
+def own_table_kernel(got, lattice, constants, table, total, columns):
+    turned = jnp.concatenate([lattice[...], jnp.zeros((5, KDEV), jnp.float32)], axis=0).T
+    for i in range(3):
+        columns[i] = jnp.broadcast_to(turned[:, i : i + 1], (KDEV, ATOM))
     total[...] = jnp.zeros_like(total)
-    add_atoms(got, constants, table, columns, total)
-
-
-def other_table_kernel(got, constants, own_total, far, table, partial, columns, total):
+    add_atoms(got, table, columns, total)
+
+
+def other_table_kernel(got, columns, own_total, far, table, partial, total):
     total[...] = own_total[...]
-    add_atoms(got, constants, table, columns, total)
+    add_atoms(got, table, columns, total)
     partial[...] = jnp.concatenate([total[:KDEV], total[KDEV:]], axis=1).astype(jnp.bfloat16)
 
 
@@ -138,14 +138,15 @@
         out[i] = total
 
 
-def filtered_sums(got, constants):
-    own, weight = constants[:F, :KDEV], constants[:F, KDEV:].astype(jnp.bfloat16)
+def filtered_sums(half, got, constants):
+    own = constants[:, pl.ds(pl.multiple_of(half[0], KDEV), KDEV)] * norm_scale
+    weight = constants[:, 2 * KDEV :].astype(jnp.bfloat16)
     total = [dot(weight, got[:, part * F : (part + 1) * F], ((0,), (1,))) for part in range(2)]
     return jnp.concatenate([own * total[0], own * total[1]], axis=1).astype(jnp.bfloat16)
 
 
-def project_other_kernel(got, constants, table, near, out):
-    filtered = filtered_sums(got, constants)
+def project_other_kernel(half, got, constants, table, near, out):
+    filtered = filtered_sums(half, got, constants)
     for first in range(0, SAME, 8):
         message = dot(filtered, table[:, first * ATOM : (first + 8) * ATOM], ((1,), (0,))).astype(jnp.bfloat16)
         for p in range(8):
@@ -153,8 +154,8 @@
     out[SAME * F :] = near[...]
 
 
-def project_own_kernel(got, constants, table, out):
-    filtered = filtered_sums(got, constants)
+def project_own_kernel(half, got, constants, table, out):
+    filtered = filtered_sums(half, got, constants)
     for first in range(0, SAME, 8):
         message = dot(filtered, table[:, first * ATOM : (first + 8) * ATOM], ((1,), (0,)))
         for p in range(8):
@@ -249,41 +250,40 @@
     own = exchanged(jnp.broadcast_to(packed, (SAME, PACK, ATOM)), same_axes)
     other = swapped(own, 0)
     own_lattice = lax.dynamic_slice_in_dim(lattice, k_at, KDEV, 1).astype(f32)
-    own_filter = lax.dynamic_slice_in_dim(kspace_filter, half_at, KDEV, 1) * norm_scale
-    constants = jnp.pad(own_filter, ((0, 8), (0, F))) + jnp.pad(own_lattice, ((F, 5), (0, F)))
-    constants = constants + jnp.pad(ewald_weight.astype(f32), ((0, 8), (KDEV, 0)))
+    constants = jnp.pad(kspace_filter, ((0, 0), (0, F)))
+    constants = constants + jnp.pad(ewald_weight.astype(f32), ((0, 0), (2 * KDEV, 0)))
+    half = half_at.astype(jnp.int32).reshape(1)
     core = lax.axis_index("c").astype(jnp.int32).reshape(1)
     halo = shape((HALO_ROWS, ATOM), bf16)
     far, near = call(halo_kernel, [SM, VM, VM, VM], (halo, halo), core, packed, vectors, halo_lists)
     far = swapped(far, 1)
     half_table = shape((2 * KDEV, SAME * ATOM), bf16)
-    own_table, own_total = call(
+    own_table, own_total, columns = call(
         own_table_kernel,
-        [VM, VM],
-        (half_table, shape((2 * KDEV, F), f32)),
-        own, constants,
-        scratch=[VM((3, KDEV, ATOM), f32)],
-        flops=3 * 10**9,
+        [VM, VM, ANY],
+        (half_table, shape((2 * KDEV, F), f32), shape((3, KDEV, ATOM), f32)),
+        own, own_lattice, constants,
+        flops=37 * 10**8,
     )
     other_table, partial = call(
         other_table_kernel,
         [VM, VM, VM, ANY],
         (half_table, shape((KDEV, 2 * F), bf16)),
-        other, constants, own_total, far,
-        scratch=[VM((3, KDEV, ATOM), f32), VM((2 * KDEV, F), f32)],
+        other, columns, own_total, far,
+        scratch=[VM((2 * KDEV, F), f32)],
     )
     arrived = exchanged(partial.reshape(DEPTH, KDEV // DEPTH, 2 * F), "z")
     owned = call(sum_kernel, [VM], shape((DEPTH, KDEV // DEPTH, 2 * F), bf16), arrived)
     totals = exchanged(owned, "z").reshape(KDEV, 2 * F)
     for_other = call(
         project_other_kernel,
-        [VM] * 4,
+        [SM] + [VM] * 4,
         shape((SAME * F + HALO_ROWS, ATOM), bf16),
-        totals, constants, other_table, near,
+        half, totals, constants, other_table, near,
     )
     received = swapped(for_other, 0)
     own_messages = call(
-        project_own_kernel, [VM] * 3, shape((SAME, F, ATOM), f32), totals, constants, own_table,
+        project_own_kernel, [SM] + [VM] * 3, shape((SAME, F, ATOM), f32), half, totals, constants, own_table,
         flops=10**9,
     )
     messages = call(join_kernel, [VM] * 2, shape((SAME, F, ATOM), bf16), own_messages, received)

time: 88.9 us -> 88 us (0.990)
  transfers between devices with their start and end apart: 5 -> 5, of which waited for: 2 -> 2; matrix products, arithmetic and copies ran while one was open for 3% -> 2% of each run, Pallas kernels for 8% -> 8%
where the time goes in v11:
time: 88 us; the launch traced here: 87.4 us
  starting transfers between devices  33.2 us (38%)
  blocking collectives  32.8 us (37%)
  Pallas kernels  11.3 us (13%)
  waiting for transfers between devices  4.67 us (5%)
  other arithmetic  2.42 us (3%)
  local copies, waits for them, and re-layouts  2.28 us (3%)
    all_to_all x2, blocking collectives, exchanged(): return lax.all_to_all(x, axes, split_axis=0, concat_axis=0, tiled=True)  32.8 us
    ppermute x3, starting transfers between devices, swapped(): return lax.ppermute(x, all_axes, pairs)  22 us
    pallas_call x9, Pallas kernels, call(): pl.pallas_call(kernel, out_shape=outs, in_specs=[pl.BlockSpec(memory_spac...  11.3 us
    all_to_all x2, starting transfers between devices, exchanged(): return lax.all_to_all(x, axes, split_axis=0, concat_axis=0, tiled=True)  11.2 us
    all_to_all x2, waiting for transfers between devices, exchanged(): return lax.all_to_all(x, axes, split_axis=0, concat_axis=0, tiled=True)  4.14 us
  transfers between devices with their start and end apart: 5, of which 2 were waited for; matrix products, arithmetic and copies ran while one was open for 2% of the time, Pallas kernels for 8%

profile of v11, /device:TPU:1, one launch (start us, length us, event | category | flops | bytes accessed | tf_op | source)
XLA Modules:
  0.0 87.4 jit_solution(8327990349354338395)
XLA Ops:
  0.6 0.8 fusion.4.packed
  1.4 0.8 broadcast_in_dim.3
  2.2 7.6 %all-to-all-start = ((bf16[16,80,128]{2,1,0:T(8,128)(2,1)}), bf16[16,80,128]{2,1,0:T(8,128)(2,1)S(1)}, u32[]{:S(2)}, u32[]{:S(2)}) async-start(bf16[16,80,128]{2,1,0:T(8,128)(2,1)} %broadcast_in_dim.3), calls=%async_computation | async-start | bytes 655360 | tf_op jit(solution)/shard_map/all_to_all | solution.py:233
  9.8 0.0 copy-start
  9.8 0.8 copy-done
  10.6 0.7 copy-done.6
  11.3 0.2 shard_map.132
  11.5 6.2 %collective-permute-start.1 = (bf16[272,128]{1,0:T(8,128)(2,1)S(1)}, bf16[272,128]{1,0:T(8,128)(2,1)S(1)}, u32[]{:S(2)}, u32[]{:S(2)}) collective-permute-start(bf16[272,128]{1,0:T(8,128)(2,1)S(1)} %get-tuple-element.13), channel_id=1, source_target_pairs={{1,2},{2,1},{3,4},{4,3},{5,6},{6,5},{7,8},{8,7},{9,10},{10,9},{11,... | collective-permute-start | bytes 208904 | tf_op jit(solution)/shard_map/ppermute | solution.py:238
  17.7 0.7 dynamic-slice_convert_fusion.lattice
  18.4 0.9 %convert_add_fusion.constants = f32[64,576]{1,0:T(8,128)S(1)} fusion(f32[64,512]{1,0:T(8,128)} %param.18, bf16[64,64]{1,0:T(8,128)(2,1)} %param.23), kind=kLoop, calls=%fused_computation | loop fusion | flops 73728 | bytes 286720 | tf_op jit(solution)/shard_map/add | solution.py:254
  19.3 0.0 all-to-all-done.got
  19.3 11.7 %collective-permute-start = (bf16[16,80,128]{2,1,0:T(8,128)(2,1)S(1)}, bf16[16,80,128]{2,1,0:T(8,128)(2,1)S(1)}, u32[]{:S(2)}, u32[]{:S(2)}) collective-permute-start(bf16[16,80,128]{2,1,0:T(8,128)(2,1)S(1)} %all-to-all-done.got), channel_id=1, source_target_pairs={{0,1},{1,0},{2,3},{3,2},{4,5},{5,4},{6,7},{7,6},{8,9},{9,8},{10,11... | collective-permute-start | bytes 983048 | tf_op jit(solution)/shard_map/ppermute | solution.py:238
  31.0 2.3 %shard_map.131 = (bf16[512,2048]{1,0:T(8,128)(2,1)S(1)}, f32[512,64]{1,0:T(8,128)S(1)}, f32[3,256,128]{2,1,0:T(8,128)S(1)}) custom-call(bf16[16,80,128]{2,1,0:T(8,128)(2,1)S(1)} %all-to-all-done.got, f32[3,256]{1,0:T(4,128)S(1)} %dynamic-slice_convert_fusion.lattice, f32[64,576]{1,0:T(8,128)S(1)} %convert_add_fusion.constants), custom_call_target="tpu_custom_call" | custom-call | flops 3700000000 | tf_op jit(solution)/shard_map/pallas_call | solution.py:65
  33.2 0.0 collective-permute-done.1.far
  33.3 2.2 %shard_map.133 = (bf16[512,2048]{1,0:T(8,128)(2,1)S(1)}, bf16[256,128]{1,0:T(8,128)(2,1)S(1)}) custom-call(bf16[16,80,128]{2,1,0:T(8,128)(2,1)S(1)} %collective-permute-done.got, f32[3,256,128]{2,1,0:T(8,128)S(1)} %get-tuple-element.11.columns, f32[512,64]{1,0:T(8,128)S(1)} %get-tuple-element.12.own_total, bf16[272,128]{1,0:T(8,128)(2,1)S(1)} %collective-permute-done.1.far), custom_call_target="tpu_custom_call" | custom-call | tf_op jit(solution)/shard_map/pallas_call | solution.py:65
  35.4 17.4 %all_to_all.20.arrived = bf16[16,16,128]{2,1,0:T(8,128)(2,1)S(1)} all-to-all(bf16[16,16,128]{2,1,0:T(8,128)(2,1)S(1)} %bitcast.7), channel_id=1, replica_groups=mesh['yh'=2,'z'=16,'yl'=2,'x'=4,'c'=2] {'z'}, dimensions={0} | all-to-all | bytes 131072 | tf_op jit(solution)/shard_map/all_to_all | solution.py:233
  52.9 15.3 %all_to_all.21 = bf16[16,16,128]{2,1,0:T(8,128)(2,1)S(1)} all-to-all(bf16[16,16,128]{2,1,0:T(8,128)(2,1)S(1)} %shard_map.134), channel_id=1, replica_groups=mesh['yh'=2,'z'=16,'yl'=2,'x'=4,'c'=2] {'z'}, dimensions={0} | all-to-all | bytes 131072 | tf_op jit(solution)/shard_map/all_to_all | solution.py:233
  68.2 0.6 shard_map.136
  68.9 4.1 %collective-permute-start.2 = (bf16[1296,128]{1,0:T(8,128)(2,1)S(1)}, bf16[1296,128]{1,0:T(8,128)(2,1)S(1)}, u32[]{:S(2)}, u32[]{:S(2)}) collective-permute-start(bf16[1296,128]{1,0:T(8,128)(2,1)S(1)} %shard_map.136), channel_id=1, source_target_pairs={{0,1},{1,0},{2,3},{3,2},{4,5},{5,4},{6,7},{7,6},{8,9},{9,8},{10,11... | collective-permute-start | bytes 995336 | tf_op jit(solution)/shard_map/ppermute | solution.py:238
  73.0 0.0 copy-start.1
  73.0 0.0 copy-start.2
  73.0 0.0 copy-start.3
  73.1 0.0 copy-start.4
  73.1 0.0 copy-start.5
  73.1 0.0 copy-start.7
  73.1 0.6 shard_map.135.own
  73.7 0.5 collective-permute-done.2.received.near
  74.3 0.8 shard_map.137.messages
  75.0 3.6 %all-to-all-start.3 = ((bf16[16,64,128]{2,1,0:T(8,128)(2,1)}), bf16[16,64,128]{2,1,0:T(8,128)(2,1)S(1)}, u32[]{:S(2)}, u32[]{:S(2)}) async-start(bf16[16,64,128]{2,1,0:T(8,128)(2,1)} %shard_map.137.messages), calls=%async_computation.3 | async-start | bytes 524288 | tf_op jit(solution)/shard_map/all_to_all | solution.py:233
  78.7 3.9 %shard_map.138 = (f32[64,128]{1,0:T(8,128)S(1)}, bf16[3,64,128]{2,1,0:T(8,128)(2,1)}) custom-call(s32[1]{0:T(128)} %bitcast.1.core, bf16[80,128]{1,0:T(8,128)(2,1)S(1)} %fusion.4.packed, bf16[3,64,128]{2,1,0:T(8,128)(2,1)S(1)} %copy-done.1, s32[16,128]{1,0:T(8,128)S(1)} %copy-done.5, bf16[1296,128]{1,0:T(8,128)(2,1)S(1)} %collective-permute-done.2.received.near, ...), custom_call_target="tpu_custom_call" | custom-call | tf_op jit(solution)/shard_map/pallas_call | solution.py:65
  82.6 4.1 %all-to-all-done.3.arrived = bf16[16,64,128]{2,1,0:T(8,128)(2,1)S(1)} async-done(((bf16[16,64,128]{2,1,0:T(8,128)(2,1)}), bf16[16,64,128]{2,1,0:T(8,128)(2,1)S(1)}, u32[]{:S(2)}, u32[]{:S(2)}) %all-to-all-start.3) | async-done | bytes 262176 | tf_op jit(solution)/shard_map/all_to_all | solution.py:233
  86.8 0.6 shard_map.139
  (9 shorter events, 0.0 us)
Async XLA Ops:
  2.2 17.1 %all-to-all-start = ((bf16[16,80,128]{2,1,0:T(8,128)(2,1)}), bf16[16,80,128]{2,1,0:T(8,128)(2,1)S(1)}, u32[]{:S(2)}, u32[]{:S(2)}) async-start(bf16[16,80,128]{2,1,0:T(8,128)(2,1)} %broadcast_in_dim.3), calls=%async_computation | async-start | bytes 655360 | tf_op jit(solution)/shard_map/all_to_all | solution.py:233
  9.8 0.8 copy-start
  10.6 0.7 copy-start.6
  11.5 21.7 %collective-permute-start.1 = (bf16[272,128]{1,0:T(8,128)(2,1)S(1)}, bf16[272,128]{1,0:T(8,128)(2,1)S(1)}, u32[]{:S(2)}, u32[]{:S(2)}) collective-permute-start(bf16[272,128]{1,0:T(8,128)(2,1)S(1)} %get-tuple-element.13), channel_id=1, source_target_pairs={{1,2},{2,1},{3,4},{4,3},{5,6},{6,5},{7,8},{8,7},{9,10},{10,9},{11,... | collective-permute-start | bytes 208904 | tf_op jit(solution)/shard_map/ppermute | solution.py:238
  19.3 14.0 %collective-permute-start = (bf16[16,80,128]{2,1,0:T(8,128)(2,1)S(1)}, bf16[16,80,128]{2,1,0:T(8,128)(2,1)S(1)}, u32[]{:S(2)}, u32[]{:S(2)}) collective-permute-start(bf16[16,80,128]{2,1,0:T(8,128)(2,1)S(1)} %all-to-all-done.got), channel_id=1, source_target_pairs={{0,1},{1,0},{2,3},{3,2},{4,5},{5,4},{6,7},{7,6},{8,9},{9,8},{10,11... | collective-permute-start | bytes 983048 | tf_op jit(solution)/shard_map/ppermute | solution.py:238
  68.9 5.4 %collective-permute-start.2 = (bf16[1296,128]{1,0:T(8,128)(2,1)S(1)}, bf16[1296,128]{1,0:T(8,128)(2,1)S(1)}, u32[]{:S(2)}, u32[]{:S(2)}) collective-permute-start(bf16[1296,128]{1,0:T(8,128)(2,1)S(1)} %shard_map.136), channel_id=1, source_target_pairs={{0,1},{1,0},{2,3},{3,2},{4,5},{5,4},{6,7},{7,6},{8,9},{9,8},{10,11... | collective-permute-start | bytes 995336 | tf_op jit(solution)/shard_map/ppermute | solution.py:238
  73.0 5.6 %copy-start.1 = (bf16[3,64,128]{2,1,0:T(8,128)(2,1)S(1)}, bf16[3,64,128]{2,1,0:T(8,128)(2,1)}, u32[]{:S(2)}) copy-start(bf16[3,64,128]{2,1,0:T(8,128)(2,1)} %vec.3) | copy-start | bytes 147460
  73.0 5.6 %copy-start.2 = (bf16[64,192]{1,0:T(8,128)(2,1)S(1)}, bf16[64,192]{1,0:T(8,128)(2,1)}, u32[]{:S(2)}) copy-start(bf16[64,192]{1,0:T(8,128)(2,1)} %message_weight.1) | copy-start | bytes 73732
  73.0 5.6 %copy-start.3 = (bf16[64,64]{1,0:T(8,128)(2,1)S(1)}, bf16[64,64]{1,0:T(8,128)(2,1)}, u32[]{:S(2)}) copy-start(bf16[64,64]{1,0:T(8,128)(2,1)} %node_weight.1) | copy-start | bytes 24580
  73.1 5.6 %copy-start.4 = (bf16[20,192]{1,0:T(8,128)(2,1)S(1)}, bf16[20,192]{1,0:T(8,128)(2,1)}, u32[]{:S(2)}) copy-start(bf16[20,192]{1,0:T(8,128)(2,1)} %radial_weight.1) | copy-start | bytes 23044
  73.1 5.6 %copy-start.5 = (s32[16,128]{1,0:T(8,128)S(1)}, s32[16,128]{1,0:T(8,128)}, u32[]{:S(2)}) copy-start(s32[16,128]{1,0:T(8,128)} %ids.1) | copy-start | bytes 24580
  73.1 5.6 %copy-start.7 = (f32[64]{0:T(128)S(1)}, f32[64]{0:T(128)}, u32[]{:S(2)}) copy-start(f32[64]{0:T(128)} %param.20) | copy-start | bytes 772
  75.0 11.7 %all-to-all-start.3 = ((bf16[16,64,128]{2,1,0:T(8,128)(2,1)}), bf16[16,64,128]{2,1,0:T(8,128)(2,1)S(1)}, u32[]{:S(2)}, u32[]{:S(2)}) async-start(bf16[16,64,128]{2,1,0:T(8,128)(2,1)} %shard_map.137.messages), calls=%async_computation.3 | async-start | bytes 524288 | tf_op jit(solution)/shard_map/all_to_all | solution.py:233

commit v12 on v11

--- a/solution.py
+++ b/solution.py
@@ -15,6 +15,7 @@
 KDEV = 256
 PLANE = 32
 SAME = 16
+KB = 16
 DEPTH = 16
 SLABS = 512
 KVEC = 8192
@@ -175,7 +176,7 @@
 
 
 def short_kernel(
-    core, packed, vec, ids, near, far, node_weight, bias, message_weight, radial_weight, messages,
+    core, packed, vec, ids, near, far_within, far_across, node_weight, bias, message_weight, radial_weight, messages,
     scalar_out, vector_out, feats, ext, chosen, filters, directions,
 ):
     pos = summed(packed[F:].astype(jnp.float32))
@@ -184,6 +185,7 @@
     ext[384:, :ATOM] = packed[F:]
     near_at = pl.ds(pl.multiple_of((2 - core[0]) * ATOM, ATOM), ATOM)
     far_at = pl.ds(pl.multiple_of((1 + core[0]) * ATOM, ATOM), ATOM)
+    far = far_within[...] + far_across[...]
     for side, start, at in ((near, SAME * F, near_at), (far, 0, far_at)):
         feats[:, at] = side[start : start + F]
         ext[192:384, at] = side[start + PACK : start + HALO_ROWS]
@@ -233,8 +235,10 @@
     return lax.all_to_all(x, axes, split_axis=0, concat_axis=0, tiled=True)
 
 
-def swapped(x, first):
+def swapped(x, first, within=None):
     pairs = [((first + i) % SLABS, (first + (i ^ 1)) % SLABS) for i in range(SLABS)]
+    if within is not None:
+        pairs = [(a, b) for a, b in pairs if (a // KB == b // KB) == within]
     return lax.ppermute(x, all_axes, pairs)
 
 
@@ -256,7 +260,7 @@
     core = lax.axis_index("c").astype(jnp.int32).reshape(1)
     halo = shape((HALO_ROWS, ATOM), bf16)
     far, near = call(halo_kernel, [SM, VM, VM, VM], (halo, halo), core, packed, vectors, halo_lists)
-    far = swapped(far, 1)
+    far_within, far_across = swapped(far, 1, True), swapped(far, 1, False)
     half_table = shape((2 * KDEV, SAME * ATOM), bf16)
     own_table, own_total, columns = call(
         own_table_kernel,
@@ -269,7 +273,7 @@
         other_table_kernel,
         [VM, VM, VM, ANY],
         (half_table, shape((KDEV, 2 * F), bf16)),
-        other, columns, own_total, far,
+        other, columns, own_total, far_within,
         scratch=[VM((2 * KDEV, F), f32)],
     )
     arrived = exchanged(partial.reshape(DEPTH, KDEV // DEPTH, 2 * F), "z")
@@ -290,9 +294,9 @@
     returned = exchanged(messages, same_axes)
     scalar, new_vectors = call(
         short_kernel,
-        [SM] + [VM] * 9 + [ANY],
+        [SM] + [VM] * 10 + [ANY],
         (shape((F, ATOM), f32), shape((3, F, ATOM), bf16)),
-        core, packed, vectors, neighbours, received, far,
+        core, packed, vectors, neighbours, received, far_within, far_across,
         node_weight, node_bias.reshape(1, F), message_weight, radial_weight, messages,
         scratch=[
             VM((F, 3 * ATOM), bf16),

time: 88 us -> 93.1 us (1.058)
  the two profiles are of different devices: /device:TPU:1 before, /device:TPU:16 now
where the time goes in v12:
time: 93.1 us; the launch traced here: 92.5 us
  blocking collectives  42.1 us (45%)
  starting transfers between devices  25.2 us (27%)
  Pallas kernels  11.3 us (12%)
  waiting for transfers between devices  8.44 us (9%)
  other arithmetic  2.42 us (3%)
  local copies, waits for them, and re-layouts  2.28 us (2%)
    all_to_all x2, blocking collectives, exchanged(): return lax.all_to_all(x, axes, split_axis=0, concat_axis=0, tiled=True)  42.1 us
    all_to_all x2, starting transfers between devices, exchanged(): return lax.all_to_all(x, axes, split_axis=0, concat_axis=0, tiled=True)  15.6 us
    pallas_call x9, Pallas kernels, call(): pl.pallas_call(kernel, out_shape=outs, in_specs=[pl.BlockSpec(memory_spac...  11.3 us
    ppermute x4, starting transfers between devices, swapped(): return lax.ppermute(x, all_axes, pairs)  9.6 us
    ppermute x4, waiting for transfers between devices, swapped(): return lax.ppermute(x, all_axes, pairs)  6 us
    all_to_all x2, waiting for transfers between devices, exchanged(): return lax.all_to_all(x, axes, split_axis=0, concat_axis=0, tiled=True)  2.45 us
  transfers between devices with their start and end apart: 6, of which 3 were waited for; matrix products, arithmetic and copies ran while one was open for 2% of the time, Pallas kernels for 8%

profile of v12, /device:TPU:16, one launch (start us, length us, event | category | flops | bytes accessed | tf_op | source)
XLA Modules:
  0.0 92.5 jit_solution(6349157211236436472)
XLA Ops:
  0.6 0.8 fusion.4.packed
  1.4 0.8 broadcast_in_dim.3
  2.2 9.1 %all-to-all-start = ((bf16[16,80,128]{2,1,0:T(8,128)(2,1)}), bf16[16,80,128]{2,1,0:T(8,128)(2,1)S(1)}, u32[]{:S(2)}, u32[]{:S(2)}) async-start(bf16[16,80,128]{2,1,0:T(8,128)(2,1)} %broadcast_in_dim.3), calls=%async_computation | async-start | bytes 655360 | tf_op jit(solution)/shard_map/all_to_all | solution.py:235
  11.3 0.8 copy-done
  12.1 0.7 copy-done.6
  12.8 0.2 shard_map.132
  13.0 0.7 collective-permute-start.1
  13.7 0.7 dynamic-slice_convert_fusion.lattice
  14.4 0.9 convert_add_fusion.constants
  15.3 2.4 %all-to-all-done.got = bf16[16,80,128]{2,1,0:T(8,128)(2,1)S(1)} async-done(((bf16[16,80,128]{2,1,0:T(8,128)(2,1)}), bf16[16,80,128]{2,1,0:T(8,128)(2,1)S(1)}, u32[]{:S(2)}, u32[]{:S(2)}) %all-to-all-start) | async-done | bytes 327712 | tf_op jit(solution)/shard_map/all_to_all | solution.py:235
  17.7 2.3 %collective-permute-start = (bf16[16,80,128]{2,1,0:T(8,128)(2,1)S(1)}, bf16[16,80,128]{2,1,0:T(8,128)(2,1)S(1)}, u32[]{:S(2)}, u32[]{:S(2)}) collective-permute-start(bf16[16,80,128]{2,1,0:T(8,128)(2,1)S(1)} %all-to-all-done.got), channel_id=1, source_target_pairs={{0,1},{1,0},{2,3},{3,2},{4,5},{5,4},{6,7},{7,6},{8,9},{9,8},{10,11... | collective-permute-start | bytes 983048 | tf_op jit(solution)/shard_map/ppermute | solution.py:242
  20.0 2.3 %shard_map.131 = (bf16[512,2048]{1,0:T(8,128)(2,1)S(1)}, f32[512,64]{1,0:T(8,128)S(1)}, f32[3,256,128]{2,1,0:T(8,128)S(1)}) custom-call(bf16[16,80,128]{2,1,0:T(8,128)(2,1)S(1)} %all-to-all-done.got, f32[3,256]{1,0:T(4,128)S(1)} %dynamic-slice_convert_fusion.lattice, f32[64,576]{1,0:T(8,128)S(1)} %convert_add_fusion.constants), custom_call_target="tpu_custom_call" | custom-call | flops 3700000000 | tf_op jit(solution)/shard_map/pallas_call | solution.py:66
  22.3 0.0 collective-permute-done.1.far.far_within
  22.3 2.2 %shard_map.133 = (bf16[512,2048]{1,0:T(8,128)(2,1)S(1)}, bf16[256,128]{1,0:T(8,128)(2,1)S(1)}) custom-call(bf16[16,80,128]{2,1,0:T(8,128)(2,1)S(1)} %collective-permute-done.got, f32[3,256,128]{2,1,0:T(8,128)S(1)} %get-tuple-element.11.columns, f32[512,64]{1,0:T(8,128)S(1)} %get-tuple-element.12.own_total, ...), custom_call_target="tpu_custom_call" | custom-call | tf_op jit(solution)/shard_map/pallas_call | solution.py:66
  24.5 26.6 %all_to_all.20.arrived = bf16[16,16,128]{2,1,0:T(8,128)(2,1)S(1)} all-to-all(bf16[16,16,128]{2,1,0:T(8,128)(2,1)S(1)} %bitcast.7), channel_id=1, replica_groups=mesh['yh'=2,'z'=16,'yl'=2,'x'=4,'c'=2] {'z'}, dimensions={0} | all-to-all | bytes 131072 | tf_op jit(solution)/shard_map/all_to_all | solution.py:235
  51.1 15.5 %all_to_all.21 = bf16[16,16,128]{2,1,0:T(8,128)(2,1)S(1)} all-to-all(bf16[16,16,128]{2,1,0:T(8,128)(2,1)S(1)} %shard_map.134), channel_id=1, replica_groups=mesh['yh'=2,'z'=16,'yl'=2,'x'=4,'c'=2] {'z'}, dimensions={0} | all-to-all | bytes 131072 | tf_op jit(solution)/shard_map/all_to_all | solution.py:235
  66.6 0.6 shard_map.136
  67.3 1.9 %collective-permute-start.2 = (bf16[1296,128]{1,0:T(8,128)(2,1)S(1)}, bf16[1296,128]{1,0:T(8,128)(2,1)S(1)}, u32[]{:S(2)}, u32[]{:S(2)}) collective-permute-start(bf16[1296,128]{1,0:T(8,128)(2,1)S(1)} %shard_map.136), channel_id=1, source_target_pairs={{0,1},{1,0},{2,3},{3,2},{4,5},{5,4},{6,7},{7,6},{8,9},{9,8},{10,11... | collective-permute-start | bytes 995336 | tf_op jit(solution)/shard_map/ppermute | solution.py:242
  69.2 0.0 copy-start.1
  69.2 0.0 copy-start.2
  69.2 0.0 copy-start.3
  69.2 0.0 copy-start.4
  69.2 0.0 copy-start.5
  69.2 0.0 copy-start.7
  69.3 0.6 shard_map.135.own
  69.9 0.9 collective-permute-done.2.received.near
  70.8 0.7 shard_map.137.messages
  71.5 6.5 %all-to-all-start.3 = ((bf16[16,64,128]{2,1,0:T(8,128)(2,1)}), bf16[16,64,128]{2,1,0:T(8,128)(2,1)S(1)}, u32[]{:S(2)}, u32[]{:S(2)}) async-start(bf16[16,64,128]{2,1,0:T(8,128)(2,1)} %shard_map.137.messages), calls=%async_computation.3 | async-start | bytes 524288 | tf_op jit(solution)/shard_map/all_to_all | solution.py:235
  78.0 4.7 %collective-permute-start.3 = (bf16[272,128]{1,0:T(8,128)(2,1)S(1)}, bf16[272,128]{1,0:T(8,128)(2,1)S(1)}, u32[]{:S(2)}, u32[]{:S(2)}) collective-permute-start(bf16[272,128]{1,0:T(8,128)(2,1)S(1)} %get-tuple-element.13), channel_id=1, source_target_pairs={{15,16},{16,15},{31,32},{32,31},{47,48},{48,47},{63,64},{64,63},{7... | collective-permute-start | bytes 208904 | tf_op jit(solution)/shard_map/ppermute | solution.py:242
  82.7 5.1 %collective-permute-done.3.far_across = bf16[272,128]{1,0:T(8,128)(2,1)S(1)} collective-permute-done((bf16[272,128]{1,0:T(8,128)(2,1)S(1)}, bf16[272,128]{1,0:T(8,128)(2,1)S(1)}, u32[]{:S(2)}, u32[]{:S(2)}) %collective-permute-start.3) | collective-permute-done | bytes 69664 | tf_op jit(solution)/shard_map/ppermute | solution.py:242
  87.9 3.9 %shard_map.138 = (f32[64,128]{1,0:T(8,128)S(1)}, bf16[3,64,128]{2,1,0:T(8,128)(2,1)}) custom-call(s32[1]{0:T(128)} %bitcast.1.core, bf16[80,128]{1,0:T(8,128)(2,1)S(1)} %fusion.4.packed, bf16[3,64,128]{2,1,0:T(8,128)(2,1)S(1)} %copy-done.1, s32[16,128]{1,0:T(8,128)S(1)} %copy-done.5, bf16[1296,128]{1,0:T(8,128)(2,1)S(1)} %collective-permute-done.2.received.near, ...), custom_call_target="tpu_custom_call" | custom-call | tf_op jit(solution)/shard_map/pallas_call | solution.py:66
  91.8 0.6 shard_map.139
  (11 shorter events, 0.0 us)
Async XLA Ops:
  2.2 15.5 %all-to-all-start = ((bf16[16,80,128]{2,1,0:T(8,128)(2,1)}), bf16[16,80,128]{2,1,0:T(8,128)(2,1)S(1)}, u32[]{:S(2)}, u32[]{:S(2)}) async-start(bf16[16,80,128]{2,1,0:T(8,128)(2,1)} %broadcast_in_dim.3), calls=%async_computation | async-start | bytes 655360 | tf_op jit(solution)/shard_map/all_to_all | solution.py:235
  11.3 0.8 copy-start
  12.1 0.7 copy-start.6
  13.0 9.3 %collective-permute-start.1 = (bf16[272,128]{1,0:T(8,128)(2,1)S(1)}, bf16[272,128]{1,0:T(8,128)(2,1)S(1)}, u32[]{:S(2)}, u32[]{:S(2)}) collective-permute-start(bf16[272,128]{1,0:T(8,128)(2,1)S(1)} %get-tuple-element.13), channel_id=1, source_target_pairs={{1,2},{2,1},{3,4},{4,3},{5,6},{6,5},{7,8},{8,7},{9,10},{10,9},{11,... | collective-permute-start | bytes 208904 | tf_op jit(solution)/shard_map/ppermute | solution.py:242
  17.7 4.6 %collective-permute-start = (bf16[16,80,128]{2,1,0:T(8,128)(2,1)S(1)}, bf16[16,80,128]{2,1,0:T(8,128)(2,1)S(1)}, u32[]{:S(2)}, u32[]{:S(2)}) collective-permute-start(bf16[16,80,128]{2,1,0:T(8,128)(2,1)S(1)} %all-to-all-done.got), channel_id=1, source_target_pairs={{0,1},{1,0},{2,3},{3,2},{4,5},{5,4},{6,7},{7,6},{8,9},{9,8},{10,11... | collective-permute-start | bytes 983048 | tf_op jit(solution)/shard_map/ppermute | solution.py:242
  67.3 3.5 %collective-permute-start.2 = (bf16[1296,128]{1,0:T(8,128)(2,1)S(1)}, bf16[1296,128]{1,0:T(8,128)(2,1)S(1)}, u32[]{:S(2)}, u32[]{:S(2)}) collective-permute-start(bf16[1296,128]{1,0:T(8,128)(2,1)S(1)} %shard_map.136), channel_id=1, source_target_pairs={{0,1},{1,0},{2,3},{3,2},{4,5},{5,4},{6,7},{7,6},{8,9},{9,8},{10,11... | collective-permute-start | bytes 995336 | tf_op jit(solution)/shard_map/ppermute | solution.py:242
  69.2 18.7 %copy-start.1 = (bf16[3,64,128]{2,1,0:T(8,128)(2,1)S(1)}, bf16[3,64,128]{2,1,0:T(8,128)(2,1)}, u32[]{:S(2)}) copy-start(bf16[3,64,128]{2,1,0:T(8,128)(2,1)} %vec.3) | copy-start | bytes 147460
  69.2 18.7 %copy-start.2 = (bf16[64,192]{1,0:T(8,128)(2,1)S(1)}, bf16[64,192]{1,0:T(8,128)(2,1)}, u32[]{:S(2)}) copy-start(bf16[64,192]{1,0:T(8,128)(2,1)} %message_weight.1) | copy-start | bytes 73732
  69.2 18.6 %copy-start.3 = (bf16[64,64]{1,0:T(8,128)(2,1)S(1)}, bf16[64,64]{1,0:T(8,128)(2,1)}, u32[]{:S(2)}) copy-start(bf16[64,64]{1,0:T(8,128)(2,1)} %node_weight.1) | copy-start | bytes 24580
  69.2 18.6 %copy-start.4 = (bf16[20,192]{1,0:T(8,128)(2,1)S(1)}, bf16[20,192]{1,0:T(8,128)(2,1)}, u32[]{:S(2)}) copy-start(bf16[20,192]{1,0:T(8,128)(2,1)} %radial_weight.1) | copy-start | bytes 23044
  69.2 18.6 %copy-start.5 = (s32[16,128]{1,0:T(8,128)S(1)}, s32[16,128]{1,0:T(8,128)}, u32[]{:S(2)}) copy-start(s32[16,128]{1,0:T(8,128)} %ids.1) | copy-start | bytes 24580
  69.2 18.6 %copy-start.7 = (f32[64]{0:T(128)S(1)}, f32[64]{0:T(128)}, u32[]{:S(2)}) copy-start(f32[64]{0:T(128)} %param.20) | copy-start | bytes 772
  71.5 20.3 %all-to-all-start.3 = ((bf16[16,64,128]{2,1,0:T(8,128)(2,1)}), bf16[16,64,128]{2,1,0:T(8,128)(2,1)S(1)}, u32[]{:S(2)}, u32[]{:S(2)}) async-start(bf16[16,64,128]{2,1,0:T(8,128)(2,1)} %shard_map.137.messages), calls=%async_computation.3 | async-start | bytes 524288 | tf_op jit(solution)/shard_map/all_to_all | solution.py:235
  78.0 9.8 %collective-permute-start.3 = (bf16[272,128]{1,0:T(8,128)(2,1)S(1)}, bf16[272,128]{1,0:T(8,128)(2,1)S(1)}, u32[]{:S(2)}, u32[]{:S(2)}) collective-permute-start(bf16[272,128]{1,0:T(8,128)(2,1)S(1)} %get-tuple-element.13), channel_id=1, source_target_pairs={{15,16},{16,15},{31,32},{32,31},{47,48},{48,47},{63,64},{64,63},{7... | collective-permute-start | bytes 208904 | tf_op jit(solution)/shard_map/ppermute | solution.py:242

commit v13 on v11

--- a/solution.py
+++ b/solution.py
@@ -22,7 +22,7 @@
 PACK = 80
 HALO_ROWS = 272
 
-same_axes = ("yh", "yl", "x")
+same_axes = ("x", "yh", "yl")
 kb_axes = ("yl", "x", "c")
 all_axes = ("yh", "z", "yl", "x", "c")
 

time: 88 us -> 87.5 us (level)
  no operation moved by 1% of the time
where the time goes in v13:
time: 87.5 us; the launch traced here: 86.8 us
  starting transfers between devices  33.4 us (38%)
  blocking collectives  32.5 us (37%)
  Pallas kernels  11.3 us (13%)
  waiting for transfers between devices  4.11 us (5%)
  other arithmetic  2.42 us (3%)
  local copies, waits for them, and re-layouts  2.28 us (3%)
    all_to_all x2, blocking collectives, exchanged(): return lax.all_to_all(x, axes, split_axis=0, concat_axis=0, tiled=True)  32.5 us
    ppermute x3, starting transfers between devices, swapped(): return lax.ppermute(x, all_axes, pairs)  22 us
    all_to_all x2, starting transfers between devices, exchanged(): return lax.all_to_all(x, axes, split_axis=0, concat_axis=0, tiled=True)  11.4 us
    pallas_call x9, Pallas kernels, call(): pl.pallas_call(kernel, out_shape=outs, in_specs=[pl.BlockSpec(memory_spac...  11.3 us
    all_to_all x2, waiting for transfers between devices, exchanged(): return lax.all_to_all(x, axes, split_axis=0, concat_axis=0, tiled=True)  3.59 us
  transfers between devices with their start and end apart: 5, of which 2 were waited for; matrix products, arithmetic and copies ran while one was open for 2% of the time, Pallas kernels for 8%

profile of v13, /device:TPU:1, one launch (start us, length us, event | category | flops | bytes accessed | tf_op | source)
XLA Modules:
  0.0 86.8 jit_solution(14590636270194423720)
XLA Ops:
  0.6 0.8 fusion.4.packed
  1.4 0.8 broadcast_in_dim.3
  2.2 7.6 %all-to-all-start = ((bf16[16,80,128]{2,1,0:T(8,128)(2,1)}), bf16[16,80,128]{2,1,0:T(8,128)(2,1)S(1)}, u32[]{:S(2)}, u32[]{:S(2)}) async-start(bf16[16,80,128]{2,1,0:T(8,128)(2,1)} %broadcast_in_dim.3), calls=%async_computation | async-start | bytes 655360 | tf_op jit(solution)/shard_map/all_to_all | solution.py:233
  9.8 0.0 copy-start
  9.8 0.8 copy-done
  10.6 0.7 copy-done.6
  11.3 0.2 shard_map.132
  11.5 6.2 %collective-permute-start.1 = (bf16[272,128]{1,0:T(8,128)(2,1)S(1)}, bf16[272,128]{1,0:T(8,128)(2,1)S(1)}, u32[]{:S(2)}, u32[]{:S(2)}) collective-permute-start(bf16[272,128]{1,0:T(8,128)(2,1)S(1)} %get-tuple-element.13), channel_id=1, source_target_pairs={{1,2},{2,1},{3,4},{4,3},{5,6},{6,5},{7,8},{8,7},{9,10},{10,9},{11,... | collective-permute-start | bytes 208904 | tf_op jit(solution)/shard_map/ppermute | solution.py:238
  17.7 0.7 dynamic-slice_convert_fusion.lattice
  18.4 0.9 %convert_add_fusion.constants = f32[64,576]{1,0:T(8,128)S(1)} fusion(f32[64,512]{1,0:T(8,128)} %param.18, bf16[64,64]{1,0:T(8,128)(2,1)} %param.23), kind=kLoop, calls=%fused_computation | loop fusion | flops 73728 | bytes 286720 | tf_op jit(solution)/shard_map/add | solution.py:254
  19.3 0.0 all-to-all-done.got
  19.3 11.7 %collective-permute-start = (bf16[16,80,128]{2,1,0:T(8,128)(2,1)S(1)}, bf16[16,80,128]{2,1,0:T(8,128)(2,1)S(1)}, u32[]{:S(2)}, u32[]{:S(2)}) collective-permute-start(bf16[16,80,128]{2,1,0:T(8,128)(2,1)S(1)} %all-to-all-done.got), channel_id=1, source_target_pairs={{0,1},{1,0},{2,3},{3,2},{4,5},{5,4},{6,7},{7,6},{8,9},{9,8},{10,11... | collective-permute-start | bytes 983048 | tf_op jit(solution)/shard_map/ppermute | solution.py:238
  31.0 2.3 %shard_map.131 = (bf16[512,2048]{1,0:T(8,128)(2,1)S(1)}, f32[512,64]{1,0:T(8,128)S(1)}, f32[3,256,128]{2,1,0:T(8,128)S(1)}) custom-call(bf16[16,80,128]{2,1,0:T(8,128)(2,1)S(1)} %all-to-all-done.got, f32[3,256]{1,0:T(4,128)S(1)} %dynamic-slice_convert_fusion.lattice, f32[64,576]{1,0:T(8,128)S(1)} %convert_add_fusion.constants), custom_call_target="tpu_custom_call" | custom-call | flops 3700000000 | tf_op jit(solution)/shard_map/pallas_call | solution.py:65
  33.3 0.0 collective-permute-done.got
  33.3 2.2 %shard_map.133 = (bf16[512,2048]{1,0:T(8,128)(2,1)S(1)}, bf16[256,128]{1,0:T(8,128)(2,1)S(1)}) custom-call(bf16[16,80,128]{2,1,0:T(8,128)(2,1)S(1)} %collective-permute-done.got, f32[3,256,128]{2,1,0:T(8,128)S(1)} %get-tuple-element.11.columns, f32[512,64]{1,0:T(8,128)S(1)} %get-tuple-element.12.own_total, bf16[272,128]{1,0:T(8,128)(2,1)S(1)} %collective-permute-done.1.far), custom_call_target="tpu_custom_call" | custom-call | tf_op jit(solution)/shard_map/pallas_call | solution.py:65
  35.4 17.2 %all_to_all.20.arrived = bf16[16,16,128]{2,1,0:T(8,128)(2,1)S(1)} all-to-all(bf16[16,16,128]{2,1,0:T(8,128)(2,1)S(1)} %bitcast.7), channel_id=1, replica_groups=mesh['yh'=2,'z'=16,'yl'=2,'x'=4,'c'=2] {'z'}, dimensions={0} | all-to-all | bytes 131072 | tf_op jit(solution)/shard_map/all_to_all | solution.py:233
  52.7 15.3 %all_to_all.21 = bf16[16,16,128]{2,1,0:T(8,128)(2,1)S(1)} all-to-all(bf16[16,16,128]{2,1,0:T(8,128)(2,1)S(1)} %shard_map.134), channel_id=1, replica_groups=mesh['yh'=2,'z'=16,'yl'=2,'x'=4,'c'=2] {'z'}, dimensions={0} | all-to-all | bytes 131072 | tf_op jit(solution)/shard_map/all_to_all | solution.py:233
  68.0 0.6 shard_map.136
  68.7 4.1 %collective-permute-start.2 = (bf16[1296,128]{1,0:T(8,128)(2,1)S(1)}, bf16[1296,128]{1,0:T(8,128)(2,1)S(1)}, u32[]{:S(2)}, u32[]{:S(2)}) collective-permute-start(bf16[1296,128]{1,0:T(8,128)(2,1)S(1)} %shard_map.136), channel_id=1, source_target_pairs={{0,1},{1,0},{2,3},{3,2},{4,5},{5,4},{6,7},{7,6},{8,9},{9,8},{10,11... | collective-permute-start | bytes 995336 | tf_op jit(solution)/shard_map/ppermute | solution.py:238
  72.8 0.0 copy-start.1
  72.8 0.0 copy-start.2
  72.8 0.0 copy-start.3
  72.8 0.0 copy-start.4
  72.8 0.0 copy-start.5
  72.9 0.0 copy-start.7
  72.9 0.6 shard_map.135.own
  73.5 0.5 collective-permute-done.2.received.near
  74.0 0.8 shard_map.137.messages
  74.8 3.8 %all-to-all-start.3 = ((bf16[16,64,128]{2,1,0:T(8,128)(2,1)}), bf16[16,64,128]{2,1,0:T(8,128)(2,1)S(1)}, u32[]{:S(2)}, u32[]{:S(2)}) async-start(bf16[16,64,128]{2,1,0:T(8,128)(2,1)} %shard_map.137.messages), calls=%async_computation.3 | async-start | bytes 524288 | tf_op jit(solution)/shard_map/all_to_all | solution.py:233
  78.7 3.9 %shard_map.138 = (f32[64,128]{1,0:T(8,128)S(1)}, bf16[3,64,128]{2,1,0:T(8,128)(2,1)}) custom-call(s32[1]{0:T(128)} %bitcast.1.core, bf16[80,128]{1,0:T(8,128)(2,1)S(1)} %fusion.4.packed, bf16[3,64,128]{2,1,0:T(8,128)(2,1)S(1)} %copy-done.1, s32[16,128]{1,0:T(8,128)S(1)} %copy-done.5, bf16[1296,128]{1,0:T(8,128)(2,1)S(1)} %collective-permute-done.2.received.near, ...), custom_call_target="tpu_custom_call" | custom-call | tf_op jit(solution)/shard_map/pallas_call | solution.py:65
  82.6 3.6 %all-to-all-done.3.arrived = bf16[16,64,128]{2,1,0:T(8,128)(2,1)S(1)} async-done(((bf16[16,64,128]{2,1,0:T(8,128)(2,1)}), bf16[16,64,128]{2,1,0:T(8,128)(2,1)S(1)}, u32[]{:S(2)}, u32[]{:S(2)}) %all-to-all-start.3) | async-done | bytes 262176 | tf_op jit(solution)/shard_map/all_to_all | solution.py:233
  86.2 0.6 shard_map.139
  (9 shorter events, 0.0 us)
Async XLA Ops:
  2.2 17.1 %all-to-all-start = ((bf16[16,80,128]{2,1,0:T(8,128)(2,1)}), bf16[16,80,128]{2,1,0:T(8,128)(2,1)S(1)}, u32[]{:S(2)}, u32[]{:S(2)}) async-start(bf16[16,80,128]{2,1,0:T(8,128)(2,1)} %broadcast_in_dim.3), calls=%async_computation | async-start | bytes 655360 | tf_op jit(solution)/shard_map/all_to_all | solution.py:233
  9.8 0.8 copy-start
  10.6 0.7 copy-start.6
  11.5 21.7 %collective-permute-start.1 = (bf16[272,128]{1,0:T(8,128)(2,1)S(1)}, bf16[272,128]{1,0:T(8,128)(2,1)S(1)}, u32[]{:S(2)}, u32[]{:S(2)}) collective-permute-start(bf16[272,128]{1,0:T(8,128)(2,1)S(1)} %get-tuple-element.13), channel_id=1, source_target_pairs={{1,2},{2,1},{3,4},{4,3},{5,6},{6,5},{7,8},{8,7},{9,10},{10,9},{11,... | collective-permute-start | bytes 208904 | tf_op jit(solution)/shard_map/ppermute | solution.py:238
  19.3 13.9 %collective-permute-start = (bf16[16,80,128]{2,1,0:T(8,128)(2,1)S(1)}, bf16[16,80,128]{2,1,0:T(8,128)(2,1)S(1)}, u32[]{:S(2)}, u32[]{:S(2)}) collective-permute-start(bf16[16,80,128]{2,1,0:T(8,128)(2,1)S(1)} %all-to-all-done.got), channel_id=1, source_target_pairs={{0,1},{1,0},{2,3},{3,2},{4,5},{5,4},{6,7},{7,6},{8,9},{9,8},{10,11... | collective-permute-start | bytes 983048 | tf_op jit(solution)/shard_map/ppermute | solution.py:238
  68.7 5.4 %collective-permute-start.2 = (bf16[1296,128]{1,0:T(8,128)(2,1)S(1)}, bf16[1296,128]{1,0:T(8,128)(2,1)S(1)}, u32[]{:S(2)}, u32[]{:S(2)}) collective-permute-start(bf16[1296,128]{1,0:T(8,128)(2,1)S(1)} %shard_map.136), channel_id=1, source_target_pairs={{0,1},{1,0},{2,3},{3,2},{4,5},{5,4},{6,7},{7,6},{8,9},{9,8},{10,11... | collective-permute-start | bytes 995336 | tf_op jit(solution)/shard_map/ppermute | solution.py:238
  72.8 5.8 %copy-start.1 = (bf16[3,64,128]{2,1,0:T(8,128)(2,1)S(1)}, bf16[3,64,128]{2,1,0:T(8,128)(2,1)}, u32[]{:S(2)}) copy-start(bf16[3,64,128]{2,1,0:T(8,128)(2,1)} %vec.3) | copy-start | bytes 147460
  72.8 5.8 %copy-start.2 = (bf16[64,192]{1,0:T(8,128)(2,1)S(1)}, bf16[64,192]{1,0:T(8,128)(2,1)}, u32[]{:S(2)}) copy-start(bf16[64,192]{1,0:T(8,128)(2,1)} %message_weight.1) | copy-start | bytes 73732
  72.8 5.8 %copy-start.3 = (bf16[64,64]{1,0:T(8,128)(2,1)S(1)}, bf16[64,64]{1,0:T(8,128)(2,1)}, u32[]{:S(2)}) copy-start(bf16[64,64]{1,0:T(8,128)(2,1)} %node_weight.1) | copy-start | bytes 24580
  72.8 5.8 %copy-start.4 = (bf16[20,192]{1,0:T(8,128)(2,1)S(1)}, bf16[20,192]{1,0:T(8,128)(2,1)}, u32[]{:S(2)}) copy-start(bf16[20,192]{1,0:T(8,128)(2,1)} %radial_weight.1) | copy-start | bytes 23044
  72.8 5.8 %copy-start.5 = (s32[16,128]{1,0:T(8,128)S(1)}, s32[16,128]{1,0:T(8,128)}, u32[]{:S(2)}) copy-start(s32[16,128]{1,0:T(8,128)} %ids.1) | copy-start | bytes 24580
  72.9 5.8 %copy-start.7 = (f32[64]{0:T(128)S(1)}, f32[64]{0:T(128)}, u32[]{:S(2)}) copy-start(f32[64]{0:T(128)} %param.20) | copy-start | bytes 772
  74.8 11.4 %all-to-all-start.3 = ((bf16[16,64,128]{2,1,0:T(8,128)(2,1)}), bf16[16,64,128]{2,1,0:T(8,128)(2,1)S(1)}, u32[]{:S(2)}, u32[]{:S(2)}) async-start(bf16[16,64,128]{2,1,0:T(8,128)(2,1)} %shard_map.137.messages), calls=%async_computation.3 | async-start | bytes 524288 | tf_op jit(solution)/shard_map/all_to_all | solution.py:233

commit v14 on v13

--- a/solution.py
+++ b/solution.py
@@ -61,12 +61,14 @@
 VM, SM, ANY = pltpu.VMEM, pltpu.SMEM, pl.ANY
 
 
-def call(kernel, places, outs, *operands, scratch=(), flops=0):
+def call(kernel, places, outs, *operands, scratch=(), flops=0, far_outs=()):
     return pl.pallas_call(
         kernel,
         out_shape=outs,
         in_specs=[pl.BlockSpec(memory_space=place) for place in places],
-        out_specs=jax.tree.map(lambda _: pl.BlockSpec(memory_space=VM), outs),
+        out_specs=jax.tree.map(lambda _: pl.BlockSpec(memory_space=VM), outs)
+        if not far_outs
+        else tuple(pl.BlockSpec(memory_space=ANY if i in far_outs else VM) for i in range(len(outs))),
         scratch_shapes=list(scratch),
         compiler_params=pltpu.CompilerParams(vmem_limit_bytes=VMEM_LIMIT),
         cost_estimate=pl.CostEstimate(flops=flops, bytes_accessed=0, transcendentals=0),
@@ -79,6 +81,14 @@
     seconds = [lax.reduce_precision(value - first, 8, 7) for value, first in zip(placed[1:], firsts[1:])]
     pieces = firsts[0] + seconds[0] + ((placed[2] - firsts[2]) - seconds[1])
     return jnp.pad(feat, ((0, PACK - F), (0, 0))) + pieces.astype(jnp.bfloat16)
+
+
+def copies_kernel(packed, out, done):
+    copies = [pltpu.make_async_copy(packed, out.at[p], done.at[p]) for p in range(SAME)]
+    for copy in copies:
+        copy.start()
+    for copy in copies:
+        copy.wait()
 
 
 def summed(pieces):
@@ -247,7 +257,12 @@
     half_at = lax.axis_index("yh") * KDEV
     k_at = lax.axis_index(kb_axes) * 2 * KDEV + half_at
     packed = packed_rows(features, positions)
-    own = exchanged(jnp.broadcast_to(packed, (SAME, PACK, ATOM)), same_axes)
+    (copies,) = call(
+        copies_kernel, [VM], (shape((SAME, PACK, ATOM), bf16),), packed,
+        scratch=[pltpu.SemaphoreType.DMA((SAME,))],
+        far_outs=(0,),
+    )
+    own = exchanged(copies, same_axes)
     other = swapped(own, 0)
     own_lattice = lax.dynamic_slice_in_dim(lattice, k_at, KDEV, 1).astype(f32)
     constants = jnp.pad(kspace_filter, ((0, 0), (0, F)))

time: 87.5 us -> 87.6 us (level)
    pallas_call x9 -> x10, Pallas kernels: 11.3 us -> 12.1 us  [call(): pl.pallas_call(kernel, out_shape=outs, in_specs=[pl.BlockSpec(memory_spac...]
where the time goes in v14:
time: 87.6 us; the launch traced here: 87 us
  starting transfers between devices  33.4 us (38%)
  blocking collectives  32.5 us (37%)
  Pallas kernels  12.1 us (14%)
  waiting for transfers between devices  4.11 us (5%)
  other arithmetic  2.42 us (3%)
  local copies, waits for them, and re-layouts  1.51 us (2%)
    all_to_all x2, blocking collectives, exchanged(): return lax.all_to_all(x, axes, split_axis=0, concat_axis=0, tiled=True)  32.5 us
    ppermute x3, starting transfers between devices, swapped(): return lax.ppermute(x, all_axes, pairs)  22 us
    pallas_call x10, Pallas kernels, call(): pl.pallas_call(kernel, out_shape=outs, in_specs=[pl.BlockSpec(memory_spac...  12.1 us
    all_to_all x2, starting transfers between devices, exchanged(): return lax.all_to_all(x, axes, split_axis=0, concat_axis=0, tiled=True)  11.4 us
    all_to_all x2, waiting for transfers between devices, exchanged(): return lax.all_to_all(x, axes, split_axis=0, concat_axis=0, tiled=True)  3.59 us
  transfers between devices with their start and end apart: 5, of which 2 were waited for; matrix products, arithmetic and copies ran while one was open for 2% of the time, Pallas kernels for 8%

profile of v14, /device:TPU:1, one launch (start us, length us, event | category | flops | bytes accessed | tf_op | source)
XLA Modules:
  0.0 87.0 jit_solution(7573537009054799759)
XLA Ops:
  0.6 0.8 fusion.4.packed
  1.4 0.9 shard_map.131
  2.3 7.6 %all-to-all-start = ((bf16[16,80,128]{2,1,0:T(8,128)(2,1)}), bf16[16,80,128]{2,1,0:T(8,128)(2,1)S(1)}, u32[]{:S(2)}, u32[]{:S(2)}) async-start(bf16[16,80,128]{2,1,0:T(8,128)(2,1)} %shard_map.131), calls=%async_computation | async-start | bytes 655360 | tf_op jit(solution)/shard_map/all_to_all | solution.py:243
  9.9 0.0 copy-start
  9.9 0.8 copy-done
  10.7 0.7 copy-done.6
  11.4 0.2 shard_map.133
  11.6 6.2 %collective-permute-start.1 = (bf16[272,128]{1,0:T(8,128)(2,1)S(1)}, bf16[272,128]{1,0:T(8,128)(2,1)S(1)}, u32[]{:S(2)}, u32[]{:S(2)}) collective-permute-start(bf16[272,128]{1,0:T(8,128)(2,1)S(1)} %get-tuple-element.13), channel_id=1, source_target_pairs={{1,2},{2,1},{3,4},{4,3},{5,6},{6,5},{7,8},{8,7},{9,10},{10,9},{11,... | collective-permute-start | bytes 208904 | tf_op jit(solution)/shard_map/ppermute | solution.py:248
  17.8 0.7 dynamic-slice_convert_fusion.lattice
  18.5 0.9 %convert_add_fusion.constants = f32[64,576]{1,0:T(8,128)S(1)} fusion(f32[64,512]{1,0:T(8,128)} %param.18, bf16[64,64]{1,0:T(8,128)(2,1)} %param.23), kind=kLoop, calls=%fused_computation | loop fusion | flops 73728 | bytes 286720 | tf_op jit(solution)/shard_map/add | solution.py:269
  19.4 0.0 all-to-all-done.got
  19.4 11.7 %collective-permute-start = (bf16[16,80,128]{2,1,0:T(8,128)(2,1)S(1)}, bf16[16,80,128]{2,1,0:T(8,128)(2,1)S(1)}, u32[]{:S(2)}, u32[]{:S(2)}) collective-permute-start(bf16[16,80,128]{2,1,0:T(8,128)(2,1)S(1)} %all-to-all-done.got), channel_id=1, source_target_pairs={{0,1},{1,0},{2,3},{3,2},{4,5},{5,4},{6,7},{7,6},{8,9},{9,8},{10,11... | collective-permute-start | bytes 983048 | tf_op jit(solution)/shard_map/ppermute | solution.py:248
  31.1 2.3 %shard_map.132 = (bf16[512,2048]{1,0:T(8,128)(2,1)S(1)}, f32[512,64]{1,0:T(8,128)S(1)}, f32[3,256,128]{2,1,0:T(8,128)S(1)}) custom-call(bf16[16,80,128]{2,1,0:T(8,128)(2,1)S(1)} %all-to-all-done.got, f32[3,256]{1,0:T(4,128)S(1)} %dynamic-slice_convert_fusion.lattice, f32[64,576]{1,0:T(8,128)S(1)} %convert_add_fusion.constants), custom_call_target="tpu_custom_call" | custom-call | flops 3700000000 | tf_op jit(solution)/shard_map/pallas_call | solution.py:65
  33.4 0.0 collective-permute-done.1.far
  33.4 2.2 %shard_map.134 = (bf16[512,2048]{1,0:T(8,128)(2,1)S(1)}, bf16[256,128]{1,0:T(8,128)(2,1)S(1)}) custom-call(bf16[16,80,128]{2,1,0:T(8,128)(2,1)S(1)} %collective-permute-done.got, f32[3,256,128]{2,1,0:T(8,128)S(1)} %get-tuple-element.11.columns, f32[512,64]{1,0:T(8,128)S(1)} %get-tuple-element.12.own_total, bf16[272,128]{1,0:T(8,128)(2,1)S(1)} %collective-permute-done.1.far), custom_call_target="tpu_custom_call" | custom-call | tf_op jit(solution)/shard_map/pallas_call | solution.py:65
  35.6 17.2 %all_to_all.20.arrived = bf16[16,16,128]{2,1,0:T(8,128)(2,1)S(1)} all-to-all(bf16[16,16,128]{2,1,0:T(8,128)(2,1)S(1)} %bitcast.7), channel_id=1, replica_groups=mesh['yh'=2,'z'=16,'yl'=2,'x'=4,'c'=2] {'z'}, dimensions={0} | all-to-all | bytes 131072 | tf_op jit(solution)/shard_map/all_to_all | solution.py:243
  52.8 15.3 %all_to_all.21 = bf16[16,16,128]{2,1,0:T(8,128)(2,1)S(1)} all-to-all(bf16[16,16,128]{2,1,0:T(8,128)(2,1)S(1)} %shard_map.135), channel_id=1, replica_groups=mesh['yh'=2,'z'=16,'yl'=2,'x'=4,'c'=2] {'z'}, dimensions={0} | all-to-all | bytes 131072 | tf_op jit(solution)/shard_map/all_to_all | solution.py:243
  68.1 0.6 shard_map.137
  68.8 4.1 %collective-permute-start.2 = (bf16[1296,128]{1,0:T(8,128)(2,1)S(1)}, bf16[1296,128]{1,0:T(8,128)(2,1)S(1)}, u32[]{:S(2)}, u32[]{:S(2)}) collective-permute-start(bf16[1296,128]{1,0:T(8,128)(2,1)S(1)} %shard_map.137), channel_id=1, source_target_pairs={{0,1},{1,0},{2,3},{3,2},{4,5},{5,4},{6,7},{7,6},{8,9},{9,8},{10,11... | collective-permute-start | bytes 995336 | tf_op jit(solution)/shard_map/ppermute | solution.py:248
  72.9 0.0 copy-start.1
  72.9 0.0 copy-start.2
  72.9 0.0 copy-start.3
  73.0 0.0 copy-start.4
  73.0 0.0 copy-start.5
  73.0 0.0 copy-start.7
  73.0 0.6 shard_map.136.own
  73.6 0.5 collective-permute-done.2.received.near
  74.2 0.8 shard_map.138.messages
  74.9 3.8 %all-to-all-start.3 = ((bf16[16,64,128]{2,1,0:T(8,128)(2,1)}), bf16[16,64,128]{2,1,0:T(8,128)(2,1)S(1)}, u32[]{:S(2)}, u32[]{:S(2)}) async-start(bf16[16,64,128]{2,1,0:T(8,128)(2,1)} %shard_map.138.messages), calls=%async_computation.3 | async-start | bytes 524288 | tf_op jit(solution)/shard_map/all_to_all | solution.py:243
  78.8 3.9 %shard_map.139 = (f32[64,128]{1,0:T(8,128)S(1)}, bf16[3,64,128]{2,1,0:T(8,128)(2,1)}) custom-call(s32[1]{0:T(128)} %bitcast.1.core, bf16[80,128]{1,0:T(8,128)(2,1)S(1)} %fusion.4.packed, bf16[3,64,128]{2,1,0:T(8,128)(2,1)S(1)} %copy-done.1, s32[16,128]{1,0:T(8,128)S(1)} %copy-done.5, bf16[1296,128]{1,0:T(8,128)(2,1)S(1)} %collective-permute-done.2.received.near, ...), custom_call_target="tpu_custom_call" | custom-call | tf_op jit(solution)/shard_map/pallas_call | solution.py:65
  82.7 3.6 %all-to-all-done.3.arrived = bf16[16,64,128]{2,1,0:T(8,128)(2,1)S(1)} async-done(((bf16[16,64,128]{2,1,0:T(8,128)(2,1)}), bf16[16,64,128]{2,1,0:T(8,128)(2,1)S(1)}, u32[]{:S(2)}, u32[]{:S(2)}) %all-to-all-start.3) | async-done | bytes 262176 | tf_op jit(solution)/shard_map/all_to_all | solution.py:243
  86.3 0.6 shard_map.140
  (9 shorter events, 0.0 us)
Async XLA Ops:
  2.3 17.1 %all-to-all-start = ((bf16[16,80,128]{2,1,0:T(8,128)(2,1)}), bf16[16,80,128]{2,1,0:T(8,128)(2,1)S(1)}, u32[]{:S(2)}, u32[]{:S(2)}) async-start(bf16[16,80,128]{2,1,0:T(8,128)(2,1)} %shard_map.131), calls=%async_computation | async-start | bytes 655360 | tf_op jit(solution)/shard_map/all_to_all | solution.py:243
  9.9 0.8 copy-start
  10.7 0.7 copy-start.6
  11.6 21.7 %collective-permute-start.1 = (bf16[272,128]{1,0:T(8,128)(2,1)S(1)}, bf16[272,128]{1,0:T(8,128)(2,1)S(1)}, u32[]{:S(2)}, u32[]{:S(2)}) collective-permute-start(bf16[272,128]{1,0:T(8,128)(2,1)S(1)} %get-tuple-element.13), channel_id=1, source_target_pairs={{1,2},{2,1},{3,4},{4,3},{5,6},{6,5},{7,8},{8,7},{9,10},{10,9},{11,... | collective-permute-start | bytes 208904 | tf_op jit(solution)/shard_map/ppermute | solution.py:248
  19.4 13.9 %collective-permute-start = (bf16[16,80,128]{2,1,0:T(8,128)(2,1)S(1)}, bf16[16,80,128]{2,1,0:T(8,128)(2,1)S(1)}, u32[]{:S(2)}, u32[]{:S(2)}) collective-permute-start(bf16[16,80,128]{2,1,0:T(8,128)(2,1)S(1)} %all-to-all-done.got), channel_id=1, source_target_pairs={{0,1},{1,0},{2,3},{3,2},{4,5},{5,4},{6,7},{7,6},{8,9},{9,8},{10,11... | collective-permute-start | bytes 983048 | tf_op jit(solution)/shard_map/ppermute | solution.py:248
  68.8 5.4 %collective-permute-start.2 = (bf16[1296,128]{1,0:T(8,128)(2,1)S(1)}, bf16[1296,128]{1,0:T(8,128)(2,1)S(1)}, u32[]{:S(2)}, u32[]{:S(2)}) collective-permute-start(bf16[1296,128]{1,0:T(8,128)(2,1)S(1)} %shard_map.137), channel_id=1, source_target_pairs={{0,1},{1,0},{2,3},{3,2},{4,5},{5,4},{6,7},{7,6},{8,9},{9,8},{10,11... | collective-permute-start | bytes 995336 | tf_op jit(solution)/shard_map/ppermute | solution.py:248
  72.9 5.8 %copy-start.1 = (bf16[3,64,128]{2,1,0:T(8,128)(2,1)S(1)}, bf16[3,64,128]{2,1,0:T(8,128)(2,1)}, u32[]{:S(2)}) copy-start(bf16[3,64,128]{2,1,0:T(8,128)(2,1)} %vec.3) | copy-start | bytes 147460
  72.9 5.8 %copy-start.2 = (bf16[64,192]{1,0:T(8,128)(2,1)S(1)}, bf16[64,192]{1,0:T(8,128)(2,1)}, u32[]{:S(2)}) copy-start(bf16[64,192]{1,0:T(8,128)(2,1)} %message_weight.1) | copy-start | bytes 73732
  72.9 5.8 %copy-start.3 = (bf16[64,64]{1,0:T(8,128)(2,1)S(1)}, bf16[64,64]{1,0:T(8,128)(2,1)}, u32[]{:S(2)}) copy-start(bf16[64,64]{1,0:T(8,128)(2,1)} %node_weight.1) | copy-start | bytes 24580
  73.0 5.8 %copy-start.4 = (bf16[20,192]{1,0:T(8,128)(2,1)S(1)}, bf16[20,192]{1,0:T(8,128)(2,1)}, u32[]{:S(2)}) copy-start(bf16[20,192]{1,0:T(8,128)(2,1)} %radial_weight.1) | copy-start | bytes 23044
  73.0 5.8 %copy-start.5 = (s32[16,128]{1,0:T(8,128)S(1)}, s32[16,128]{1,0:T(8,128)}, u32[]{:S(2)}) copy-start(s32[16,128]{1,0:T(8,128)} %ids.1) | copy-start | bytes 24580
  73.0 5.8 %copy-start.7 = (f32[64]{0:T(128)S(1)}, f32[64]{0:T(128)}, u32[]{:S(2)}) copy-start(f32[64]{0:T(128)} %param.20) | copy-start | bytes 772
  74.9 11.4 %all-to-all-start.3 = ((bf16[16,64,128]{2,1,0:T(8,128)(2,1)}), bf16[16,64,128]{2,1,0:T(8,128)(2,1)S(1)}, u32[]{:S(2)}, u32[]{:S(2)}) async-start(bf16[16,64,128]{2,1,0:T(8,128)(2,1)} %shard_map.138.messages), calls=%async_computation.3 | async-start | bytes 524288 | tf_op jit(solution)/shard_map/all_to_all | solution.py:243
